TPU v7x, 32 devices: a whole 2x2x4 slice. The times are simulated.
32 devices in a mesh: groups: 1, wide: 32 (over z, y, x, core).
Axes of the slice: x: 2, y: 2, z: 4, core: 2. Of those that a mesh axis runs over, the one named last changes fastest.
Arguments:
- tokens: bfloat16 [128, 16384], P(('groups', 'wide')), may hold values from -6 to 6
- norm_gain: float32 [16384], replicated, may hold values from 0.1 to 1.9
- w_query: bfloat16 [16384, 16384], P(None, 'wide'), may hold values from -0.046875 to 0.046875
- w_keyval: bfloat16 [2048, 16384], P('wide'), may hold values from -0.046875 to 0.046875
- w_out: bfloat16 [16384, 16384], P(None, 'wide'), may hold values from -0.046875 to 0.046875
- cache_keys: bfloat16 [128, 8, 128, 128], P(('groups', 'wide'))
- cache_values: bfloat16 [128, 8, 128, 128], P(('groups', 'wide')), may hold values from -6 to 6
- session_ids: int32 [128], P('groups'), may hold values from 0 to 127, each once
- lengths: int32 [128], P(('groups', 'wide')), may hold values from 1 to 128, as said below
Outputs:
- attn_out: bfloat16 [128, 16384], P('groups', 'wide')
Inputs may be any that keep to these rules, and one draw needn't show every extreme that they name: `session_ids`: a permutation of the sessions 0 to 127. `lengths`: some session has exactly 128 cached positions in every draw.
All inputs are finite; a program needn't handle non-finite values.
Results may differ from a plain program's by a relative error of at most 0.007.
The roundings to bfloat16 on the way count: a program that leaves them out, or rounds other values in their place, can miss the bound.
Values may be sent and summed in bfloat16 or wider, within the bound.
No kernel may reach another device: no remote copies, remote signals or barrier semaphores. Data moves between devices by JAX's collectives and lax.ppermute only.
A program may use at most 128 MiB of HBM per device.

v0:
```python
import math

import jax
import jax.numpy as jnp
from jax import lax
from jax.sharding import PartitionSpec as P

HEADS = 128
KVH = 8


ROPE_BASE = 500000.0


def rms_rows(rows, gain):
    values = rows.astype(jnp.float32)
    meansq = jnp.mean(values * values, axis=-1, keepdims=True)
    return (values * lax.rsqrt(meansq + 1e-05) * gain).astype(jnp.bfloat16)


def rotate_heads(values, positions):
    width = values.shape[-1]
    halfway = width // 2
    indices = jnp.arange(halfway).astype(jnp.float32)
    inverse_freq = jnp.exp(indices * (-2.0 * math.log(ROPE_BASE) / width))
    angles = positions.astype(jnp.float32)[:, None, None] * inverse_freq
    cosine = jnp.cos(angles)
    sine = jnp.sin(angles)
    first = values[..., :halfway]
    second = values[..., halfway:]
    return jnp.concatenate(
        [first * cosine - second * sine, second * cosine + first * sine], axis=-1
    )


def attend_sessions(query_sess, keyval_sess, cache_keys, cache_values, lengths):
    sessions = query_sess.shape[0]
    head_dim = query_sess.shape[1] // HEADS
    group = HEADS // KVH
    scale = head_dim ** (-0.5)
    rot_query = rotate_heads(
        query_sess.astype(jnp.float32).reshape(sessions, HEADS, head_dim), lengths
    )
    rot_query = rot_query.astype(jnp.bfloat16).reshape(sessions, KVH, group, head_dim)
    new_keys = keyval_sess[:, : KVH * head_dim].astype(jnp.float32).reshape(sessions, KVH, head_dim)
    own_key = rotate_heads(new_keys, lengths).astype(jnp.bfloat16)
    own_value = keyval_sess[:, KVH * head_dim :].reshape(sessions, KVH, head_dim)
    scores = (
        jnp.einsum("sgqd,sgpd->sgqp", rot_query, cache_keys, preferred_element_type=jnp.float32)
        * scale
    )
    valid = jnp.arange(cache_keys.shape[2])[None, :] < lengths[:, None]
    scores = jnp.where(valid[:, None, None, :], scores, -jnp.inf)
    own_score = (
        jnp.einsum("sgqd,sgd->sgq", rot_query, own_key, preferred_element_type=jnp.float32) * scale
    )
    highest = jnp.maximum(jnp.max(scores, axis=-1), own_score)
    cached_exp = jnp.exp(scores - highest[..., None])
    own_exp = jnp.exp(own_score - highest)
    total = jnp.sum(cached_exp, axis=-1) + own_exp
    cached_weight = (cached_exp / total[..., None]).astype(jnp.bfloat16)
    own_weight = (own_exp / total).astype(jnp.bfloat16)
    attended = jnp.einsum(
        "sgqp,sgpd->sgqd", cached_weight, cache_values, preferred_element_type=jnp.float32
    )
    attended = (
        attended
        + own_weight.astype(jnp.float32)[..., None] * own_value.astype(jnp.float32)[:, :, None, :]
    )
    return attended.reshape(sessions, HEADS * head_dim).astype(jnp.bfloat16)


def on_device(
    tokens, norm_gain, w_query, w_keyval, w_out, cache_keys, cache_values, session_ids, lengths
):
    normed = rms_rows(tokens, norm_gain)
    query_cols = w_query.shape[1]
    everyone = lax.all_gather(normed, "wide", axis=0, tiled=True)
    query_part = jnp.dot(everyone, w_query, preferred_element_type=jnp.float32).astype(jnp.bfloat16)
    keyval_part = lax.dot_general(
        everyone, w_keyval, (((1,), (1,)), ((), ())), preferred_element_type=jnp.float32
    ).astype(jnp.bfloat16)
    joined = jnp.concatenate([query_part, keyval_part], axis=1)
    inverse = jnp.argsort(session_ids)
    ordered = joined[inverse]
    query_local = ordered[:, :query_cols]
    keyval_local = ordered[:, query_cols:]
    query_sess, keyval_sess = (
        lax.all_to_all(query_local, "wide", split_axis=0, concat_axis=1, tiled=True),
        lax.all_to_all(keyval_local, "wide", split_axis=0, concat_axis=1, tiled=True),
    )
    attended = attend_sessions(query_sess, keyval_sess, cache_keys, cache_values, lengths)
    all_attended = lax.all_gather(attended, "wide", axis=0, tiled=True)
    out_sess = jnp.dot(all_attended, w_out, preferred_element_type=jnp.float32)
    return out_sess[session_ids].astype(jnp.bfloat16)


def solution(mesh):
    return jax.shard_map(
        on_device,
        mesh=mesh,
        in_specs=(
            P(("groups", "wide"), None),
            P(),
            P(None, "wide"),
            P("wide", None),
            P(None, "wide"),
            P(("groups", "wide"), None, None, None),
            P(("groups", "wide"), None, None, None),
            P("groups"),
            P(("groups", "wide")),
        ),
        out_specs=P("groups", "wide"),
        check_vma=False,
    )
```

profile of v0, /device:TPU:0, one launch (start us, length us, event | category | flops | bytes accessed | tf_op | source)
XLA Modules:
  0.0 207.2 jit_solution(9121155686482615312)
XLA Ops:
  6.5 1.3 fusion.2
  7.8 1.7 fusion.6
  9.6 0.7 convert_element_type.73
  10.2 3.2 %sort.17 = (s32[128]{0:T(128)}, s32[128]{0:T(128)S(1)}) sort(s32[128]{0:T(128)} %param.16, s32[128]{0:T(128)S(1)} %iota.17), dimensions={0}, to_apply=%region_1.0 | sort | flops 896 | bytes 2048 | tf_op jit(solution)/shard_map/jit(argsort)/sort | solution.py:84
  13.5 0.1 multiply_cosine_fusion
  13.6 61.4 %all-gather.5.cloned.1.call-done = bf16[32,4,16384]{2,1,0:T(4,128)(2,1)} async-done(((bf16[1,4,16384]{2,1,0:T(4,128)(2,1)}), bf16[32,4,16384]{2,1,0:T(4,128)(2,1)}) %all-gather.5.cloned.1.call-update) | async-done | bytes 4194320 | tf_op jit(solution)/shard_map/all_gather | solution.py:78
  75.0 7.0 %reshape.145 = bf16[128,16384]{1,0:T(8,128)(2,1)} reshape(bf16[32,4,16384]{2,1,0:T(4,128)(2,1)} %all-gather.5.cloned.1.call-done) | data formatting | bytes 8388608
  82.0 9.5 %convolution_convert_fusion = bf16[128,512]{1,0:T(8,128)(2,1)S(1)} fusion(bf16[128,16384]{1,0:T(8,128)(2,1)} %reshape.145, bf16[16384,512]{1,0:T(8,128)(2,1)} %param.11), kind=kOutput, calls=%fused_computation.6 | convolution fusion | flops 2147549184 | bytes 21102592 | tf_op jit(solution)/shard_map/dot_general | solution.py:79
  91.5 1.6 convolution_convert_fusion.1
  93.1 0.1 copy.18
  93.3 1.5 gather_fusion
  94.8 0.8 slice.39
  95.6 0.7 reshape.152
  96.3 3.2 %all-to-all-start.1 = ((bf16[32,2,128]{2,1,0:T(2,128)(2,1)}), bf16[32,2,128]{2,1,0:T(2,128)(2,1)S(1)}, u32[]{:S(2)}, u32[]{:S(2)}) async-start(bf16[32,2,128]{2,1,0:T(2,128)(2,1)} %reshape.152), calls=%async_computation.1 | async-start | bytes 32768 | tf_op jit(solution)/shard_map/all_to_all | solution.py:90
  99.5 0.9 slice.36
  100.4 0.7 all_to_all.24
  101.1 5.5 %all-to-all-done.1 = bf16[32,2,128]{2,1,0:T(2,128)(2,1)S(1)} async-done(((bf16[32,2,128]{2,1,0:T(2,128)(2,1)}), bf16[32,2,128]{2,1,0:T(2,128)(2,1)S(1)}, u32[]{:S(2)}, u32[]{:S(2)}) %all-to-all-start.1) | async-done | bytes 16416 | tf_op jit(solution)/shard_map/all_to_all | solution.py:90
  106.6 2.6 %all-to-all-start = ((bf16[32,4,512]{2,1,0:T(4,128)(2,1)}), bf16[32,4,512]{2,1,0:T(4,128)(2,1)S(1)}, u32[]{:S(2)}, u32[]{:S(2)}) async-start(bf16[32,4,512]{2,1,0:T(4,128)(2,1)} %all_to_all.24), calls=%async_computation | async-start | bytes 262144 | tf_op jit(solution)/shard_map/all_to_all | solution.py:89
  109.3 0.1 all_to_all.29
  109.6 7.8 %all-to-all-done = bf16[32,4,512]{2,1,0:T(4,128)(2,1)S(1)} async-done(((bf16[32,4,512]{2,1,0:T(4,128)(2,1)}), bf16[32,4,512]{2,1,0:T(4,128)(2,1)S(1)}, u32[]{:S(2)}, u32[]{:S(2)}) %all-to-all-start) | async-done | bytes 131104 | tf_op jit(solution)/shard_map/all_to_all | solution.py:89
  117.4 0.8 copy.19
  118.2 1.0 reshape.122
  119.2 0.1 subtract_convert_fusion
  119.3 0.2 fusion.9
  119.6 0.8 fusion.15
  120.4 0.3 fusion.5
  120.7 1.7 fusion.1
  122.4 0.7 reshape.146
  123.1 59.4 %all-gather.7.cloned.1.call-done = bf16[32,4,16384]{2,1,0:T(4,128)(2,1)} async-done(((bf16[1,4,16384]{2,1,0:T(4,128)(2,1)}), bf16[32,4,16384]{2,1,0:T(4,128)(2,1)}) %all-gather.7.cloned.1.call-update) | async-done | bytes 4194320 | tf_op jit(solution)/shard_map/all_gather | solution.py:93
  182.6 7.0 %reshape.147 = bf16[128,16384]{1,0:T(8,128)(2,1)} reshape(bf16[32,4,16384]{2,1,0:T(4,128)(2,1)} %all-gather.7.cloned.1.call-done) | data formatting | bytes 8388608
  189.5 9.4 %fusion.16 = bf16[128,512]{1,0:T(8,128)(2,1)S(1)} fusion(bf16[128,16384]{1,0:T(8,128)(2,1)} %reshape.147, bf16[16384,512]{1,0:T(8,128)(2,1)} %param.13), kind=kOutput, calls=%fused_computation.50 | convolution fusion | flops 2147483648 | bytes 21102592 | tf_op jit(solution)/shard_map/dot_general | solution.py:94
  198.9 1.5 gather_fusion.1
  (32 shorter events, 0.5 us)
Async XLA Ops:
  6.5 85.0 %copy-start = (bf16[64,16384]{1,0:T(8,128)(2,1)S(1)}, bf16[64,16384]{1,0:T(8,128)(2,1)}, u32[]{:S(2)}) copy-start(bf16[64,16384]{1,0:T(8,128)(2,1)} %param.12) | copy-start | bytes 6291460
  6.5 68.5 %all-gather.5.cloned.1.call-start = ((), (), s32[]{:S(2)}) async-start(), calls=%async_computation.2 | async-start | bytes 4325376 | tf_op jit(solution)/shard_map/all_gather | solution.py:78
  82.0 9.5 %copy-start.1 = (bf16[128,16384]{1,0:T(8,128)(2,1)S(1)}, bf16[128,16384]{1,0:T(8,128)(2,1)}, u32[]{:S(2)}) copy-start(bf16[128,16384]{1,0:T(8,128)(2,1)} %reshape.145) | copy-start | bytes 12582916
  91.5 7.9 %copy-start.3 = (s32[4]{0:T(128)S(1)}, s32[4]{0:T(128)}, u32[]{:S(2)}) copy-start(s32[4]{0:T(128)} %param.17) | copy-start | bytes 52
  93.1 26.5 %copy-start.2 = (bf16[4,8,128,128]{3,2,1,0:T(8,128)(2,1)S(1)}, bf16[4,8,128,128]{3,2,1,0:T(8,128)(2,1)}, u32[]{:S(2)}) copy-start(bf16[4,8,128,128]{3,2,1,0:T(8,128)(2,1)} %param.14) | copy-start | bytes 3145732
  94.8 28.3 %copy-start.4 = (s32[128]{0:T(128)S(1)}, s32[128]{0:T(128)}, u32[]{:S(2)}) copy-start(s32[128]{0:T(128)} %param.16) | copy-start | bytes 1540
  96.3 10.3 %all-to-all-start.1 = ((bf16[32,2,128]{2,1,0:T(2,128)(2,1)}), bf16[32,2,128]{2,1,0:T(2,128)(2,1)S(1)}, u32[]{:S(2)}, u32[]{:S(2)}) async-start(bf16[32,2,128]{2,1,0:T(2,128)(2,1)} %reshape.152), calls=%async_computation.1 | async-start | bytes 32768 | tf_op jit(solution)/shard_map/all_to_all | solution.py:90
  106.6 10.8 %all-to-all-start = ((bf16[32,4,512]{2,1,0:T(4,128)(2,1)}), bf16[32,4,512]{2,1,0:T(4,128)(2,1)S(1)}, u32[]{:S(2)}, u32[]{:S(2)}) async-start(bf16[32,4,512]{2,1,0:T(4,128)(2,1)} %all_to_all.24), calls=%async_computation | async-start | bytes 262144 | tf_op jit(solution)/shard_map/all_to_all | solution.py:89
  109.2 73.4 %all-gather.7.cloned.1.call-start = ((), (), s32[]{:S(2)}) async-start(), calls=%async_computation.3 | async-start | bytes 4325376 | tf_op jit(solution)/shard_map/all_gather | solution.py:93
Sparse Core Ops, SparseCore 0:
  10.2 64.7 all-gather.4
  123.2 59.2 all-gather.6
where the time goes:
time: 208 us; the launch traced here: 207 us
  waiting for transfers between devices  134 us (64%)
  matrix products  23.2 us (11%)
  local copies, waits for them, and re-layouts  22.8 us (11%)
  between operations  13.6 us (7%)
  other arithmetic  7.75 us (4%)
  starting transfers between devices  5.77 us (3%)
    all_gather x1, waiting for transfers between devices, on_device(): everyone = lax.all_gather(normed, 'wide', axis=0, tiled=True)  61.4 us
    all_gather x1, waiting for transfers between devices, on_device(): all_attended = lax.all_gather(attended, 'wide', axis=0, tiled=True)  59.4 us
    unnamed x15, local copies, waits for them, and re-layouts  15.4 us
    dot_general x1, matrix products, on_device(): jnp.dot(everyone, w_query, preferred_element_type=jnp.float32)  9.51 us
    dot_general x1, matrix products, on_device(): out_sess = jnp.dot(all_attended, w_out, preferred_element_type=jnp.float32)  9.38 us
    all_to_all x1, waiting for transfers between devices, on_device(): lax.all_to_all(query_local, 'wide', split_axis=0, concat_axis=1, tiled=True)  7.8 us
    all_to_all x1, waiting for transfers between devices, on_device(): lax.all_to_all(keyval_local, 'wide', split_axis=0, concat_axis=1, tiled=T...  5.45 us
  transfers between devices with their start and end apart: 4, of which 4 were waited for; matrix products, arithmetic and copies ran while one was open for 3% of the time, Pallas kernels for 0%

commit v1 on v0

--- a/solution.py
+++ b/solution.py
@@ -1,8 +1,11 @@
+import functools
 import math
 
 import jax
 import jax.numpy as jnp
 from jax import lax
+from jax.experimental import pallas as pl
+from jax.experimental.pallas import tpu as pltpu
 from jax.sharding import PartitionSpec as P
 
 HEADS = 128
@@ -10,6 +13,11 @@
 
 
 ROPE_BASE = 500000.0
+
+LANES = 128
+PIECE = 4
+TILE = 16
+MIB = 1 << 20
 
 
 def rms_rows(rows, gain):
@@ -70,7 +78,7 @@
     return attended.reshape(sessions, HEADS * head_dim).astype(jnp.bfloat16)
 
 
-def on_device(
+def on_any(
     tokens, norm_gain, w_query, w_keyval, w_out, cache_keys, cache_values, session_ids, lengths
 ):
     normed = rms_rows(tokens, norm_gain)
@@ -95,9 +103,376 @@
     return out_sess[session_ids].astype(jnp.bfloat16)
 
 
+def norm_pack_kernel(own, z1, z2, z3, gain, low, high, full):
+    width = own.shape[1]
+    blocks = width // LANES
+    pieces = (own, z1, z2, z3)
+    scales = []
+    for piece in pieces:
+        values = piece[...].astype(jnp.float32)
+        meansq = jnp.sum(values * values, axis=-1, keepdims=True) * (1.0 / width)
+        scales.append(lax.rsqrt(meansq + 1e-05))
+    for block in range(blocks):
+        lanes = slice(block * LANES, (block + 1) * LANES)
+        factor = gain[:, lanes]
+        rows = jnp.concatenate(
+            [piece[:, lanes].astype(jnp.float32) * scale * factor for piece, scale in zip(pieces, scales)],
+            axis=0,
+        ).astype(jnp.bfloat16)
+        full[block] = rows
+        if block < blocks // 2:
+            low[block] = rows
+        else:
+            high[block - blocks // 2] = rows
+
+
+def pack_kernel(own, z1, z2, z3, low, high, full):
+    blocks = own.shape[0] // PIECE
+    pieces = (own, z1, z2, z3)
+    for first in range(0, blocks, 4):
+        tiles = [
+            piece[first * PIECE : (first + 4) * PIECE, :].astype(jnp.float32) for piece in pieces
+        ]
+        for at in range(4):
+            block = first + at
+            rows = jnp.concatenate(
+                [tile[at * PIECE : (at + 1) * PIECE, :] for tile in tiles], axis=0
+            ).astype(jnp.bfloat16)
+            full[block] = rows
+            if block < blocks // 2:
+                low[block] = rows
+            else:
+                high[block - blocks // 2] = rows
+
+
+def packed_shapes(blocks):
+    half = jax.ShapeDtypeStruct((blocks // 2, TILE, LANES), jnp.bfloat16)
+    return (half, half, jax.ShapeDtypeStruct((blocks, TILE, LANES), jnp.bfloat16))
+
+
+def norm_pack(own, z1, z2, z3, gain):
+    blocks = own.shape[1] // LANES
+    return pl.pallas_call(
+        norm_pack_kernel,
+        out_shape=packed_shapes(blocks),
+        compiler_params=pltpu.CompilerParams(vmem_limit_bytes=24 * MIB),
+        cost_estimate=pl.CostEstimate(flops=4_000_000, bytes_accessed=2_000_000, transcendentals=0),
+    )(own, z1, z2, z3, gain[None, :])
+
+
+def pack(own, z1, z2, z3):
+    blocks = own.shape[0] // PIECE
+    return pl.pallas_call(
+        pack_kernel,
+        out_shape=packed_shapes(blocks),
+        compiler_params=pltpu.CompilerParams(vmem_limit_bytes=24 * MIB),
+        cost_estimate=pl.CostEstimate(flops=1_000_000, bytes_accessed=2_000_000, transcendentals=0),
+    )(own, z1, z2, z3)
+
+
+def swapped(array, mask, devices):
+    return lax.ppermute(array, "wide", [(i, i ^ mask) for i in range(devices)])
+
+
+def gather_rows(piece, pack_pieces, devices):
+    swap = functools.partial(swapped, devices=devices)
+    z2, z3, z1 = swap(piece, 16), swap(piece, 24), swap(piece, 8)
+    low, high, full = pack_pieces(piece, z1, z2, z3)
+    x_low, y_high = swap(low, 2), swap(high, 4)
+    x_high, y_low = swap(high, 2), swap(low, 4)
+    d_low, d_high = swap(x_low, 4), swap(y_high, 2)
+    other = swap(full, 1)
+    mine = [(low, high), (x_low, x_high), (y_low, y_high), (d_low, d_high)]
+    theirs = [(swap(a, 1), swap(b, 1)) for a, b in mine[1:]]
+    return mine, other, theirs
+
+
+def row_devices(devices):
+    rows = jnp.arange(devices * PIECE, dtype=jnp.int32)
+    core = rows // (devices * PIECE // 2)
+    plane = (rows // TILE) % 4
+    column = (rows // PIECE) % 4
+    me = lax.axis_index("wide").astype(jnp.int32)
+    return (me ^ (core + 2 * plane + 8 * column)) * PIECE + rows % PIECE
+
+
+def gathered_tile(refs, count):
+    blocks = []
+    for block in range(count):
+        blocks.append(jnp.concatenate([ref[block] for ref in refs], axis=0))
+    return jnp.concatenate(blocks, axis=1)
+
+
+def query_kernel(*refs, steps):
+    low, high = refs[0:8], refs[8:16]
+    weight, weight_kv, codes, sess, parity, out, total, total_kv = refs[16:]
+    step = pl.program_id(0)
+    count = low[0].shape[0]
+
+    @pl.when(step == 0)
+    def _():
+        total[...] = jnp.zeros_like(total)
+        total_kv[...] = jnp.zeros_like(total_kv)
+
+    def add(parts):
+        rows = gathered_tile(parts, count)
+        total[...] += jnp.dot(rows, weight[...], preferred_element_type=jnp.float32)
+        total_kv[...] += lax.dot_general(
+            rows, weight_kv[...], (((1,), (1,)), ((), ())), preferred_element_type=jnp.float32
+        )
+
+    pl.when(step < steps // 2)(lambda: add(low))
+    pl.when(step >= steps // 2)(lambda: add(high))
+
+    @pl.when(step == steps - 1)
+    def _():
+        rows, width = total.shape
+        heads = width // LANES
+        stacked = jnp.concatenate(
+            [total[:, h * LANES : (h + 1) * LANES].astype(jnp.bfloat16) for h in range(heads)], axis=0
+        )
+        at = lax.broadcasted_iota(jnp.int32, (rows * heads, rows * heads), 0)
+        wanted = ((at // PIECE) % heads) * rows + (at // (PIECE * heads)) * PIECE + at % PIECE
+        chosen = (wanted == codes[...]).astype(jnp.float32).astype(jnp.bfloat16)
+        query = jnp.dot(chosen, stacked, preferred_element_type=jnp.float32).astype(jnp.bfloat16)
+        devices = rows // PIECE
+        out[:, 0:TILE, :] = query.reshape(devices, TILE, LANES)
+        columns = total_kv.shape[1]
+        keyval = total_kv[...].astype(jnp.bfloat16)
+        at = lax.broadcasted_iota(jnp.int32, (devices * TILE, rows), 0)
+        wanted = jnp.where(at % TILE < PIECE, (at // TILE) * PIECE + at % TILE, -1)
+        chosen = (wanted == sess[...]).astype(jnp.float32).astype(jnp.bfloat16)
+        ordered = jnp.dot(chosen, keyval, preferred_element_type=jnp.float32).astype(jnp.bfloat16)
+        here = lax.broadcasted_iota(jnp.int32, (columns, LANES), 0)
+        there = lax.broadcasted_iota(jnp.int32, (columns, LANES), 1)
+        place = (there == here + parity[0] * columns).astype(jnp.float32).astype(jnp.bfloat16)
+        placed = jnp.dot(ordered, place, preferred_element_type=jnp.float32).astype(jnp.bfloat16)
+        out[:, TILE : 2 * TILE, :] = placed.reshape(devices, TILE, LANES)
+
+
+def out_kernel(*refs, steps):
+    low, high = refs[0:8], refs[8:16]
+    weight, sess, wanted, out, total = refs[16:]
+    step = pl.program_id(0)
+    count = low[0].shape[0]
+
+    @pl.when(step == 0)
+    def _():
+        total[...] = jnp.zeros_like(total)
+
+    def add(parts):
+        rows = gathered_tile(parts, count)
+        total[...] += jnp.dot(rows, weight[...], preferred_element_type=jnp.float32)
+
+    pl.when(step < steps // 2)(lambda: add(low))
+    pl.when(step >= steps // 2)(lambda: add(high))
+
+    @pl.when(step == steps - 1)
+    def _():
+        chosen = (wanted[...] == sess[...]).astype(jnp.float32).astype(jnp.bfloat16)
+        rounded = total[...].astype(jnp.bfloat16)
+        out[...] = jnp.dot(chosen, rounded, preferred_element_type=jnp.float32).astype(jnp.bfloat16)
+
+
+STEPS = 16
+
+
+def gathered_operands(gathered, steps):
+    mine, other, theirs = gathered
+    blocks = other.shape[0]
+    count = blocks // steps
+    operands, specs = [], []
+    for half in range(2):
+        if half == 0:
+            index = lambda k: (jnp.minimum(k, steps // 2 - 1), 0, 0)
+            index_full = index
+        else:
+            index = lambda k: (jnp.maximum(k - steps // 2, 0), 0, 0)
+            index_full = lambda k: (jnp.maximum(k, steps // 2), 0, 0)
+        block = (count, TILE, LANES)
+        for pair in mine:
+            operands.append(pair[half])
+            specs.append(pl.BlockSpec(block, index))
+        operands.append(other)
+        specs.append(pl.BlockSpec(block, index_full))
+        for pair in theirs:
+            operands.append(pair[half])
+            specs.append(pl.BlockSpec(block, index))
+    return operands, specs
+
+
+def project_query(gathered, w_query, w_keyval, sess, devices):
+    operands, specs = gathered_operands(gathered, STEPS)
+    depth, columns = w_query.shape
+    rows = devices * PIECE
+    heads = columns // LANES
+    codes = (jnp.arange(heads, dtype=jnp.int32)[:, None] * rows + sess[None, :]).reshape(1, -1)
+    parity = (lax.axis_index("wide") % 2).astype(jnp.int32)[None]
+    chunk = depth // STEPS
+    return pl.pallas_call(
+        functools.partial(query_kernel, steps=STEPS),
+        grid=(STEPS,),
+        in_specs=specs
+        + [
+            pl.BlockSpec((chunk, columns), lambda k: (k, 0)),
+            pl.BlockSpec((w_keyval.shape[0], chunk), lambda k: (0, k)),
+            pl.BlockSpec((1, heads * rows), lambda k: (0, 0)),
+            pl.BlockSpec((1, rows), lambda k: (0, 0)),
+            pl.BlockSpec(memory_space=pltpu.SMEM),
+        ],
+        out_specs=pl.BlockSpec((devices, 2 * TILE, LANES), lambda k: (0, 0, 0)),
+        out_shape=jax.ShapeDtypeStruct((devices, 2 * TILE, LANES), jnp.bfloat16),
+        scratch_shapes=[
+            pltpu.VMEM((rows, columns), jnp.float32),
+            pltpu.VMEM((rows, w_keyval.shape[0]), jnp.float32),
+        ],
+        compiler_params=pltpu.CompilerParams(vmem_limit_bytes=24 * MIB),
+        cost_estimate=pl.CostEstimate(
+            flops=2 * rows * depth * columns, bytes_accessed=2 * depth * (columns + rows), transcendentals=0
+        ),
+    )(*operands, w_query, w_keyval, codes, sess[None, :], parity)
+
+
+def project_out(gathered, w_out, sess, wanted, devices):
+    operands, specs = gathered_operands(gathered, STEPS)
+    depth, columns = w_out.shape
+    rows = devices * PIECE
+    chunk = depth // STEPS
+    return pl.pallas_call(
+        functools.partial(out_kernel, steps=STEPS),
+        grid=(STEPS,),
+        in_specs=specs
+        + [
+            pl.BlockSpec((chunk, columns), lambda k: (k, 0)),
+            pl.BlockSpec((1, rows), lambda k: (0, 0)),
+            pl.BlockSpec((rows, 1), lambda k: (0, 0)),
+        ],
+        out_specs=pl.BlockSpec((rows, columns), lambda k: (0, 0)),
+        out_shape=jax.ShapeDtypeStruct((rows, columns), jnp.bfloat16),
+        scratch_shapes=[pltpu.VMEM((rows, columns), jnp.float32)],
+        compiler_params=pltpu.CompilerParams(vmem_limit_bytes=24 * MIB),
+        cost_estimate=pl.CostEstimate(
+            flops=2 * rows * depth * columns, bytes_accessed=2 * depth * (columns + rows), transcendentals=0
+        ),
+    )(*operands, w_out, sess[None, :], wanted[:, None])
+
+
+def attend_kernel(received, keys, values, cosine, sine, limits, out):
+    sessions, kv_heads, cache_len, width = keys.shape
+    devices = received.shape[0]
+    per_group = devices // kv_heads
+    rows = per_group * TILE
+    scale = width ** (-0.5)
+
+    def rotate(vectors):
+        count = vectors.shape[0]
+        return (
+            vectors * cosine[0:count, :] + pltpu.roll(vectors, width // 2, 1) * sine[0:count, :]
+        ).astype(jnp.bfloat16)
+
+    own = received[:, TILE : 2 * TILE, :].astype(jnp.float32)
+    pairs = devices // 2
+    own = own.reshape(pairs, 2, TILE, width)
+    own = own[:, 0] + own[:, 1]
+    own = own[:, 0:8]
+    own_rows = kv_heads * 8
+    own_key = rotate(own[0:kv_heads].reshape(own_rows, width))
+    own_value = own[kv_heads:].reshape(own_rows, width).astype(jnp.bfloat16)
+
+    session = lax.broadcasted_iota(jnp.int32, (rows, sessions * cache_len), 0) % PIECE
+    column = lax.broadcasted_iota(jnp.int32, (rows, sessions * cache_len), 1)
+    valid = (column // cache_len == session) & (column % cache_len < limits[...])
+    own_session = lax.broadcasted_iota(jnp.int32, (rows, own_rows), 0) % PIECE
+    own_column = lax.broadcasted_iota(jnp.int32, (rows, own_rows), 1)
+    for group in range(kv_heads):
+        query = received[group * per_group : (group + 1) * per_group, 0:TILE, :]
+        query = rotate(query.reshape(rows, width).astype(jnp.float32))
+        group_keys = keys[:, group].reshape(sessions * cache_len, width)
+        group_values = values[:, group].reshape(sessions * cache_len, width)
+        contract = (((1,), (1,)), ((), ()))
+        scores = (
+            lax.dot_general(query, group_keys, contract, preferred_element_type=jnp.float32) * scale
+        )
+        scores = jnp.where(valid, scores, -jnp.inf)
+        own_scores = (
+            lax.dot_general(query, own_key, contract, preferred_element_type=jnp.float32) * scale
+        )
+        own_scores = jnp.where(own_column == group * 8 + own_session, own_scores, -jnp.inf)
+        highest = jnp.maximum(
+            jnp.max(scores, axis=-1, keepdims=True), jnp.max(own_scores, axis=-1, keepdims=True)
+        )
+        cached_exp = jnp.exp(scores - highest)
+        own_exp = jnp.exp(own_scores - highest)
+        total = jnp.sum(cached_exp, axis=-1, keepdims=True) + jnp.sum(
+            own_exp, axis=-1, keepdims=True
+        )
+        weights = (cached_exp / total).astype(jnp.bfloat16)
+        own_weights = (own_exp / total).astype(jnp.bfloat16)
+        attended = jnp.dot(weights, group_values, preferred_element_type=jnp.float32)
+        attended += jnp.dot(own_weights, own_value, preferred_element_type=jnp.float32)
+        out[group * rows : (group + 1) * rows, :] = attended.astype(jnp.bfloat16)
+
+
+def attend(received, keys, values, lengths):
+    sessions, kv_heads, cache_len, width = keys.shape
+    devices = received.shape[0]
+    rows = devices // kv_heads * TILE
+    halfway = width // 2
+    indices = jnp.arange(halfway).astype(jnp.float32)
+    inverse_freq = jnp.exp(indices * (-2.0 * math.log(ROPE_BASE) / width))
+    angles = lengths.astype(jnp.float32)[:, None] * inverse_freq
+    cosine = jnp.cos(angles)
+    sine = jnp.sin(angles)
+    cosine = jnp.tile(jnp.concatenate([cosine, cosine], axis=1), (rows // sessions, 1))
+    sine = jnp.tile(jnp.concatenate([-sine, sine], axis=1), (rows // sessions, 1))
+    limits = jnp.repeat(lengths, cache_len)[None, :]
+    return pl.pallas_call(
+        attend_kernel,
+        out_shape=jax.ShapeDtypeStruct((devices * TILE, width), jnp.bfloat16),
+        compiler_params=pltpu.CompilerParams(vmem_limit_bytes=24 * MIB),
+        cost_estimate=pl.CostEstimate(
+            flops=150_000_000, bytes_accessed=3_000_000, transcendentals=300_000
+        ),
+    )(received, keys, values, cosine, sine, limits)
+
+
+def on_block(
+    tokens, norm_gain, w_query, w_keyval, w_out, cache_keys, cache_values, session_ids, lengths, devices
+):
+    source = row_devices(devices)
+    pack_tokens = functools.partial(norm_pack, gain=norm_gain)
+    gathered = gather_rows(tokens, pack_tokens, devices)
+    local = project_query(gathered, w_query, w_keyval, session_ids[source], devices)
+    received = lax.all_to_all(local, "wide", split_axis=0, concat_axis=0, tiled=True)
+    attended = attend(received, cache_keys, cache_values, lengths)
+    gathered = gather_rows(attended, pack, devices)
+    return project_out(gathered, w_out, source, session_ids, devices)
+
+
+def fits_block(devices, tokens, w_query, w_keyval, cache_keys):
+    sessions, kv_heads, cache_len, width = cache_keys.shape
+    return (
+        devices == 32
+        and tokens.shape[0] == PIECE
+        and sessions == PIECE
+        and width == LANES
+        and cache_len == LANES
+        and kv_heads == KVH
+        and w_query.shape[1] == 4 * LANES
+        and w_keyval.shape[0] == LANES // 2
+    )
+
+
+def on_device(*args, devices):
+    tokens, _, w_query, w_keyval, _, cache_keys = args[:6]
+    if fits_block(devices, tokens, w_query, w_keyval, cache_keys):
+        return on_block(*args, devices)
+    return on_any(*args)
+
+
 def solution(mesh):
     return jax.shard_map(
-        on_device,
+        functools.partial(on_device, devices=mesh.shape["wide"]),
         mesh=mesh,
         in_specs=(
             P(("groups", "wide"), None),

time: 208 us -> 142 us (0.68)
  waiting for transfers between devices: 134 us -> 62.5 us
  Pallas kernels: 0 us -> 26.4 us
  matrix products: 23.2 us -> 0 us
  starting transfers between devices: 5.77 us -> 28.5 us
  between operations: 13.6 us -> 0.18 us
  other arithmetic: 7.75 us -> 0.32 us
    all_gather x2 -> x0, waiting for transfers between devices: 121 us -> none  [the longest x1 61.4 us: on_device(): everyone = lax.all_gather(normed, 'wide', axis=0, tiled=True)]
    ppermute x0 -> x32, waiting for transfers between devices: none -> 52.1 us  [swapped(): return lax.ppermute(array, 'wide', [(i, i ^ mask) for i in range(devices)])]
    pallas_call x0 -> x5, Pallas kernels: none -> 26.4 us  [the longest x1 11.6 us: project_query(): pl.pallas_call(functools.partial(query_kernel, steps=STEPS), grid=(STEPS,...]
    ppermute x0 -> x32, starting transfers between devices: none -> 24.2 us  [swapped(): return lax.ppermute(array, 'wide', [(i, i ^ mask) for i in range(devices)])]
    dot_general x6 -> x0, matrix products: 23.2 us -> none  [the longest x1 9.51 us: on_device(): jnp.dot(everyone, w_query, preferred_element_type=jnp.float32)]
    unnamed x15 -> x34, local copies, waits for them, and re-layouts: 15.4 us -> 20.1 us
    sort x1 -> x0, other arithmetic: 3.22 us -> none  [on_device(): inverse = jnp.argsort(session_ids)]
    all_to_all x2 -> x1, waiting for transfers between devices: 13.3 us -> 10.4 us  [on_block(): lax.all_to_all(local, 'wide', split_axis=0, concat_axis=0, tiled=True)]
  transfers between devices with their start and end apart: 4 -> 33, of which waited for: 4 -> 17; matrix products, arithmetic and copies ran while one was open for 3% -> 1% of each run, Pallas kernels for 0% -> 0%
where the time goes in v1:
time: 142 us; the launch traced here: 140 us
  waiting for transfers between devices  62.5 us (44%)
  starting transfers between devices  28.5 us (20%)
  Pallas kernels  26.4 us (19%)
  local copies, waits for them, and re-layouts  21.9 us (15%)
    ppermute x32, waiting for transfers between devices, swapped(): return lax.ppermute(array, 'wide', [(i, i ^ mask) for i in range(devices)])  52.1 us
    ppermute x32, starting transfers between devices, swapped(): return lax.ppermute(array, 'wide', [(i, i ^ mask) for i in range(devices)])  24.2 us
    unnamed x34, local copies, waits for them, and re-layouts  20.1 us
    pallas_call x1, Pallas kernels, project_query(): pl.pallas_call(functools.partial(query_kernel, steps=STEPS), grid=(STEPS,...  11.6 us
    all_to_all x1, waiting for transfers between devices, on_block(): lax.all_to_all(local, 'wide', split_axis=0, concat_axis=0, tiled=True)  10.4 us
    pallas_call x1, Pallas kernels, project_out(): pl.pallas_call(functools.partial(out_kernel, steps=STEPS), grid=(STEPS,),...  10.1 us
    all_to_all x1, starting transfers between devices, on_block(): lax.all_to_all(local, 'wide', split_axis=0, concat_axis=0, tiled=True)  4.27 us
    pallas_call x1, Pallas kernels, attend(): pl.pallas_call(attend_kernel, out_shape=jax.ShapeDtypeStruct((devices * T...  3.14 us
  transfers between devices with their start and end apart: 33, of which 17 were waited for; matrix products, arithmetic and copies ran while one was open for 1% of the time, Pallas kernels for 0%

profile of v1, /device:TPU:0, one launch (start us, length us, event | category | flops | bytes accessed | tf_op | source)
XLA Modules:
  0.0 139.7 jit_solution(13022127621588005312)
XLA Ops:
  0.0 3.0 %collective-permute-start = (bf16[4,16384]{1,0:T(4,128)(2,1)}, bf16[4,16384]{1,0:T(4,128)(2,1)S(1)}, u32[]{:S(2)}, u32[]{:S(2)}) collective-permute-start(bf16[4,16384]{1,0:T(4,128)(2,1)} %own.1), channel_id=1, source_target_pairs={{0,8},{1,9},{2,10},{3,11},{4,12},{5,13},{6,14},{7,15},{8,0},{9,1},... | collective-permute-start | bytes 393224 | tf_op jit(solution)/shard_map/ppermute | solution.py:174
  3.0 2.6 %collective-permute-start.1 = (bf16[4,16384]{1,0:T(4,128)(2,1)}, bf16[4,16384]{1,0:T(4,128)(2,1)S(1)}, u32[]{:S(2)}, u32[]{:S(2)}) collective-permute-start(bf16[4,16384]{1,0:T(4,128)(2,1)} %own.1), channel_id=1, source_target_pairs={{0,16},{1,17},{2,18},{3,19},{4,20},{5,21},{6,22},{7,23},{8,24},{9,... | collective-permute-start | bytes 393224 | tf_op jit(solution)/shard_map/ppermute | solution.py:174
  5.6 2.6 %collective-permute-done.z1 = bf16[4,16384]{1,0:T(4,128)(2,1)S(1)} collective-permute-done((bf16[4,16384]{1,0:T(4,128)(2,1)}, bf16[4,16384]{1,0:T(4,128)(2,1)S(1)}, u32[]{:S(2)}, u32[]{:S(2)}) %collective-permute-start) | collective-permute-done | bytes 131104 | tf_op jit(solution)/shard_map/ppermute | solution.py:174
  8.3 7.9 %collective-permute-done.1.z2 = bf16[4,16384]{1,0:T(4,128)(2,1)S(1)} collective-permute-done((bf16[4,16384]{1,0:T(4,128)(2,1)}, bf16[4,16384]{1,0:T(4,128)(2,1)S(1)}, u32[]{:S(2)}, u32[]{:S(2)}) %collective-permute-start.1) | collective-permute-done | bytes 131104 | tf_op jit(solution)/shard_map/ppermute | solution.py:174
  17.9 1.4 %shard_map.91 = (bf16[64,16,128]{2,1,0:T(8,128)(2,1)S(1)}, bf16[64,16,128]{2,1,0:T(8,128)(2,1)S(1)}, bf16[128,16,128]{2,1,0:T(8,128)(2,1)}) custom-call(bf16[4,16384]{1,0:T(4,128)(2,1)S(1)} %copy-done.13, bf16[4,16384]{1,0:T(4,128)(2,1)S(1)} %collective-permute-done.z1, bf16[4,16384]{1,0:T(4,128)(2,1)S(1)} %collective-permute-done.1.z2, ...), custom_call_target="tpu_custom_call" | custom-call | flops 4000000 | bytes 2000000 | tf_op jit(solution)/shard_map/pallas_call | solution.py:155
  19.3 1.5 %collective-permute-start.3 = (bf16[64,16,128]{2,1,0:T(8,128)(2,1)S(1)}, bf16[64,16,128]{2,1,0:T(8,128)(2,1)S(1)}, u32[]{:S(2)}, u32[]{:S(2)}) collective-permute-start(bf16[64,16,128]{2,1,0:T(8,128)(2,1)S(1)} %get-tuple-element.11.refs_0_), channel_id=1, source_target_pairs={{0,2},{1,3},{2,0},{3,1},{4,6},{5,7},{6,4},{7,5},{8,10},{9,11},{10,... | collective-permute-start | bytes 786440 | tf_op jit(solution)/shard_map/ppermute | solution.py:174
  20.8 1.5 %collective-permute-start.4 = (bf16[64,16,128]{2,1,0:T(8,128)(2,1)S(1)}, bf16[64,16,128]{2,1,0:T(8,128)(2,1)S(1)}, u32[]{:S(2)}, u32[]{:S(2)}) collective-permute-start(bf16[64,16,128]{2,1,0:T(8,128)(2,1)S(1)} %get-tuple-element.11.refs_0_), channel_id=1, source_target_pairs={{0,4},{1,5},{2,6},{3,7},{4,0},{5,1},{6,2},{7,3},{8,12},{9,13},{10,... | collective-permute-start | bytes 786440 | tf_op jit(solution)/shard_map/ppermute | solution.py:174
  23.4 2.6 %collective-permute-done.3.refs_1_ = bf16[64,16,128]{2,1,0:T(8,128)(2,1)S(1)} collective-permute-done((bf16[64,16,128]{2,1,0:T(8,128)(2,1)S(1)}, bf16[64,16,128]{2,1,0:T(8,128)(2,1)S(1)}, u32[]{:S(2)}, u32[]{:S(2)}) %collective-permute-start.3) | collective-permute-done | bytes 262176 | tf_op jit(solution)/shard_map/ppermute | solution.py:174
  26.0 1.5 %collective-permute-start.5 = (bf16[64,16,128]{2,1,0:T(8,128)(2,1)S(1)}, bf16[64,16,128]{2,1,0:T(8,128)(2,1)S(1)}, u32[]{:S(2)}, u32[]{:S(2)}) collective-permute-start(bf16[64,16,128]{2,1,0:T(8,128)(2,1)S(1)} %collective-permute-done.3.refs_1_), channel_id=1, source_target_pairs={{0,4},{1,5},{2,6},{3,7},{4,0},{5,1},{6,2},{7,3},{8,12},{9,13},{10,... | collective-permute-start | bytes 786440 | tf_op jit(solution)/shard_map/ppermute | solution.py:174
  27.5 2.5 %collective-permute-done.4.refs_2_ = bf16[64,16,128]{2,1,0:T(8,128)(2,1)S(1)} collective-permute-done((bf16[64,16,128]{2,1,0:T(8,128)(2,1)S(1)}, bf16[64,16,128]{2,1,0:T(8,128)(2,1)S(1)}, u32[]{:S(2)}, u32[]{:S(2)}) %collective-permute-start.4) | collective-permute-done | bytes 262176 | tf_op jit(solution)/shard_map/ppermute | solution.py:174
  29.9 5.6 %collective-permute-done.11.refs_10_ = bf16[64,16,128]{2,1,0:T(8,128)(2,1)S(1)} collective-permute-done((bf16[64,16,128]{2,1,0:T(8,128)(2,1)S(1)}, bf16[64,16,128]{2,1,0:T(8,128)(2,1)S(1)}, u32[]{:S(2)}, u32[]{:S(2)}) %collective-permute-start.11) | collective-permute-done | bytes 262176 | tf_op jit(solution)/shard_map/ppermute | solution.py:174
  36.2 4.6 %collective-permute-done.5.refs_3_ = bf16[64,16,128]{2,1,0:T(8,128)(2,1)S(1)} collective-permute-done((bf16[64,16,128]{2,1,0:T(8,128)(2,1)S(1)}, bf16[64,16,128]{2,1,0:T(8,128)(2,1)S(1)}, u32[]{:S(2)}, u32[]{:S(2)}) %collective-permute-start.5) | collective-permute-done | bytes 262176 | tf_op jit(solution)/shard_map/ppermute | solution.py:174
  43.2 1.6 %gather_fusion = s32[128]{0:T(128)S(1)} fusion(s32[128]{0:T(128)} %param.16, s32[1024]{0:T(1024)S(1)} %pad_clamp_fusion), kind=kCustom, calls=%fused_computation | custom fusion | bytes 1536 | tf_op jit(solution)/shard_map/gather | solution.py:445
  45.1 5.8 %copy-done = bf16[16384,512]{1,0:T(8,128)(2,1)S(1)} copy-done((bf16[16384,512]{1,0:T(8,128)(2,1)S(1)}, bf16[16384,512]{1,0:T(8,128)(2,1)}, u32[]{:S(2)}) %copy-start) | copy-done | bytes 16777240
  50.9 1.6 %copy-done.2 = bf16[64,16384]{1,0:T(8,128)(2,1)S(1)} copy-done((bf16[64,16384]{1,0:T(8,128)(2,1)S(1)}, bf16[64,16384]{1,0:T(8,128)(2,1)}, u32[]{:S(2)}) %copy-start.2) | copy-done | bytes 2097176
  56.3 11.6 %shard_map.92 = bf16[32,32,128]{2,1,0:T(8,128)(2,1)} custom-call(bf16[64,16,128]{2,1,0:T(8,128)(2,1)S(1)} %get-tuple-element.11.refs_0_, bf16[64,16,128]{2,1,0:T(8,128)(2,1)S(1)} %collective-permute-done.3.refs_1_, bf16[64,16,128]{2,1,0:T(8,128)(2,1)S(1)} %copy-done.6, bf16[64,16,128]{2,1,0:T(8,128)(2,1)S(1)} %copy-done.12, ...), custom_call_target="tpu_custom_call" | custom-call | flops 2147483648 | bytes 20971520 | tf_op jit(solution)/shard_map/pallas_call | solution.py:312
  67.8 4.3 %all-to-all-start = ((bf16[32,32,128]{2,1,0:T(8,128)(2,1)}), bf16[32,32,128]{2,1,0:T(8,128)(2,1)S(1)}, u32[]{:S(2)}, u32[]{:S(2)}) async-start(bf16[32,32,128]{2,1,0:T(8,128)(2,1)} %shard_map.92), calls=%async_computation | async-start | bytes 524288 | tf_op jit(solution)/shard_map/all_to_all | solution.py:446
  72.3 10.4 %all-to-all-done.received = bf16[32,32,128]{2,1,0:T(8,128)(2,1)S(1)} async-done(((bf16[32,32,128]{2,1,0:T(8,128)(2,1)}), bf16[32,32,128]{2,1,0:T(8,128)(2,1)S(1)}, u32[]{:S(2)}, u32[]{:S(2)}) %all-to-all-start) | async-done | bytes 262176 | tf_op jit(solution)/shard_map/all_to_all | solution.py:446
  82.8 3.1 %shard_map.93.own = bf16[512,128]{1,0:T(8,128)(2,1)S(1)} custom-call(bf16[32,32,128]{2,1,0:T(8,128)(2,1)S(1)} %all-to-all-done.received, bf16[4,8,128,128]{3,2,1,0:T(8,128)(2,1)S(1)} %copy-done.3, bf16[4,8,128,128]{3,2,1,0:T(8,128)(2,1)S(1)} %copy-done.4, f32[64,128]{1,0:T(8,128)S(1)} %bitcast.10, f32[64,128]{1,0:T(8,128)S(1)} %bitcast.11, s32[1,512]{1,0:T(1,128)S(1)} %bitcast.14), custom_call_target="tpu_custom_call" | custom-call | flops 150000000 | bytes 3000000 | tf_op jit(solution)/shard_map/pallas_call | solution.py:429
  87.9 2.5 %collective-permute-start.18 = (bf16[512,128]{1,0:T(8,128)(2,1)S(1)}, bf16[512,128]{1,0:T(8,128)(2,1)S(1)}, u32[]{:S(2)}, u32[]{:S(2)}) collective-permute-start(bf16[512,128]{1,0:T(8,128)(2,1)S(1)} %shard_map.93.own), channel_id=1, source_target_pairs={{0,24},{1,25},{2,26},{3,27},{4,28},{5,29},{6,30},{7,31},{8,16},{9,... | collective-permute-start | bytes 393224 | tf_op jit(solution)/shard_map/ppermute | solution.py:174
  90.4 2.5 %collective-permute-done.16.z1 = bf16[512,128]{1,0:T(8,128)(2,1)S(1)} collective-permute-done((bf16[512,128]{1,0:T(8,128)(2,1)S(1)}, bf16[512,128]{1,0:T(8,128)(2,1)S(1)}, u32[]{:S(2)}, u32[]{:S(2)}) %collective-permute-start.16) | collective-permute-done | bytes 131104 | tf_op jit(solution)/shard_map/ppermute | solution.py:174
  92.9 6.5 %collective-permute-done.17.z2 = bf16[512,128]{1,0:T(8,128)(2,1)S(1)} collective-permute-done((bf16[512,128]{1,0:T(8,128)(2,1)S(1)}, bf16[512,128]{1,0:T(8,128)(2,1)S(1)}, u32[]{:S(2)}, u32[]{:S(2)}) %collective-permute-start.17) | collective-permute-done | bytes 131104 | tf_op jit(solution)/shard_map/ppermute | solution.py:174
  99.7 1.4 %collective-permute-start.20 = (bf16[64,16,128]{2,1,0:T(8,128)(2,1)S(1)}, bf16[64,16,128]{2,1,0:T(8,128)(2,1)S(1)}, u32[]{:S(2)}, u32[]{:S(2)}) collective-permute-start(bf16[64,16,128]{2,1,0:T(8,128)(2,1)S(1)} %get-tuple-element.14.refs_0_), channel_id=1, source_target_pairs={{0,4},{1,5},{2,6},{3,7},{4,0},{5,1},{6,2},{7,3},{8,12},{9,13},{10,... | collective-permute-start | bytes 786440 | tf_op jit(solution)/shard_map/ppermute | solution.py:174
  101.8 1.9 %collective-permute-start.26 = (bf16[64,16,128]{2,1,0:T(8,128)(2,1)S(1)}, bf16[64,16,128]{2,1,0:T(8,128)(2,1)S(1)}, u32[]{:S(2)}, u32[]{:S(2)}) collective-permute-start(bf16[64,16,128]{2,1,0:T(8,128)(2,1)S(1)} %get-tuple-element.16.refs_8_), channel_id=1, source_target_pairs={{0,2},{1,3},{2,0},{3,1},{4,6},{5,7},{6,4},{7,5},{8,10},{9,11},{10,... | collective-permute-start | bytes 786440 | tf_op jit(solution)/shard_map/ppermute | solution.py:174
  103.6 3.8 %collective-permute-done.19.refs_1_ = bf16[64,16,128]{2,1,0:T(8,128)(2,1)S(1)} collective-permute-done((bf16[64,16,128]{2,1,0:T(8,128)(2,1)S(1)}, bf16[64,16,128]{2,1,0:T(8,128)(2,1)S(1)}, u32[]{:S(2)}, u32[]{:S(2)}) %collective-permute-start.19) | collective-permute-done | bytes 262176 | tf_op jit(solution)/shard_map/ppermute | solution.py:174
  108.8 5.6 %collective-permute-done.27.refs_10_ = bf16[64,16,128]{2,1,0:T(8,128)(2,1)S(1)} collective-permute-done((bf16[64,16,128]{2,1,0:T(8,128)(2,1)S(1)}, bf16[64,16,128]{2,1,0:T(8,128)(2,1)S(1)}, u32[]{:S(2)}, u32[]{:S(2)}) %collective-permute-start.27) | collective-permute-done | bytes 262176 | tf_op jit(solution)/shard_map/ppermute | solution.py:174
  114.5 1.9 %collective-permute-start.28 = (bf16[64,16,128]{2,1,0:T(8,128)(2,1)S(1)}, bf16[64,16,128]{2,1,0:T(8,128)(2,1)S(1)}, u32[]{:S(2)}, u32[]{:S(2)}) collective-permute-start(bf16[64,16,128]{2,1,0:T(8,128)(2,1)S(1)} %collective-permute-done.27.refs_10_), channel_id=1, source_target_pairs={{0,2},{1,3},{2,0},{3,1},{4,6},{5,7},{6,4},{7,5},{8,10},{9,11},{10,... | collective-permute-start | bytes 786440 | tf_op jit(solution)/shard_map/ppermute | solution.py:174
  116.3 3.3 %collective-permute-done.21.refs_3_ = bf16[64,16,128]{2,1,0:T(8,128)(2,1)S(1)} collective-permute-done((bf16[64,16,128]{2,1,0:T(8,128)(2,1)S(1)}, bf16[64,16,128]{2,1,0:T(8,128)(2,1)S(1)}, u32[]{:S(2)}, u32[]{:S(2)}) %collective-permute-start.21) | collective-permute-done | bytes 262176 | tf_op jit(solution)/shard_map/ppermute | solution.py:174
  120.2 1.9 %collective-permute-done.28.refs_11_ = bf16[64,16,128]{2,1,0:T(8,128)(2,1)S(1)} collective-permute-done((bf16[64,16,128]{2,1,0:T(8,128)(2,1)S(1)}, bf16[64,16,128]{2,1,0:T(8,128)(2,1)S(1)}, u32[]{:S(2)}, u32[]{:S(2)}) %collective-permute-start.28) | collective-permute-done | bytes 262176 | tf_op jit(solution)/shard_map/ppermute | solution.py:174
  122.3 1.5 %collective-permute-done.31.refs_15_ = bf16[64,16,128]{2,1,0:T(8,128)(2,1)} collective-permute-done((bf16[64,16,128]{2,1,0:T(8,128)(2,1)S(1)}, bf16[64,16,128]{2,1,0:T(8,128)(2,1)}, u32[]{:S(2)}, u32[]{:S(2)}) %collective-permute-start.31) | collective-permute-done | bytes 262176 | tf_op jit(solution)/shard_map/ppermute | solution.py:174
  123.8 5.8 %copy-done.1 = bf16[16384,512]{1,0:T(8,128)(2,1)S(1)} copy-done((bf16[16384,512]{1,0:T(8,128)(2,1)S(1)}, bf16[16384,512]{1,0:T(8,128)(2,1)}, u32[]{:S(2)}) %copy-start.1) | copy-done | bytes 16777240
  129.6 10.1 %shard_map.95 = bf16[128,512]{1,0:T(8,128)(2,1)} custom-call(bf16[64,16,128]{2,1,0:T(8,128)(2,1)S(1)} %get-tuple-element.14.refs_0_, bf16[64,16,128]{2,1,0:T(8,128)(2,1)S(1)} %collective-permute-done.19.refs_1_, bf16[64,16,128]{2,1,0:T(8,128)(2,1)S(1)} %collective-permute-done.20.refs_2_, bf16[64,16,128]{2,1,0:T(8,128)(2,1)S(1)} %collective-permute-done.21.refs_3_, ...), custom_call_target="tpu_custom_call" | custom-call | flops 2147483648 | bytes 20971520 | tf_op jit(solution)/shard_map/pallas_call | solution.py:341
  (87 shorter events, 15.3 us)
Async XLA Ops:
  0.0 8.3 %collective-permute-start = (bf16[4,16384]{1,0:T(4,128)(2,1)}, bf16[4,16384]{1,0:T(4,128)(2,1)S(1)}, u32[]{:S(2)}, u32[]{:S(2)}) collective-permute-start(bf16[4,16384]{1,0:T(4,128)(2,1)} %own.1), channel_id=1, source_target_pairs={{0,8},{1,9},{2,10},{3,11},{4,12},{5,13},{6,14},{7,15},{8,0},{9,1},... | collective-permute-start | bytes 393224 | tf_op jit(solution)/shard_map/ppermute | solution.py:174
  3.0 13.2 %collective-permute-start.1 = (bf16[4,16384]{1,0:T(4,128)(2,1)}, bf16[4,16384]{1,0:T(4,128)(2,1)S(1)}, u32[]{:S(2)}, u32[]{:S(2)}) collective-permute-start(bf16[4,16384]{1,0:T(4,128)(2,1)} %own.1), channel_id=1, source_target_pairs={{0,16},{1,17},{2,18},{3,19},{4,20},{5,21},{6,22},{7,23},{8,24},{9,... | collective-permute-start | bytes 393224 | tf_op jit(solution)/shard_map/ppermute | solution.py:174
  5.6 10.6 %collective-permute-start.2 = (bf16[4,16384]{1,0:T(4,128)(2,1)}, bf16[4,16384]{1,0:T(4,128)(2,1)S(1)}, u32[]{:S(2)}, u32[]{:S(2)}) collective-permute-start(bf16[4,16384]{1,0:T(4,128)(2,1)} %own.1), channel_id=1, source_target_pairs={{0,24},{1,25},{2,26},{3,27},{4,28},{5,29},{6,30},{7,31},{8,16},{9,... | collective-permute-start | bytes 393224 | tf_op jit(solution)/shard_map/ppermute | solution.py:174
  19.3 6.6 %collective-permute-start.3 = (bf16[64,16,128]{2,1,0:T(8,128)(2,1)S(1)}, bf16[64,16,128]{2,1,0:T(8,128)(2,1)S(1)}, u32[]{:S(2)}, u32[]{:S(2)}) collective-permute-start(bf16[64,16,128]{2,1,0:T(8,128)(2,1)S(1)} %get-tuple-element.11.refs_0_), channel_id=1, source_target_pairs={{0,2},{1,3},{2,0},{3,1},{4,6},{5,7},{6,4},{7,5},{8,10},{9,11},{10,... | collective-permute-start | bytes 786440 | tf_op jit(solution)/shard_map/ppermute | solution.py:174
  20.8 20.0 %collective-permute-start.6 = (bf16[128,16,128]{2,1,0:T(8,128)(2,1)}, bf16[128,16,128]{2,1,0:T(8,128)(2,1)S(1)}, u32[]{:S(2)}, u32[]{:S(2)}) collective-permute-start(bf16[128,16,128]{2,1,0:T(8,128)(2,1)} %get-tuple-element.12), channel_id=1, source_target_pairs={{0,1},{1,0},{2,3},{3,2},{4,5},{5,4},{6,7},{7,6},{8,9},{9,8},{10,11... | collective-permute-start | bytes 1572872 | tf_op jit(solution)/shard_map/ppermute | solution.py:174
  20.8 9.1 %collective-permute-start.4 = (bf16[64,16,128]{2,1,0:T(8,128)(2,1)S(1)}, bf16[64,16,128]{2,1,0:T(8,128)(2,1)S(1)}, u32[]{:S(2)}, u32[]{:S(2)}) collective-permute-start(bf16[64,16,128]{2,1,0:T(8,128)(2,1)S(1)} %get-tuple-element.11.refs_0_), channel_id=1, source_target_pairs={{0,4},{1,5},{2,6},{3,7},{4,0},{5,1},{6,2},{7,3},{8,12},{9,13},{10,... | collective-permute-start | bytes 786440 | tf_op jit(solution)/shard_map/ppermute | solution.py:174
  22.4 13.2 %collective-permute-start.11 = (bf16[64,16,128]{2,1,0:T(8,128)(2,1)S(1)}, bf16[64,16,128]{2,1,0:T(8,128)(2,1)S(1)}, u32[]{:S(2)}, u32[]{:S(2)}) collective-permute-start(bf16[64,16,128]{2,1,0:T(8,128)(2,1)S(1)} %get-tuple-element.13.refs_8_), channel_id=1, source_target_pairs={{0,4},{1,5},{2,6},{3,7},{4,0},{5,1},{6,2},{7,3},{8,12},{9,13},{10,... | collective-permute-start | bytes 786440 | tf_op jit(solution)/shard_map/ppermute | solution.py:174
  22.9 13.3 %collective-permute-start.10 = (bf16[64,16,128]{2,1,0:T(8,128)(2,1)S(1)}, bf16[64,16,128]{2,1,0:T(8,128)(2,1)S(1)}, u32[]{:S(2)}, u32[]{:S(2)}) collective-permute-start(bf16[64,16,128]{2,1,0:T(8,128)(2,1)S(1)} %get-tuple-element.13.refs_8_), channel_id=1, source_target_pairs={{0,2},{1,3},{2,0},{3,1},{4,6},{5,7},{6,4},{7,5},{8,10},{9,11},{10,... | collective-permute-start | bytes 786440 | tf_op jit(solution)/shard_map/ppermute | solution.py:174
  26.0 14.8 %collective-permute-start.5 = (bf16[64,16,128]{2,1,0:T(8,128)(2,1)S(1)}, bf16[64,16,128]{2,1,0:T(8,128)(2,1)S(1)}, u32[]{:S(2)}, u32[]{:S(2)}) collective-permute-start(bf16[64,16,128]{2,1,0:T(8,128)(2,1)S(1)} %collective-permute-done.3.refs_1_), channel_id=1, source_target_pairs={{0,4},{1,5},{2,6},{3,7},{4,0},{5,1},{6,2},{7,3},{8,12},{9,13},{10,... | collective-permute-start | bytes 786440 | tf_op jit(solution)/shard_map/ppermute | solution.py:174
  29.9 12.1 %collective-permute-start.7 = (bf16[64,16,128]{2,1,0:T(8,128)(2,1)S(1)}, bf16[64,16,128]{2,1,0:T(8,128)(2,1)}, u32[]{:S(2)}, u32[]{:S(2)}) collective-permute-start(bf16[64,16,128]{2,1,0:T(8,128)(2,1)S(1)} %collective-permute-done.3.refs_1_), channel_id=1, source_target_pairs={{0,1},{1,0},{2,3},{3,2},{4,5},{5,4},{6,7},{7,6},{8,9},{9,8},{10,11... | collective-permute-start | bytes 786440 | tf_op jit(solution)/shard_map/ppermute | solution.py:174
  35.6 7.7 %collective-permute-start.12 = (bf16[64,16,128]{2,1,0:T(8,128)(2,1)S(1)}, bf16[64,16,128]{2,1,0:T(8,128)(2,1)}, u32[]{:S(2)}, u32[]{:S(2)}) collective-permute-start(bf16[64,16,128]{2,1,0:T(8,128)(2,1)S(1)} %collective-permute-done.11.refs_10_), channel_id=1, source_target_pairs={{0,2},{1,3},{2,0},{3,1},{4,6},{5,7},{6,4},{7,5},{8,10},{9,11},{10,... | collective-permute-start | bytes 786440 | tf_op jit(solution)/shard_map/ppermute | solution.py:174
  36.1 8.8 %collective-permute-start.14 = (bf16[64,16,128]{2,1,0:T(8,128)(2,1)S(1)}, bf16[64,16,128]{2,1,0:T(8,128)(2,1)}, u32[]{:S(2)}, u32[]{:S(2)}) collective-permute-start(bf16[64,16,128]{2,1,0:T(8,128)(2,1)S(1)} %collective-permute-done.11.refs_10_), channel_id=1, source_target_pairs={{0,1},{1,0},{2,3},{3,2},{4,5},{5,4},{6,7},{7,6},{8,9},{9,8},{10,11... | collective-permute-start | bytes 786440 | tf_op jit(solution)/shard_map/ppermute | solution.py:174
  40.8 4.1 %collective-permute-start.8 = (bf16[64,16,128]{2,1,0:T(8,128)(2,1)S(1)}, bf16[64,16,128]{2,1,0:T(8,128)(2,1)}, u32[]{:S(2)}, u32[]{:S(2)}) collective-permute-start(bf16[64,16,128]{2,1,0:T(8,128)(2,1)S(1)} %collective-permute-done.4.refs_2_), channel_id=1, source_target_pairs={{0,1},{1,0},{2,3},{3,2},{4,5},{5,4},{6,7},{7,6},{8,9},{9,8},{10,11... | collective-permute-start | bytes 786440 | tf_op jit(solution)/shard_map/ppermute | solution.py:174
  40.8 4.1 %collective-permute-start.13 = (bf16[64,16,128]{2,1,0:T(8,128)(2,1)S(1)}, bf16[64,16,128]{2,1,0:T(8,128)(2,1)}, u32[]{:S(2)}, u32[]{:S(2)}) collective-permute-start(bf16[64,16,128]{2,1,0:T(8,128)(2,1)S(1)} %collective-permute-done.10.refs_9_), channel_id=1, source_target_pairs={{0,1},{1,0},{2,3},{3,2},{4,5},{5,4},{6,7},{7,6},{8,9},{9,8},{10,11... | collective-permute-start | bytes 786440 | tf_op jit(solution)/shard_map/ppermute | solution.py:174
  42.0 2.9 %collective-permute-start.9 = (bf16[64,16,128]{2,1,0:T(8,128)(2,1)S(1)}, bf16[64,16,128]{2,1,0:T(8,128)(2,1)}, u32[]{:S(2)}, u32[]{:S(2)}) collective-permute-start(bf16[64,16,128]{2,1,0:T(8,128)(2,1)S(1)} %collective-permute-done.5.refs_3_), channel_id=1, source_target_pairs={{0,1},{1,0},{2,3},{3,2},{4,5},{5,4},{6,7},{7,6},{8,9},{9,8},{10,11... | collective-permute-start | bytes 786440 | tf_op jit(solution)/shard_map/ppermute | solution.py:174
  43.2 1.9 %collective-permute-start.15 = (bf16[64,16,128]{2,1,0:T(8,128)(2,1)}, bf16[64,16,128]{2,1,0:T(8,128)(2,1)}, u32[]{:S(2)}, u32[]{:S(2)}) collective-permute-start(bf16[64,16,128]{2,1,0:T(8,128)(2,1)} %collective-permute-done.12.refs_11_), channel_id=1, source_target_pairs={{0,1},{1,0},{2,3},{3,2},{4,5},{5,4},{6,7},{7,6},{8,9},{9,8},{10,11... | collective-permute-start | bytes 786440 | tf_op jit(solution)/shard_map/ppermute | solution.py:174
  67.8 14.9 %all-to-all-start = ((bf16[32,32,128]{2,1,0:T(8,128)(2,1)}), bf16[32,32,128]{2,1,0:T(8,128)(2,1)S(1)}, u32[]{:S(2)}, u32[]{:S(2)}) async-start(bf16[32,32,128]{2,1,0:T(8,128)(2,1)} %shard_map.92), calls=%async_computation | async-start | bytes 524288 | tf_op jit(solution)/shard_map/all_to_all | solution.py:446
  85.9 7.0 %collective-permute-start.16 = (bf16[512,128]{1,0:T(8,128)(2,1)S(1)}, bf16[512,128]{1,0:T(8,128)(2,1)S(1)}, u32[]{:S(2)}, u32[]{:S(2)}) collective-permute-start(bf16[512,128]{1,0:T(8,128)(2,1)S(1)} %shard_map.93.own), channel_id=1, source_target_pairs={{0,8},{1,9},{2,10},{3,11},{4,12},{5,13},{6,14},{7,15},{8,0},{9,1},... | collective-permute-start | bytes 393224 | tf_op jit(solution)/shard_map/ppermute | solution.py:174
  86.9 12.5 %collective-permute-start.17 = (bf16[512,128]{1,0:T(8,128)(2,1)S(1)}, bf16[512,128]{1,0:T(8,128)(2,1)S(1)}, u32[]{:S(2)}, u32[]{:S(2)}) collective-permute-start(bf16[512,128]{1,0:T(8,128)(2,1)S(1)} %shard_map.93.own), channel_id=1, source_target_pairs={{0,16},{1,17},{2,18},{3,19},{4,20},{5,21},{6,22},{7,23},{8,24},{9,... | collective-permute-start | bytes 393224 | tf_op jit(solution)/shard_map/ppermute | solution.py:174
  87.9 11.5 %collective-permute-start.18 = (bf16[512,128]{1,0:T(8,128)(2,1)S(1)}, bf16[512,128]{1,0:T(8,128)(2,1)S(1)}, u32[]{:S(2)}, u32[]{:S(2)}) collective-permute-start(bf16[512,128]{1,0:T(8,128)(2,1)S(1)} %shard_map.93.own), channel_id=1, source_target_pairs={{0,24},{1,25},{2,26},{3,27},{4,28},{5,29},{6,30},{7,31},{8,16},{9,... | collective-permute-start | bytes 393224 | tf_op jit(solution)/shard_map/ppermute | solution.py:174
  99.5 7.9 %collective-permute-start.19 = (bf16[64,16,128]{2,1,0:T(8,128)(2,1)S(1)}, bf16[64,16,128]{2,1,0:T(8,128)(2,1)S(1)}, u32[]{:S(2)}, u32[]{:S(2)}) collective-permute-start(bf16[64,16,128]{2,1,0:T(8,128)(2,1)S(1)} %get-tuple-element.14.refs_0_), channel_id=1, source_target_pairs={{0,2},{1,3},{2,0},{3,1},{4,6},{5,7},{6,4},{7,5},{8,10},{9,11},{10,... | collective-permute-start | bytes 786440 | tf_op jit(solution)/shard_map/ppermute | solution.py:174
  99.7 20.0 %collective-permute-start.22 = (bf16[128,16,128]{2,1,0:T(8,128)(2,1)S(1)}, bf16[128,16,128]{2,1,0:T(8,128)(2,1)S(1)}, u32[]{:S(2)}, u32[]{:S(2)}) collective-permute-start(bf16[128,16,128]{2,1,0:T(8,128)(2,1)S(1)} %get-tuple-element.15), channel_id=1, source_target_pairs={{0,1},{1,0},{2,3},{3,2},{4,5},{5,4},{6,7},{7,6},{8,9},{9,8},{10,11... | collective-permute-start | bytes 1572872 | tf_op jit(solution)/shard_map/ppermute | solution.py:174
  99.7 9.2 %collective-permute-start.20 = (bf16[64,16,128]{2,1,0:T(8,128)(2,1)S(1)}, bf16[64,16,128]{2,1,0:T(8,128)(2,1)S(1)}, u32[]{:S(2)}, u32[]{:S(2)}) collective-permute-start(bf16[64,16,128]{2,1,0:T(8,128)(2,1)S(1)} %get-tuple-element.14.refs_0_), channel_id=1, source_target_pairs={{0,4},{1,5},{2,6},{3,7},{4,0},{5,1},{6,2},{7,3},{8,12},{9,13},{10,... | collective-permute-start | bytes 786440 | tf_op jit(solution)/shard_map/ppermute | solution.py:174
  101.1 13.4 %collective-permute-start.27 = (bf16[64,16,128]{2,1,0:T(8,128)(2,1)S(1)}, bf16[64,16,128]{2,1,0:T(8,128)(2,1)S(1)}, u32[]{:S(2)}, u32[]{:S(2)}) collective-permute-start(bf16[64,16,128]{2,1,0:T(8,128)(2,1)S(1)} %get-tuple-element.16.refs_8_), channel_id=1, source_target_pairs={{0,4},{1,5},{2,6},{3,7},{4,0},{5,1},{6,2},{7,3},{8,12},{9,13},{10,... | collective-permute-start | bytes 786440 | tf_op jit(solution)/shard_map/ppermute | solution.py:174
  101.8 14.6 %collective-permute-start.26 = (bf16[64,16,128]{2,1,0:T(8,128)(2,1)S(1)}, bf16[64,16,128]{2,1,0:T(8,128)(2,1)S(1)}, u32[]{:S(2)}, u32[]{:S(2)}) collective-permute-start(bf16[64,16,128]{2,1,0:T(8,128)(2,1)S(1)} %get-tuple-element.16.refs_8_), channel_id=1, source_target_pairs={{0,2},{1,3},{2,0},{3,1},{4,6},{5,7},{6,4},{7,5},{8,10},{9,11},{10,... | collective-permute-start | bytes 786440 | tf_op jit(solution)/shard_map/ppermute | solution.py:174
  107.4 12.2 %collective-permute-start.21 = (bf16[64,16,128]{2,1,0:T(8,128)(2,1)S(1)}, bf16[64,16,128]{2,1,0:T(8,128)(2,1)S(1)}, u32[]{:S(2)}, u32[]{:S(2)}) collective-permute-start(bf16[64,16,128]{2,1,0:T(8,128)(2,1)S(1)} %collective-permute-done.19.refs_1_), channel_id=1, source_target_pairs={{0,4},{1,5},{2,6},{3,7},{4,0},{5,1},{6,2},{7,3},{8,12},{9,13},{10,... | collective-permute-start | bytes 786440 | tf_op jit(solution)/shard_map/ppermute | solution.py:174
  108.8 11.3 %collective-permute-start.23 = (bf16[64,16,128]{2,1,0:T(8,128)(2,1)S(1)}, bf16[64,16,128]{2,1,0:T(8,128)(2,1)S(1)}, u32[]{:S(2)}, u32[]{:S(2)}) collective-permute-start(bf16[64,16,128]{2,1,0:T(8,128)(2,1)S(1)} %collective-permute-done.19.refs_1_), channel_id=1, source_target_pairs={{0,1},{1,0},{2,3},{3,2},{4,5},{5,4},{6,7},{7,6},{8,9},{9,8},{10,11... | collective-permute-start | bytes 786440 | tf_op jit(solution)/shard_map/ppermute | solution.py:174
  114.5 7.7 %collective-permute-start.28 = (bf16[64,16,128]{2,1,0:T(8,128)(2,1)S(1)}, bf16[64,16,128]{2,1,0:T(8,128)(2,1)S(1)}, u32[]{:S(2)}, u32[]{:S(2)}) collective-permute-start(bf16[64,16,128]{2,1,0:T(8,128)(2,1)S(1)} %collective-permute-done.27.refs_10_), channel_id=1, source_target_pairs={{0,2},{1,3},{2,0},{3,1},{4,6},{5,7},{6,4},{7,5},{8,10},{9,11},{10,... | collective-permute-start | bytes 786440 | tf_op jit(solution)/shard_map/ppermute | solution.py:174
  116.3 6.0 %collective-permute-start.30 = (bf16[64,16,128]{2,1,0:T(8,128)(2,1)S(1)}, bf16[64,16,128]{2,1,0:T(8,128)(2,1)S(1)}, u32[]{:S(2)}, u32[]{:S(2)}) collective-permute-start(bf16[64,16,128]{2,1,0:T(8,128)(2,1)S(1)} %collective-permute-done.27.refs_10_), channel_id=1, source_target_pairs={{0,1},{1,0},{2,3},{3,2},{4,5},{5,4},{6,7},{7,6},{8,9},{9,8},{10,11... | collective-permute-start | bytes 786440 | tf_op jit(solution)/shard_map/ppermute | solution.py:174
  119.6 2.7 %collective-permute-start.24 = (bf16[64,16,128]{2,1,0:T(8,128)(2,1)S(1)}, bf16[64,16,128]{2,1,0:T(8,128)(2,1)S(1)}, u32[]{:S(2)}, u32[]{:S(2)}) collective-permute-start(bf16[64,16,128]{2,1,0:T(8,128)(2,1)S(1)} %collective-permute-done.20.refs_2_), channel_id=1, source_target_pairs={{0,1},{1,0},{2,3},{3,2},{4,5},{5,4},{6,7},{7,6},{8,9},{9,8},{10,11... | collective-permute-start | bytes 786440 | tf_op jit(solution)/shard_map/ppermute | solution.py:174
  119.6 2.7 %collective-permute-start.29 = (bf16[64,16,128]{2,1,0:T(8,128)(2,1)S(1)}, bf16[64,16,128]{2,1,0:T(8,128)(2,1)}, u32[]{:S(2)}, u32[]{:S(2)}) collective-permute-start(bf16[64,16,128]{2,1,0:T(8,128)(2,1)S(1)} %collective-permute-done.26.refs_9_), channel_id=1, source_target_pairs={{0,1},{1,0},{2,3},{3,2},{4,5},{5,4},{6,7},{7,6},{8,9},{9,8},{10,11... | collective-permute-start | bytes 786440 | tf_op jit(solution)/shard_map/ppermute | solution.py:174
  120.1 2.2 %collective-permute-start.25 = (bf16[64,16,128]{2,1,0:T(8,128)(2,1)S(1)}, bf16[64,16,128]{2,1,0:T(8,128)(2,1)}, u32[]{:S(2)}, u32[]{:S(2)}) collective-permute-start(bf16[64,16,128]{2,1,0:T(8,128)(2,1)S(1)} %collective-permute-done.21.refs_3_), channel_id=1, source_target_pairs={{0,1},{1,0},{2,3},{3,2},{4,5},{5,4},{6,7},{7,6},{8,9},{9,8},{10,11... | collective-permute-start | bytes 786440 | tf_op jit(solution)/shard_map/ppermute | solution.py:174
  (18 other events, 314.2 us)

commit v2 on v0

--- a/solution.py
+++ b/solution.py
@@ -1,8 +1,11 @@
+import functools
 import math
 
 import jax
 import jax.numpy as jnp
 from jax import lax
+from jax.experimental import pallas as pl
+from jax.experimental.pallas import tpu as pltpu
 from jax.sharding import PartitionSpec as P
 
 HEADS = 128
@@ -10,6 +13,11 @@
 
 
 ROPE_BASE = 500000.0
+
+LANES = 128
+PIECE = 4
+TILE = 16
+MIB = 1 << 20
 
 
 def rms_rows(rows, gain):
@@ -70,7 +78,7 @@
     return attended.reshape(sessions, HEADS * head_dim).astype(jnp.bfloat16)
 
 
-def on_device(
+def on_any(
     tokens, norm_gain, w_query, w_keyval, w_out, cache_keys, cache_values, session_ids, lengths
 ):
     normed = rms_rows(tokens, norm_gain)
@@ -95,9 +103,377 @@
     return out_sess[session_ids].astype(jnp.bfloat16)
 
 
+def norm_pack_kernel(own, z1, z2, z3, gain, low, high, full):
+    width = own.shape[1]
+    blocks = width // LANES
+    pieces = (own, z1, z2, z3)
+    scales = []
+    for piece in pieces:
+        values = piece[...].astype(jnp.float32)
+        meansq = jnp.sum(values * values, axis=-1, keepdims=True) * (1.0 / width)
+        scales.append(lax.rsqrt(meansq + 1e-05))
+    for block in range(blocks):
+        lanes = slice(block * LANES, (block + 1) * LANES)
+        factor = gain[:, lanes]
+        rows = jnp.concatenate(
+            [piece[:, lanes].astype(jnp.float32) * scale * factor for piece, scale in zip(pieces, scales)],
+            axis=0,
+        ).astype(jnp.bfloat16)
+        full[block] = rows
+        if block < blocks // 2:
+            low[block] = rows
+        else:
+            high[block - blocks // 2] = rows
+
+
+def pack_kernel(own, z1, z2, z3, low, high, full):
+    blocks = own.shape[0] // PIECE
+    pieces = (own, z1, z2, z3)
+    for first in range(0, blocks, 4):
+        tiles = [
+            piece[first * PIECE : (first + 4) * PIECE, :].astype(jnp.float32) for piece in pieces
+        ]
+        for at in range(4):
+            block = first + at
+            rows = jnp.concatenate(
+                [tile[at * PIECE : (at + 1) * PIECE, :] for tile in tiles], axis=0
+            ).astype(jnp.bfloat16)
+            full[block] = rows
+            if block < blocks // 2:
+                low[block] = rows
+            else:
+                high[block - blocks // 2] = rows
+
+
+def packed_shapes(blocks):
+    half = jax.ShapeDtypeStruct((blocks // 2, TILE, LANES), jnp.bfloat16)
+    return (half, half, jax.ShapeDtypeStruct((blocks, TILE, LANES), jnp.bfloat16))
+
+
+def norm_pack(own, z1, z2, z3, gain):
+    blocks = own.shape[1] // LANES
+    return pl.pallas_call(
+        norm_pack_kernel,
+        out_shape=packed_shapes(blocks),
+        compiler_params=pltpu.CompilerParams(vmem_limit_bytes=8 * MIB),
+        cost_estimate=pl.CostEstimate(flops=4_000_000, bytes_accessed=2_000_000, transcendentals=0),
+    )(own, z1, z2, z3, gain[None, :])
+
+
+def pack(own, z1, z2, z3):
+    blocks = own.shape[0] // PIECE
+    return pl.pallas_call(
+        pack_kernel,
+        out_shape=packed_shapes(blocks),
+        compiler_params=pltpu.CompilerParams(vmem_limit_bytes=8 * MIB),
+        cost_estimate=pl.CostEstimate(flops=1_000_000, bytes_accessed=2_000_000, transcendentals=0),
+    )(own, z1, z2, z3)
+
+
+def swapped(array, mask, devices):
+    return lax.ppermute(array, "wide", [(i, i ^ mask) for i in range(devices)])
+
+
+def gather_rows(piece, near, pack_pieces, devices):
+    swap = functools.partial(swapped, devices=devices)
+    z2, z3, z1 = swap(piece, 16), swap(piece, 24), swap(piece, 8)
+    low, high, full = pack_pieces(near, z1, z2, z3)
+    x_low, y_high = swap(low, 2), swap(high, 4)
+    x_high, y_low = swap(high, 2), swap(low, 4)
+    d_low, d_high = swap(x_low, 4), swap(y_high, 2)
+    other = swap(full, 1)
+    mine = [(low, high), (x_low, x_high), (y_low, y_high), (d_low, d_high)]
+    theirs = [(swap(a, 1), swap(b, 1)) for a, b in mine[1:]]
+    return mine, other, theirs
+
+
+def prefetch_kernel(*refs):
+    count = len(refs) // 3
+    copies = [
+        pltpu.make_async_copy(refs[at], refs[count + at], refs[2 * count + at]) for at in range(count)
+    ]
+    for copy in copies:
+        copy.start()
+    for copy in copies:
+        copy.wait()
+
+
+def prefetch(far, near=()):
+    arrays = (*far, *near)
+    return pl.pallas_call(
+        prefetch_kernel,
+        in_specs=[pl.BlockSpec(memory_space=pltpu.HBM)] * len(far)
+        + [pl.BlockSpec(memory_space=pl.ANY)] * len(near),
+        out_specs=[pl.BlockSpec(memory_space=pl.ANY)] * len(arrays),
+        out_shape=[pltpu.VMEM(array.shape, array.dtype) for array in arrays],
+        scratch_shapes=[pltpu.SemaphoreType.DMA] * len(arrays),
+        compiler_params=pltpu.CompilerParams(vmem_limit_bytes=MIB),
+        cost_estimate=pl.CostEstimate(
+            flops=0,
+            bytes_accessed=sum(array.size * array.dtype.itemsize for array in arrays),
+            transcendentals=0,
+        ),
+    )(*[pltpu.with_memory_space_constraint(array, pltpu.HBM) for array in far], *near)
+
+
+def source_rows(me, rows):
+    at = lax.broadcasted_iota(jnp.int32, (1, rows), 1)
+    core = at // (rows // 2)
+    plane = (at // TILE) % 4
+    column = (at // PIECE) % 4
+    return (me ^ (core + 2 * plane + 8 * column)) * PIECE + at % PIECE
+
+
+COUNT = 16
+
+
+def multiply(refs, weight, total, weight_kv=None, total_kv=None):
+    low, high = refs[0:8], refs[8:16]
+    total[...] = jnp.zeros_like(total)
+    if weight_kv is not None:
+        total_kv[...] = jnp.zeros_like(total_kv)
+    half = low[0].shape[0]
+    blocks = 2 * half
+    for parts, base in ((low, 0), (high, half)):
+
+        def add(step, _, parts=parts, base=base):
+            first = step * COUNT
+            columns = []
+            for at in range(COUNT):
+                column = []
+                for ref in parts:
+                    offset = base if ref.shape[0] == blocks else 0
+                    column.append(ref[first + at + offset])
+                columns.append(jnp.concatenate(column, axis=0))
+            rows = jnp.concatenate(columns, axis=1)
+            depth = pl.ds(pl.multiple_of((base + first) * LANES, COUNT * LANES), COUNT * LANES)
+            total[...] += jnp.dot(rows, weight[depth, :], preferred_element_type=jnp.float32)
+            if weight_kv is not None:
+                total_kv[...] += lax.dot_general(
+                    rows, weight_kv[:, depth], (((1,), (1,)), ((), ())), preferred_element_type=jnp.float32
+                )
+
+        lax.fori_loop(0, half // COUNT, add, None)
+
+
+def one_hot(equal):
+    return equal.astype(jnp.float32).astype(jnp.bfloat16)
+
+
+def as_column(row):
+    count = row.shape[1]
+    square = jnp.broadcast_to(row[...].astype(jnp.float32), (count, count))
+    return jnp.transpose(square).astype(jnp.int32)
+
+
+def query_kernel(*refs):
+    weight, weight_kv, sessions, out, total, total_kv = refs[16:]
+    me = lax.axis_index("wide")
+    multiply(refs, weight, total, weight_kv, total_kv)
+    rows, width = total.shape
+    heads = width // LANES
+    devices = rows // PIECE
+    source = source_rows(me, rows)
+    at = lax.broadcasted_iota(jnp.int32, (rows, rows), 0)
+    session = jnp.sum(jnp.where(at == source, as_column(sessions), 0), axis=0, keepdims=True)
+    stacked = jnp.concatenate(
+        [total[:, h * LANES : (h + 1) * LANES].astype(jnp.bfloat16) for h in range(heads)], axis=0
+    )
+    codes = jnp.concatenate([session + h * rows for h in range(heads)], axis=1)
+    at = lax.broadcasted_iota(jnp.int32, (rows * heads, rows * heads), 0)
+    wanted = ((at // PIECE) % heads) * rows + (at // (PIECE * heads)) * PIECE + at % PIECE
+    query = jnp.dot(one_hot(wanted == codes), stacked, preferred_element_type=jnp.float32)
+    out[:, 0:TILE, :] = query.astype(jnp.bfloat16).reshape(devices, TILE, LANES)
+    columns = total_kv.shape[1]
+    at = lax.broadcasted_iota(jnp.int32, (devices * TILE, rows), 0)
+    wanted = jnp.where(at % TILE < PIECE, (at // TILE) * PIECE + at % TILE, -1)
+    keyval = total_kv[...].astype(jnp.bfloat16)
+    ordered = jnp.dot(one_hot(wanted == session), keyval, preferred_element_type=jnp.float32)
+    here = lax.broadcasted_iota(jnp.int32, (columns, LANES), 0)
+    there = lax.broadcasted_iota(jnp.int32, (columns, LANES), 1)
+    place = one_hot(there == here + (me % 2) * columns)
+    placed = jnp.dot(ordered.astype(jnp.bfloat16), place, preferred_element_type=jnp.float32)
+    out[:, TILE : 2 * TILE, :] = placed.astype(jnp.bfloat16).reshape(devices, TILE, LANES)
+
+
+def out_kernel(*refs):
+    weight, sessions, out, total = refs[16:]
+    multiply(refs, weight, total)
+    rows = total.shape[0]
+    source = source_rows(lax.axis_index("wide"), rows)
+    chosen = one_hot(as_column(sessions) == source)
+    rounded = total[...].astype(jnp.bfloat16)
+    out[...] = jnp.dot(chosen, rounded, preferred_element_type=jnp.float32).astype(jnp.bfloat16)
+
+
+def gathered_operands(gathered):
+    mine, other, theirs = gathered
+    operands = []
+    for half in range(2):
+        operands += [pair[half] for pair in mine] + [other] + [pair[half] for pair in theirs]
+    return operands
+
+
+def project(kernel, gathered, weights, session_ids, out_shape, scratch):
+    operands = gathered_operands(gathered) + list(weights) + [session_ids[None, :]]
+    whole = pl.BlockSpec(memory_space=pltpu.VMEM)
+    rows = session_ids.shape[0]
+    depth = weights[0].shape[0]
+    columns = sum(width for width in scratch)
+    return pl.pallas_call(
+        kernel,
+        in_specs=[whole] * len(operands),
+        out_specs=whole,
+        out_shape=jax.ShapeDtypeStruct(out_shape, jnp.bfloat16),
+        scratch_shapes=[pltpu.VMEM((rows, width), jnp.float32) for width in scratch],
+        compiler_params=pltpu.CompilerParams(vmem_limit_bytes=PROJECT_MIB * MIB),
+        cost_estimate=pl.CostEstimate(
+            flops=2 * rows * depth * columns, bytes_accessed=2 * depth * (columns + rows), transcendentals=0
+        ),
+    )(*operands)
+
+
+PROJECT_MIB = 8
+
+
+def attend_kernel(received, keys, values, lengths, out):
+    sessions, kv_heads, cache_len, width = keys.shape
+    devices = received.shape[0]
+    per_group = devices // kv_heads
+    rows = per_group * TILE
+    scale = width ** (-0.5)
+
+    at = lax.broadcasted_iota(jnp.int32, (8, width), 0) % PIECE
+    lane = lax.broadcasted_iota(jnp.int32, (8, width), 1)
+    position = jnp.full((8, width), lengths[0], jnp.int32)
+    for session in range(1, sessions):
+        position = jnp.where(at == session, lengths[session], position)
+    halfway = width // 2
+    indices = (lane % halfway).astype(jnp.float32)
+    inverse_freq = jnp.exp(indices * (-2.0 * math.log(ROPE_BASE) / width))
+    angles = position.astype(jnp.float32) * inverse_freq
+    cosine = jnp.cos(angles)
+    sine = jnp.where(lane < halfway, -1.0, 1.0) * jnp.sin(angles)
+    cosine = jnp.concatenate([cosine] * (rows // 8), axis=0)
+    sine = jnp.concatenate([sine] * (rows // 8), axis=0)
+    limits = jnp.concatenate(
+        [jnp.full((1, cache_len), lengths[session], jnp.int32) for session in range(sessions)], axis=1
+    )
+
+    def rotate(vectors):
+        return (vectors * cosine + pltpu.roll(vectors, halfway, 1) * sine).astype(jnp.bfloat16)
+
+    own = received[:, TILE : 2 * TILE, :].astype(jnp.float32)
+    pairs = devices // 2
+    own = own.reshape(pairs, 2, TILE, width)
+    own = own[:, 0] + own[:, 1]
+    own = own[:, 0:8]
+    own_rows = kv_heads * 8
+    own_key = rotate(own[0:kv_heads].reshape(own_rows, width))
+    own_value = own[kv_heads:].reshape(own_rows, width).astype(jnp.bfloat16)
+
+    session = lax.broadcasted_iota(jnp.int32, (rows, sessions * cache_len), 0) % PIECE
+    column = lax.broadcasted_iota(jnp.int32, (rows, sessions * cache_len), 1)
+    valid = (column // cache_len == session) & (column % cache_len < limits)
+    own_session = lax.broadcasted_iota(jnp.int32, (rows, own_rows), 0) % PIECE
+    own_column = lax.broadcasted_iota(jnp.int32, (rows, own_rows), 1)
+    for group in range(kv_heads):
+        query = received[group * per_group : (group + 1) * per_group, 0:TILE, :]
+        query = rotate(query.reshape(rows, width).astype(jnp.float32))
+        group_keys = keys[:, group].reshape(sessions * cache_len, width)
+        group_values = values[:, group].reshape(sessions * cache_len, width)
+        contract = (((1,), (1,)), ((), ()))
+        scores = (
+            lax.dot_general(query, group_keys, contract, preferred_element_type=jnp.float32) * scale
+        )
+        scores = jnp.where(valid, scores, -jnp.inf)
+        own_scores = (
+            lax.dot_general(query, own_key, contract, preferred_element_type=jnp.float32) * scale
+        )
+        own_scores = jnp.where(own_column == group * 8 + own_session, own_scores, -jnp.inf)
+        highest = jnp.maximum(
+            jnp.max(scores, axis=-1, keepdims=True), jnp.max(own_scores, axis=-1, keepdims=True)
+        )
+        cached_exp = jnp.exp(scores - highest)
+        own_exp = jnp.exp(own_scores - highest)
+        total = jnp.sum(cached_exp, axis=-1, keepdims=True) + jnp.sum(
+            own_exp, axis=-1, keepdims=True
+        )
+        weights = (cached_exp / total).astype(jnp.bfloat16)
+        own_weights = (own_exp / total).astype(jnp.bfloat16)
+        attended = jnp.dot(weights, group_values, preferred_element_type=jnp.float32)
+        attended += jnp.dot(own_weights, own_value, preferred_element_type=jnp.float32)
+        out[group * rows : (group + 1) * rows, :] = attended.astype(jnp.bfloat16)
+
+
+def attend(received, keys, values, lengths):
+    devices, _, width = received.shape
+    whole = pl.BlockSpec(memory_space=pltpu.VMEM)
+    return pl.pallas_call(
+        attend_kernel,
+        in_specs=[whole] * 3 + [pl.BlockSpec(memory_space=pltpu.SMEM)],
+        out_shape=jax.ShapeDtypeStruct((devices * TILE, width), jnp.bfloat16),
+        compiler_params=pltpu.CompilerParams(vmem_limit_bytes=8 * MIB),
+        cost_estimate=pl.CostEstimate(
+            flops=150_000_000, bytes_accessed=3_000_000, transcendentals=300_000
+        ),
+    )(received, keys, values, lengths)
+
+
+def inside(array):
+    return pltpu.with_memory_space_constraint(array, pltpu.VMEM)
+
+
+def on_block(
+    tokens, norm_gain, w_query, w_keyval, w_out, cache_keys, cache_values, session_ids, lengths, devices
+):
+    rows = devices * PIECE
+    near, gain, near_query, near_keyval, near_keys, near_values = prefetch(
+        (tokens, norm_gain, w_query, w_keyval, cache_keys, cache_values)
+    )
+    pack_tokens = functools.partial(norm_pack, gain=gain)
+    gathered = gather_rows(tokens, near, pack_tokens, devices)
+    local = project(
+        query_kernel,
+        gathered,
+        (inside(near_query), inside(near_keyval)),
+        session_ids,
+        (devices, 2 * TILE, LANES),
+        (w_query.shape[1], w_keyval.shape[0]),
+    )
+    received = lax.all_to_all(local, "wide", split_axis=0, concat_axis=0, tiled=True)
+    attended = attend(received, inside(near_keys), inside(near_values), lengths)
+    near_out, near = prefetch((w_out,), (attended,))
+    gathered = gather_rows(attended, near, pack, devices)
+    return project(
+        out_kernel, gathered, (inside(near_out),), session_ids, (rows, w_out.shape[1]), (w_out.shape[1],)
+    )
+
+
+def fits_block(devices, tokens, w_query, w_keyval, cache_keys):
+    sessions, kv_heads, cache_len, width = cache_keys.shape
+    return (
+        devices == 32
+        and tokens.shape[0] == PIECE
+        and sessions == PIECE
+        and width == LANES
+        and cache_len == LANES
+        and kv_heads == KVH
+        and w_query.shape[1] == 4 * LANES
+        and w_keyval.shape[0] == LANES // 2
+    )
+
+
+def on_device(*args, devices):
+    tokens, _, w_query, w_keyval, _, cache_keys = args[:6]
+    if fits_block(devices, tokens, w_query, w_keyval, cache_keys):
+        return on_block(*args, devices)
+    return on_any(*args)
+
+
 def solution(mesh):
     return jax.shard_map(
-        on_device,
+        functools.partial(on_device, devices=mesh.shape["wide"]),
         mesh=mesh,
         in_specs=(
             P(("groups", "wide"), None),

time: 208 us -> 108 us (0.52)
  waiting for transfers between devices: 134 us -> 41.9 us
  Pallas kernels: 0 us -> 27 us
  matrix products: 23.2 us -> 0 us
  local copies, waits for them, and re-layouts: 22.8 us -> 0.01 us
  starting transfers between devices: 5.77 us -> 24.3 us
  blocking collectives: 0 us -> 14.7 us
  between operations: 13.6 us -> 0.14 us
  other arithmetic: 7.75 us -> 0 us
    all_gather x2 -> x0, waiting for transfers between devices: 121 us -> none  [the longest x1 61.4 us: on_device(): everyone = lax.all_gather(normed, 'wide', axis=0, tiled=True)]
    ppermute x0 -> x32, waiting for transfers between devices: none -> 41.9 us  [swapped(): return lax.ppermute(array, 'wide', [(i, i ^ mask) for i in range(devices)])]
    pallas_call x0 -> x7, Pallas kernels: none -> 27 us  [the longest x2 12.8 us: prefetch(): pl.pallas_call(prefetch_kernel, in_specs=[pl.BlockSpec(memory_space=pltpu...]
    ppermute x0 -> x32, starting transfers between devices: none -> 24.3 us  [swapped(): return lax.ppermute(array, 'wide', [(i, i ^ mask) for i in range(devices)])]
    dot_general x6 -> x0, matrix products: 23.2 us -> none  [the longest x1 9.51 us: on_device(): jnp.dot(everyone, w_query, preferred_element_type=jnp.float32)]
    unnamed x15 -> x4, local copies, waits for them, and re-layouts: 15.4 us -> 0.01 us
    all_to_all x0 -> x1, blocking collectives: none -> 14.7 us  [on_block(): lax.all_to_all(local, 'wide', split_axis=0, concat_axis=0, tiled=True)]
    all_to_all x2 -> x0, waiting for transfers between devices: 13.3 us -> none  [the longest x1 7.8 us: on_device(): lax.all_to_all(query_local, 'wide', split_axis=0, concat_axis=1, tiled=True)]
  transfers between devices with their start and end apart: 4 -> 32, of which waited for: 4 -> 14; matrix products, arithmetic and copies ran while one was open for 3% -> 0% of each run, Pallas kernels for 0% -> 12%
where the time goes in v2:
time: 108 us
  waiting for transfers between devices  41.9 us (39%)
  Pallas kernels  27 us (25%)
  starting transfers between devices  24.3 us (22%)
  blocking collectives  14.7 us (14%)
    ppermute x32, waiting for transfers between devices, swapped(): return lax.ppermute(array, 'wide', [(i, i ^ mask) for i in range(devices)])  41.9 us
    ppermute x32, starting transfers between devices, swapped(): return lax.ppermute(array, 'wide', [(i, i ^ mask) for i in range(devices)])  24.3 us
    all_to_all x1, blocking collectives, on_block(): lax.all_to_all(local, 'wide', split_axis=0, concat_axis=0, tiled=True)  14.7 us
    pallas_call x2, Pallas kernels, prefetch(): pl.pallas_call(prefetch_kernel, in_specs=[pl.BlockSpec(memory_space=pltpu...  12.8 us
    pallas_call x2, Pallas kernels, project(): pl.pallas_call(kernel, in_specs=[whole] * len(operands), out_specs=whole,...  9.73 us
    pallas_call x1, Pallas kernels, attend(): pl.pallas_call(attend_kernel, in_specs=[whole] * 3 + [pl.BlockSpec(memory...  3.67 us
  transfers between devices with their start and end apart: 32, of which 14 were waited for; matrix products, arithmetic and copies ran while one was open for 0% of the time, Pallas kernels for 12%

profile of v2, /device:TPU:0, one launch (start us, length us, event | category | flops | bytes accessed | tf_op | source)
XLA Modules:
  0.0 108.0 jit_solution(5517418956301305689)
XLA Ops:
  0.0 3.0 %collective-permute-start = (bf16[4,16384]{1,0:T(4,128)(2,1)}, bf16[4,16384]{1,0:T(4,128)(2,1)S(1)}, u32[]{:S(2)}, u32[]{:S(2)}) collective-permute-start(bf16[4,16384]{1,0:T(4,128)(2,1)} %refs_0_.2), channel_id=1, source_target_pairs={{0,8},{1,9},{2,10},{3,11},{4,12},{5,13},{6,14},{7,15},{8,0},{9,1},... | collective-permute-start | bytes 393224 | tf_op jit(solution)/shard_map/ppermute | solution.py:174
  3.0 2.6 %collective-permute-start.1 = (bf16[4,16384]{1,0:T(4,128)(2,1)}, bf16[4,16384]{1,0:T(4,128)(2,1)S(1)}, u32[]{:S(2)}, u32[]{:S(2)}) collective-permute-start(bf16[4,16384]{1,0:T(4,128)(2,1)} %refs_0_.2), channel_id=1, source_target_pairs={{0,16},{1,17},{2,18},{3,19},{4,20},{5,21},{6,22},{7,23},{8,24},{9,... | collective-permute-start | bytes 393224 | tf_op jit(solution)/shard_map/ppermute | solution.py:174
  5.6 7.1 %shard_map.91 = (bf16[4,16384]{1,0:T(4,128)(2,1)S(1)}, f32[16384]{0:T(1024)S(1)}, bf16[16384,512]{1,0:T(8,128)(2,1)S(1)}, bf16[64,16384]{1,0:T(8,128)(2,1)S(1)},...) custom-call(bf16[4,16384]{1,0:T(4,128)(2,1)} %refs_0_.2, f32[16384]{0:T(1024)} %refs_1_.1, ...), custom_call_target="tpu_custom_call" | custom-call | bytes 21168128 | tf_op jit(solution)/shard_map/pallas_call | solution.py:203
  12.7 3.5 %collective-permute-done.1.z2 = bf16[4,16384]{1,0:T(4,128)(2,1)S(1)} collective-permute-done((bf16[4,16384]{1,0:T(4,128)(2,1)}, bf16[4,16384]{1,0:T(4,128)(2,1)S(1)}, u32[]{:S(2)}, u32[]{:S(2)}) %collective-permute-start.1) | collective-permute-done | bytes 131104 | tf_op jit(solution)/shard_map/ppermute | solution.py:174
  16.8 1.6 %collective-permute-start.3 = (bf16[64,16,128]{2,1,0:T(8,128)(2,1)S(1)}, bf16[64,16,128]{2,1,0:T(8,128)(2,1)S(1)}, u32[]{:S(2)}, u32[]{:S(2)}) collective-permute-start(bf16[64,16,128]{2,1,0:T(8,128)(2,1)S(1)} %get-tuple-element.21.refs_0_), channel_id=1, source_target_pairs={{0,2},{1,3},{2,0},{3,1},{4,6},{5,7},{6,4},{7,5},{8,10},{9,11},{10,... | collective-permute-start | bytes 786440 | tf_op jit(solution)/shard_map/ppermute | solution.py:174
  18.4 1.5 %collective-permute-start.4 = (bf16[64,16,128]{2,1,0:T(8,128)(2,1)S(1)}, bf16[64,16,128]{2,1,0:T(8,128)(2,1)S(1)}, u32[]{:S(2)}, u32[]{:S(2)}) collective-permute-start(bf16[64,16,128]{2,1,0:T(8,128)(2,1)S(1)} %get-tuple-element.21.refs_0_), channel_id=1, source_target_pairs={{0,4},{1,5},{2,6},{3,7},{4,0},{5,1},{6,2},{7,3},{8,12},{9,13},{10,... | collective-permute-start | bytes 786440 | tf_op jit(solution)/shard_map/ppermute | solution.py:174
  20.9 2.6 %collective-permute-done.3.refs_1_ = bf16[64,16,128]{2,1,0:T(8,128)(2,1)S(1)} collective-permute-done((bf16[64,16,128]{2,1,0:T(8,128)(2,1)S(1)}, bf16[64,16,128]{2,1,0:T(8,128)(2,1)S(1)}, u32[]{:S(2)}, u32[]{:S(2)}) %collective-permute-start.3) | collective-permute-done | bytes 262176 | tf_op jit(solution)/shard_map/ppermute | solution.py:174
  23.5 1.5 %collective-permute-start.5 = (bf16[64,16,128]{2,1,0:T(8,128)(2,1)S(1)}, bf16[64,16,128]{2,1,0:T(8,128)(2,1)S(1)}, u32[]{:S(2)}, u32[]{:S(2)}) collective-permute-start(bf16[64,16,128]{2,1,0:T(8,128)(2,1)S(1)} %collective-permute-done.3.refs_1_), channel_id=1, source_target_pairs={{0,4},{1,5},{2,6},{3,7},{4,0},{5,1},{6,2},{7,3},{8,12},{9,13},{10,... | collective-permute-start | bytes 786440 | tf_op jit(solution)/shard_map/ppermute | solution.py:174
  25.0 2.5 %collective-permute-done.4.refs_2_ = bf16[64,16,128]{2,1,0:T(8,128)(2,1)S(1)} collective-permute-done((bf16[64,16,128]{2,1,0:T(8,128)(2,1)S(1)}, bf16[64,16,128]{2,1,0:T(8,128)(2,1)S(1)}, u32[]{:S(2)}, u32[]{:S(2)}) %collective-permute-start.4) | collective-permute-done | bytes 262176 | tf_op jit(solution)/shard_map/ppermute | solution.py:174
  27.5 5.6 %collective-permute-done.11.refs_10_ = bf16[64,16,128]{2,1,0:T(8,128)(2,1)S(1)} collective-permute-done((bf16[64,16,128]{2,1,0:T(8,128)(2,1)S(1)}, bf16[64,16,128]{2,1,0:T(8,128)(2,1)S(1)}, u32[]{:S(2)}, u32[]{:S(2)}) %collective-permute-start.11) | collective-permute-done | bytes 262176 | tf_op jit(solution)/shard_map/ppermute | solution.py:174
  33.6 4.7 %collective-permute-done.5.refs_3_ = bf16[64,16,128]{2,1,0:T(8,128)(2,1)S(1)} collective-permute-done((bf16[64,16,128]{2,1,0:T(8,128)(2,1)S(1)}, bf16[64,16,128]{2,1,0:T(8,128)(2,1)S(1)}, u32[]{:S(2)}, u32[]{:S(2)}) %collective-permute-start.5) | collective-permute-done | bytes 262176 | tf_op jit(solution)/shard_map/ppermute | solution.py:174
  38.9 1.7 %collective-permute-done.12.refs_11_ = bf16[64,16,128]{2,1,0:T(8,128)(2,1)S(1)} collective-permute-done((bf16[64,16,128]{2,1,0:T(8,128)(2,1)S(1)}, bf16[64,16,128]{2,1,0:T(8,128)(2,1)S(1)}, u32[]{:S(2)}, u32[]{:S(2)}) %collective-permute-start.12) | collective-permute-done | bytes 262176 | tf_op jit(solution)/shard_map/ppermute | solution.py:174
  40.7 1.5 %collective-permute-done.15.refs_15_ = bf16[64,16,128]{2,1,0:T(8,128)(2,1)S(1)} collective-permute-done((bf16[64,16,128]{2,1,0:T(8,128)(2,1)S(1)}, bf16[64,16,128]{2,1,0:T(8,128)(2,1)S(1)}, u32[]{:S(2)}, u32[]{:S(2)}) %collective-permute-start.15) | collective-permute-done | bytes 262176 | tf_op jit(solution)/shard_map/ppermute | solution.py:174
  42.2 5.3 %shard_map.93 = bf16[32,32,128]{2,1,0:T(8,128)(2,1)S(1)} custom-call(bf16[64,16,128]{2,1,0:T(8,128)(2,1)S(1)} %get-tuple-element.21.refs_0_, bf16[64,16,128]{2,1,0:T(8,128)(2,1)S(1)} %collective-permute-done.3.refs_1_, bf16[64,16,128]{2,1,0:T(8,128)(2,1)S(1)} %collective-permute-done.4.refs_2_, bf16[64,16,128]{2,1,0:T(8,128)(2,1)S(1)} %collective-permute-done.5.refs_3_, ...), custom_call_target="tpu_custom_call" | custom-call | flops 2415919104 | bytes 23068672 | tf_op jit(solution)/shard_map/pallas_call | solution.py:323
  47.4 14.7 %all_to_all.5.received = bf16[32,32,128]{2,1,0:T(8,128)(2,1)S(1)} all-to-all(bf16[32,32,128]{2,1,0:T(8,128)(2,1)S(1)} %shard_map.93), channel_id=1, replica_groups=mesh['groups'=1,'wide'=32] {'wide'}, dimensions={0} | all-to-all | bytes 524288 | tf_op jit(solution)/shard_map/all_to_all | solution.py:444
  62.1 3.7 %shard_map.94.refs_1_ = bf16[512,128]{1,0:T(8,128)(2,1)S(1)} custom-call(bf16[32,32,128]{2,1,0:T(8,128)(2,1)S(1)} %all_to_all.5.received, bf16[4,8,128,128]{3,2,1,0:T(8,128)(2,1)S(1)} %get-tuple-element.26.keys, bf16[4,8,128,128]{3,2,1,0:T(8,128)(2,1)S(1)} %get-tuple-element.27.values, s32[4]{0:T(128)S(1)} %copy-done.1), custom_call_target="tpu_custom_call" | custom-call | flops 150000000 | bytes 3000000 | tf_op jit(solution)/shard_map/pallas_call | solution.py:412
  65.8 1.0 collective-permute-start.16
  66.8 1.0 collective-permute-start.17
  67.8 2.5 %collective-permute-start.18 = (bf16[512,128]{1,0:T(8,128)(2,1)S(1)}, bf16[512,128]{1,0:T(8,128)(2,1)S(1)}, u32[]{:S(2)}, u32[]{:S(2)}) collective-permute-start(bf16[512,128]{1,0:T(8,128)(2,1)S(1)} %shard_map.94.refs_1_), channel_id=1, source_target_pairs={{0,24},{1,25},{2,26},{3,27},{4,28},{5,29},{6,30},{7,31},{8,16},{9,... | collective-permute-start | bytes 393224 | tf_op jit(solution)/shard_map/ppermute | solution.py:174
  70.3 5.8 %shard_map.95 = (bf16[16384,512]{1,0:T(8,128)(2,1)S(1)}, bf16[512,128]{1,0:T(8,128)(2,1)S(1)}) custom-call(bf16[16384,512]{1,0:T(8,128)(2,1)} %refs_0_.3, bf16[512,128]{1,0:T(8,128)(2,1)S(1)} %shard_map.94.refs_1_), custom_call_target="tpu_custom_call" | custom-call | bytes 16908288 | tf_op jit(solution)/shard_map/pallas_call | solution.py:203
  76.1 3.2 %collective-permute-done.17.z2 = bf16[512,128]{1,0:T(8,128)(2,1)S(1)} collective-permute-done((bf16[512,128]{1,0:T(8,128)(2,1)S(1)}, bf16[512,128]{1,0:T(8,128)(2,1)S(1)}, u32[]{:S(2)}, u32[]{:S(2)}) %collective-permute-start.17) | collective-permute-done | bytes 131104 | tf_op jit(solution)/shard_map/ppermute | solution.py:174
  79.5 1.4 %collective-permute-start.20 = (bf16[64,16,128]{2,1,0:T(8,128)(2,1)S(1)}, bf16[64,16,128]{2,1,0:T(8,128)(2,1)S(1)}, u32[]{:S(2)}, u32[]{:S(2)}) collective-permute-start(bf16[64,16,128]{2,1,0:T(8,128)(2,1)S(1)} %get-tuple-element.29.refs_0_), channel_id=1, source_target_pairs={{0,4},{1,5},{2,6},{3,7},{4,0},{5,1},{6,2},{7,3},{8,12},{9,13},{10,... | collective-permute-start | bytes 786440 | tf_op jit(solution)/shard_map/ppermute | solution.py:174
  80.9 0.7 collective-permute-start.27
  81.6 1.9 %collective-permute-start.26 = (bf16[64,16,128]{2,1,0:T(8,128)(2,1)S(1)}, bf16[64,16,128]{2,1,0:T(8,128)(2,1)S(1)}, u32[]{:S(2)}, u32[]{:S(2)}) collective-permute-start(bf16[64,16,128]{2,1,0:T(8,128)(2,1)S(1)} %get-tuple-element.31.refs_8_), channel_id=1, source_target_pairs={{0,2},{1,3},{2,0},{3,1},{4,6},{5,7},{6,4},{7,5},{8,10},{9,11},{10,... | collective-permute-start | bytes 786440 | tf_op jit(solution)/shard_map/ppermute | solution.py:174
  83.5 3.8 %collective-permute-done.19.refs_1_ = bf16[64,16,128]{2,1,0:T(8,128)(2,1)S(1)} collective-permute-done((bf16[64,16,128]{2,1,0:T(8,128)(2,1)S(1)}, bf16[64,16,128]{2,1,0:T(8,128)(2,1)S(1)}, u32[]{:S(2)}, u32[]{:S(2)}) %collective-permute-start.19) | collective-permute-done | bytes 262176 | tf_op jit(solution)/shard_map/ppermute | solution.py:174
  87.3 0.9 collective-permute-start.21
  88.7 5.6 %collective-permute-done.27.refs_10_ = bf16[64,16,128]{2,1,0:T(8,128)(2,1)S(1)} collective-permute-done((bf16[64,16,128]{2,1,0:T(8,128)(2,1)S(1)}, bf16[64,16,128]{2,1,0:T(8,128)(2,1)S(1)}, u32[]{:S(2)}, u32[]{:S(2)}) %collective-permute-start.27) | collective-permute-done | bytes 262176 | tf_op jit(solution)/shard_map/ppermute | solution.py:174
  94.3 1.9 %collective-permute-start.28 = (bf16[64,16,128]{2,1,0:T(8,128)(2,1)S(1)}, bf16[64,16,128]{2,1,0:T(8,128)(2,1)S(1)}, u32[]{:S(2)}, u32[]{:S(2)}) collective-permute-start(bf16[64,16,128]{2,1,0:T(8,128)(2,1)S(1)} %collective-permute-done.27.refs_10_), channel_id=1, source_target_pairs={{0,2},{1,3},{2,0},{3,1},{4,6},{5,7},{6,4},{7,5},{8,10},{9,11},{10,... | collective-permute-start | bytes 786440 | tf_op jit(solution)/shard_map/ppermute | solution.py:174
  96.2 3.3 %collective-permute-done.21.refs_3_ = bf16[64,16,128]{2,1,0:T(8,128)(2,1)S(1)} collective-permute-done((bf16[64,16,128]{2,1,0:T(8,128)(2,1)S(1)}, bf16[64,16,128]{2,1,0:T(8,128)(2,1)S(1)}, u32[]{:S(2)}, u32[]{:S(2)}) %collective-permute-start.21) | collective-permute-done | bytes 262176 | tf_op jit(solution)/shard_map/ppermute | solution.py:174
  100.1 1.9 %collective-permute-done.28.refs_11_ = bf16[64,16,128]{2,1,0:T(8,128)(2,1)S(1)} collective-permute-done((bf16[64,16,128]{2,1,0:T(8,128)(2,1)S(1)}, bf16[64,16,128]{2,1,0:T(8,128)(2,1)S(1)}, u32[]{:S(2)}, u32[]{:S(2)}) %collective-permute-start.28) | collective-permute-done | bytes 262176 | tf_op jit(solution)/shard_map/ppermute | solution.py:174
  102.0 1.5 %collective-permute-done.31.refs_15_ = bf16[64,16,128]{2,1,0:T(8,128)(2,1)S(1)} collective-permute-done((bf16[64,16,128]{2,1,0:T(8,128)(2,1)S(1)}, bf16[64,16,128]{2,1,0:T(8,128)(2,1)S(1)}, u32[]{:S(2)}, u32[]{:S(2)}) %collective-permute-start.31) | collective-permute-done | bytes 262176 | tf_op jit(solution)/shard_map/ppermute | solution.py:174
  103.5 4.5 %shard_map.97 = bf16[128,512]{1,0:T(8,128)(2,1)} custom-call(bf16[64,16,128]{2,1,0:T(8,128)(2,1)S(1)} %get-tuple-element.29.refs_0_, bf16[64,16,128]{2,1,0:T(8,128)(2,1)S(1)} %collective-permute-done.19.refs_1_, bf16[64,16,128]{2,1,0:T(8,128)(2,1)S(1)} %collective-permute-done.20.refs_2_, bf16[64,16,128]{2,1,0:T(8,128)(2,1)S(1)} %collective-permute-done.21.refs_3_, ...), custom_call_target="tpu_custom_call" | custom-call | flops 2147483648 | bytes 20971520 | tf_op jit(solution)/shard_map/pallas_call | solution.py:323
  (44 shorter events, 4.2 us)
Async XLA Ops:
  0.0 12.7 %collective-permute-start = (bf16[4,16384]{1,0:T(4,128)(2,1)}, bf16[4,16384]{1,0:T(4,128)(2,1)S(1)}, u32[]{:S(2)}, u32[]{:S(2)}) collective-permute-start(bf16[4,16384]{1,0:T(4,128)(2,1)} %refs_0_.2), channel_id=1, source_target_pairs={{0,8},{1,9},{2,10},{3,11},{4,12},{5,13},{6,14},{7,15},{8,0},{9,1},... | collective-permute-start | bytes 393224 | tf_op jit(solution)/shard_map/ppermute | solution.py:174
  3.0 13.2 %collective-permute-start.1 = (bf16[4,16384]{1,0:T(4,128)(2,1)}, bf16[4,16384]{1,0:T(4,128)(2,1)S(1)}, u32[]{:S(2)}, u32[]{:S(2)}) collective-permute-start(bf16[4,16384]{1,0:T(4,128)(2,1)} %refs_0_.2), channel_id=1, source_target_pairs={{0,16},{1,17},{2,18},{3,19},{4,20},{5,21},{6,22},{7,23},{8,24},{9,... | collective-permute-start | bytes 393224 | tf_op jit(solution)/shard_map/ppermute | solution.py:174
  5.6 10.6 %collective-permute-start.2 = (bf16[4,16384]{1,0:T(4,128)(2,1)}, bf16[4,16384]{1,0:T(4,128)(2,1)S(1)}, u32[]{:S(2)}, u32[]{:S(2)}) collective-permute-start(bf16[4,16384]{1,0:T(4,128)(2,1)} %refs_0_.2), channel_id=1, source_target_pairs={{0,24},{1,25},{2,26},{3,27},{4,28},{5,29},{6,30},{7,31},{8,16},{9,... | collective-permute-start | bytes 393224 | tf_op jit(solution)/shard_map/ppermute | solution.py:174
  16.8 6.7 %collective-permute-start.3 = (bf16[64,16,128]{2,1,0:T(8,128)(2,1)S(1)}, bf16[64,16,128]{2,1,0:T(8,128)(2,1)S(1)}, u32[]{:S(2)}, u32[]{:S(2)}) collective-permute-start(bf16[64,16,128]{2,1,0:T(8,128)(2,1)S(1)} %get-tuple-element.21.refs_0_), channel_id=1, source_target_pairs={{0,2},{1,3},{2,0},{3,1},{4,6},{5,7},{6,4},{7,5},{8,10},{9,11},{10,... | collective-permute-start | bytes 786440 | tf_op jit(solution)/shard_map/ppermute | solution.py:174
  18.4 20.0 %collective-permute-start.6 = (bf16[128,16,128]{2,1,0:T(8,128)(2,1)S(1)}, bf16[128,16,128]{2,1,0:T(8,128)(2,1)S(1)}, u32[]{:S(2)}, u32[]{:S(2)}) collective-permute-start(bf16[128,16,128]{2,1,0:T(8,128)(2,1)S(1)} %get-tuple-element.22), channel_id=1, source_target_pairs={{0,1},{1,0},{2,3},{3,2},{4,5},{5,4},{6,7},{7,6},{8,9},{9,8},{10,11... | collective-permute-start | bytes 1572872 | tf_op jit(solution)/shard_map/ppermute | solution.py:174
  18.4 9.1 %collective-permute-start.4 = (bf16[64,16,128]{2,1,0:T(8,128)(2,1)S(1)}, bf16[64,16,128]{2,1,0:T(8,128)(2,1)S(1)}, u32[]{:S(2)}, u32[]{:S(2)}) collective-permute-start(bf16[64,16,128]{2,1,0:T(8,128)(2,1)S(1)} %get-tuple-element.21.refs_0_), channel_id=1, source_target_pairs={{0,4},{1,5},{2,6},{3,7},{4,0},{5,1},{6,2},{7,3},{8,12},{9,13},{10,... | collective-permute-start | bytes 786440 | tf_op jit(solution)/shard_map/ppermute | solution.py:174
  19.9 13.2 %collective-permute-start.11 = (bf16[64,16,128]{2,1,0:T(8,128)(2,1)S(1)}, bf16[64,16,128]{2,1,0:T(8,128)(2,1)S(1)}, u32[]{:S(2)}, u32[]{:S(2)}) collective-permute-start(bf16[64,16,128]{2,1,0:T(8,128)(2,1)S(1)} %get-tuple-element.23.refs_8_), channel_id=1, source_target_pairs={{0,4},{1,5},{2,6},{3,7},{4,0},{5,1},{6,2},{7,3},{8,12},{9,13},{10,... | collective-permute-start | bytes 786440 | tf_op jit(solution)/shard_map/ppermute | solution.py:174
  20.4 13.2 %collective-permute-start.10 = (bf16[64,16,128]{2,1,0:T(8,128)(2,1)S(1)}, bf16[64,16,128]{2,1,0:T(8,128)(2,1)S(1)}, u32[]{:S(2)}, u32[]{:S(2)}) collective-permute-start(bf16[64,16,128]{2,1,0:T(8,128)(2,1)S(1)} %get-tuple-element.23.refs_8_), channel_id=1, source_target_pairs={{0,2},{1,3},{2,0},{3,1},{4,6},{5,7},{6,4},{7,5},{8,10},{9,11},{10,... | collective-permute-start | bytes 786440 | tf_op jit(solution)/shard_map/ppermute | solution.py:174
  23.5 14.8 %collective-permute-start.5 = (bf16[64,16,128]{2,1,0:T(8,128)(2,1)S(1)}, bf16[64,16,128]{2,1,0:T(8,128)(2,1)S(1)}, u32[]{:S(2)}, u32[]{:S(2)}) collective-permute-start(bf16[64,16,128]{2,1,0:T(8,128)(2,1)S(1)} %collective-permute-done.3.refs_1_), channel_id=1, source_target_pairs={{0,4},{1,5},{2,6},{3,7},{4,0},{5,1},{6,2},{7,3},{8,12},{9,13},{10,... | collective-permute-start | bytes 786440 | tf_op jit(solution)/shard_map/ppermute | solution.py:174
  27.5 11.4 %collective-permute-start.7 = (bf16[64,16,128]{2,1,0:T(8,128)(2,1)S(1)}, bf16[64,16,128]{2,1,0:T(8,128)(2,1)S(1)}, u32[]{:S(2)}, u32[]{:S(2)}) collective-permute-start(bf16[64,16,128]{2,1,0:T(8,128)(2,1)S(1)} %collective-permute-done.3.refs_1_), channel_id=1, source_target_pairs={{0,1},{1,0},{2,3},{3,2},{4,5},{5,4},{6,7},{7,6},{8,9},{9,8},{10,11... | collective-permute-start | bytes 786440 | tf_op jit(solution)/shard_map/ppermute | solution.py:174
  33.1 7.6 %collective-permute-start.12 = (bf16[64,16,128]{2,1,0:T(8,128)(2,1)S(1)}, bf16[64,16,128]{2,1,0:T(8,128)(2,1)S(1)}, u32[]{:S(2)}, u32[]{:S(2)}) collective-permute-start(bf16[64,16,128]{2,1,0:T(8,128)(2,1)S(1)} %collective-permute-done.11.refs_10_), channel_id=1, source_target_pairs={{0,2},{1,3},{2,0},{3,1},{4,6},{5,7},{6,4},{7,5},{8,10},{9,11},{10,... | collective-permute-start | bytes 786440 | tf_op jit(solution)/shard_map/ppermute | solution.py:174
  33.6 7.0 %collective-permute-start.14 = (bf16[64,16,128]{2,1,0:T(8,128)(2,1)S(1)}, bf16[64,16,128]{2,1,0:T(8,128)(2,1)S(1)}, u32[]{:S(2)}, u32[]{:S(2)}) collective-permute-start(bf16[64,16,128]{2,1,0:T(8,128)(2,1)S(1)} %collective-permute-done.11.refs_10_), channel_id=1, source_target_pairs={{0,1},{1,0},{2,3},{3,2},{4,5},{5,4},{6,7},{7,6},{8,9},{9,8},{10,11... | collective-permute-start | bytes 786440 | tf_op jit(solution)/shard_map/ppermute | solution.py:174
  38.3 2.3 %collective-permute-start.8 = (bf16[64,16,128]{2,1,0:T(8,128)(2,1)S(1)}, bf16[64,16,128]{2,1,0:T(8,128)(2,1)S(1)}, u32[]{:S(2)}, u32[]{:S(2)}) collective-permute-start(bf16[64,16,128]{2,1,0:T(8,128)(2,1)S(1)} %collective-permute-done.4.refs_2_), channel_id=1, source_target_pairs={{0,1},{1,0},{2,3},{3,2},{4,5},{5,4},{6,7},{7,6},{8,9},{9,8},{10,11... | collective-permute-start | bytes 786440 | tf_op jit(solution)/shard_map/ppermute | solution.py:174
  38.3 2.3 %collective-permute-start.13 = (bf16[64,16,128]{2,1,0:T(8,128)(2,1)S(1)}, bf16[64,16,128]{2,1,0:T(8,128)(2,1)S(1)}, u32[]{:S(2)}, u32[]{:S(2)}) collective-permute-start(bf16[64,16,128]{2,1,0:T(8,128)(2,1)S(1)} %collective-permute-done.10.refs_9_), channel_id=1, source_target_pairs={{0,1},{1,0},{2,3},{3,2},{4,5},{5,4},{6,7},{7,6},{8,9},{9,8},{10,11... | collective-permute-start | bytes 786440 | tf_op jit(solution)/shard_map/ppermute | solution.py:174
  38.8 1.8 %collective-permute-start.9 = (bf16[64,16,128]{2,1,0:T(8,128)(2,1)S(1)}, bf16[64,16,128]{2,1,0:T(8,128)(2,1)S(1)}, u32[]{:S(2)}, u32[]{:S(2)}) collective-permute-start(bf16[64,16,128]{2,1,0:T(8,128)(2,1)S(1)} %collective-permute-done.5.refs_3_), channel_id=1, source_target_pairs={{0,1},{1,0},{2,3},{3,2},{4,5},{5,4},{6,7},{7,6},{8,9},{9,8},{10,11... | collective-permute-start | bytes 786440 | tf_op jit(solution)/shard_map/ppermute | solution.py:174
  40.6 1.5 %collective-permute-start.15 = (bf16[64,16,128]{2,1,0:T(8,128)(2,1)S(1)}, bf16[64,16,128]{2,1,0:T(8,128)(2,1)S(1)}, u32[]{:S(2)}, u32[]{:S(2)}) collective-permute-start(bf16[64,16,128]{2,1,0:T(8,128)(2,1)S(1)} %collective-permute-done.12.refs_11_), channel_id=1, source_target_pairs={{0,1},{1,0},{2,3},{3,2},{4,5},{5,4},{6,7},{7,6},{8,9},{9,8},{10,11... | collective-permute-start | bytes 786440 | tf_op jit(solution)/shard_map/ppermute | solution.py:174
  65.8 10.3 %collective-permute-start.16 = (bf16[512,128]{1,0:T(8,128)(2,1)S(1)}, bf16[512,128]{1,0:T(8,128)(2,1)S(1)}, u32[]{:S(2)}, u32[]{:S(2)}) collective-permute-start(bf16[512,128]{1,0:T(8,128)(2,1)S(1)} %shard_map.94.refs_1_), channel_id=1, source_target_pairs={{0,8},{1,9},{2,10},{3,11},{4,12},{5,13},{6,14},{7,15},{8,0},{9,1},... | collective-permute-start | bytes 393224 | tf_op jit(solution)/shard_map/ppermute | solution.py:174
  66.8 12.4 %collective-permute-start.17 = (bf16[512,128]{1,0:T(8,128)(2,1)S(1)}, bf16[512,128]{1,0:T(8,128)(2,1)S(1)}, u32[]{:S(2)}, u32[]{:S(2)}) collective-permute-start(bf16[512,128]{1,0:T(8,128)(2,1)S(1)} %shard_map.94.refs_1_), channel_id=1, source_target_pairs={{0,16},{1,17},{2,18},{3,19},{4,20},{5,21},{6,22},{7,23},{8,24},{9,... | collective-permute-start | bytes 393224 | tf_op jit(solution)/shard_map/ppermute | solution.py:174
  67.8 11.5 %collective-permute-start.18 = (bf16[512,128]{1,0:T(8,128)(2,1)S(1)}, bf16[512,128]{1,0:T(8,128)(2,1)S(1)}, u32[]{:S(2)}, u32[]{:S(2)}) collective-permute-start(bf16[512,128]{1,0:T(8,128)(2,1)S(1)} %shard_map.94.refs_1_), channel_id=1, source_target_pairs={{0,24},{1,25},{2,26},{3,27},{4,28},{5,29},{6,30},{7,31},{8,16},{9,... | collective-permute-start | bytes 393224 | tf_op jit(solution)/shard_map/ppermute | solution.py:174
  79.4 7.9 %collective-permute-start.19 = (bf16[64,16,128]{2,1,0:T(8,128)(2,1)S(1)}, bf16[64,16,128]{2,1,0:T(8,128)(2,1)S(1)}, u32[]{:S(2)}, u32[]{:S(2)}) collective-permute-start(bf16[64,16,128]{2,1,0:T(8,128)(2,1)S(1)} %get-tuple-element.29.refs_0_), channel_id=1, source_target_pairs={{0,2},{1,3},{2,0},{3,1},{4,6},{5,7},{6,4},{7,5},{8,10},{9,11},{10,... | collective-permute-start | bytes 786440 | tf_op jit(solution)/shard_map/ppermute | solution.py:174
  79.5 20.0 %collective-permute-start.22 = (bf16[128,16,128]{2,1,0:T(8,128)(2,1)S(1)}, bf16[128,16,128]{2,1,0:T(8,128)(2,1)S(1)}, u32[]{:S(2)}, u32[]{:S(2)}) collective-permute-start(bf16[128,16,128]{2,1,0:T(8,128)(2,1)S(1)} %get-tuple-element.30), channel_id=1, source_target_pairs={{0,1},{1,0},{2,3},{3,2},{4,5},{5,4},{6,7},{7,6},{8,9},{9,8},{10,11... | collective-permute-start | bytes 1572872 | tf_op jit(solution)/shard_map/ppermute | solution.py:174
  79.5 9.2 %collective-permute-start.20 = (bf16[64,16,128]{2,1,0:T(8,128)(2,1)S(1)}, bf16[64,16,128]{2,1,0:T(8,128)(2,1)S(1)}, u32[]{:S(2)}, u32[]{:S(2)}) collective-permute-start(bf16[64,16,128]{2,1,0:T(8,128)(2,1)S(1)} %get-tuple-element.29.refs_0_), channel_id=1, source_target_pairs={{0,4},{1,5},{2,6},{3,7},{4,0},{5,1},{6,2},{7,3},{8,12},{9,13},{10,... | collective-permute-start | bytes 786440 | tf_op jit(solution)/shard_map/ppermute | solution.py:174
  80.9 13.4 %collective-permute-start.27 = (bf16[64,16,128]{2,1,0:T(8,128)(2,1)S(1)}, bf16[64,16,128]{2,1,0:T(8,128)(2,1)S(1)}, u32[]{:S(2)}, u32[]{:S(2)}) collective-permute-start(bf16[64,16,128]{2,1,0:T(8,128)(2,1)S(1)} %get-tuple-element.31.refs_8_), channel_id=1, source_target_pairs={{0,4},{1,5},{2,6},{3,7},{4,0},{5,1},{6,2},{7,3},{8,12},{9,13},{10,... | collective-permute-start | bytes 786440 | tf_op jit(solution)/shard_map/ppermute | solution.py:174
  81.6 14.6 %collective-permute-start.26 = (bf16[64,16,128]{2,1,0:T(8,128)(2,1)S(1)}, bf16[64,16,128]{2,1,0:T(8,128)(2,1)S(1)}, u32[]{:S(2)}, u32[]{:S(2)}) collective-permute-start(bf16[64,16,128]{2,1,0:T(8,128)(2,1)S(1)} %get-tuple-element.31.refs_8_), channel_id=1, source_target_pairs={{0,2},{1,3},{2,0},{3,1},{4,6},{5,7},{6,4},{7,5},{8,10},{9,11},{10,... | collective-permute-start | bytes 786440 | tf_op jit(solution)/shard_map/ppermute | solution.py:174
  87.3 12.2 %collective-permute-start.21 = (bf16[64,16,128]{2,1,0:T(8,128)(2,1)S(1)}, bf16[64,16,128]{2,1,0:T(8,128)(2,1)S(1)}, u32[]{:S(2)}, u32[]{:S(2)}) collective-permute-start(bf16[64,16,128]{2,1,0:T(8,128)(2,1)S(1)} %collective-permute-done.19.refs_1_), channel_id=1, source_target_pairs={{0,4},{1,5},{2,6},{3,7},{4,0},{5,1},{6,2},{7,3},{8,12},{9,13},{10,... | collective-permute-start | bytes 786440 | tf_op jit(solution)/shard_map/ppermute | solution.py:174
  88.7 11.3 %collective-permute-start.23 = (bf16[64,16,128]{2,1,0:T(8,128)(2,1)S(1)}, bf16[64,16,128]{2,1,0:T(8,128)(2,1)S(1)}, u32[]{:S(2)}, u32[]{:S(2)}) collective-permute-start(bf16[64,16,128]{2,1,0:T(8,128)(2,1)S(1)} %collective-permute-done.19.refs_1_), channel_id=1, source_target_pairs={{0,1},{1,0},{2,3},{3,2},{4,5},{5,4},{6,7},{7,6},{8,9},{9,8},{10,11... | collective-permute-start | bytes 786440 | tf_op jit(solution)/shard_map/ppermute | solution.py:174
  94.3 7.7 %collective-permute-start.28 = (bf16[64,16,128]{2,1,0:T(8,128)(2,1)S(1)}, bf16[64,16,128]{2,1,0:T(8,128)(2,1)S(1)}, u32[]{:S(2)}, u32[]{:S(2)}) collective-permute-start(bf16[64,16,128]{2,1,0:T(8,128)(2,1)S(1)} %collective-permute-done.27.refs_10_), channel_id=1, source_target_pairs={{0,2},{1,3},{2,0},{3,1},{4,6},{5,7},{6,4},{7,5},{8,10},{9,11},{10,... | collective-permute-start | bytes 786440 | tf_op jit(solution)/shard_map/ppermute | solution.py:174
  96.2 5.8 %collective-permute-start.30 = (bf16[64,16,128]{2,1,0:T(8,128)(2,1)S(1)}, bf16[64,16,128]{2,1,0:T(8,128)(2,1)S(1)}, u32[]{:S(2)}, u32[]{:S(2)}) collective-permute-start(bf16[64,16,128]{2,1,0:T(8,128)(2,1)S(1)} %collective-permute-done.27.refs_10_), channel_id=1, source_target_pairs={{0,1},{1,0},{2,3},{3,2},{4,5},{5,4},{6,7},{7,6},{8,9},{9,8},{10,11... | collective-permute-start | bytes 786440 | tf_op jit(solution)/shard_map/ppermute | solution.py:174
  99.5 2.5 %collective-permute-start.24 = (bf16[64,16,128]{2,1,0:T(8,128)(2,1)S(1)}, bf16[64,16,128]{2,1,0:T(8,128)(2,1)S(1)}, u32[]{:S(2)}, u32[]{:S(2)}) collective-permute-start(bf16[64,16,128]{2,1,0:T(8,128)(2,1)S(1)} %collective-permute-done.20.refs_2_), channel_id=1, source_target_pairs={{0,1},{1,0},{2,3},{3,2},{4,5},{5,4},{6,7},{7,6},{8,9},{9,8},{10,11... | collective-permute-start | bytes 786440 | tf_op jit(solution)/shard_map/ppermute | solution.py:174
  99.5 2.5 %collective-permute-start.29 = (bf16[64,16,128]{2,1,0:T(8,128)(2,1)S(1)}, bf16[64,16,128]{2,1,0:T(8,128)(2,1)S(1)}, u32[]{:S(2)}, u32[]{:S(2)}) collective-permute-start(bf16[64,16,128]{2,1,0:T(8,128)(2,1)S(1)} %collective-permute-done.26.refs_9_), channel_id=1, source_target_pairs={{0,1},{1,0},{2,3},{3,2},{4,5},{5,4},{6,7},{7,6},{8,9},{9,8},{10,11... | collective-permute-start | bytes 786440 | tf_op jit(solution)/shard_map/ppermute | solution.py:174
  100.0 2.0 %collective-permute-start.25 = (bf16[64,16,128]{2,1,0:T(8,128)(2,1)S(1)}, bf16[64,16,128]{2,1,0:T(8,128)(2,1)S(1)}, u32[]{:S(2)}, u32[]{:S(2)}) collective-permute-start(bf16[64,16,128]{2,1,0:T(8,128)(2,1)S(1)} %collective-permute-done.21.refs_3_), channel_id=1, source_target_pairs={{0,1},{1,0},{2,3},{3,2},{4,5},{5,4},{6,7},{7,6},{8,9},{9,8},{10,11... | collective-permute-start | bytes 786440 | tf_op jit(solution)/shard_map/ppermute | solution.py:174
  102.0 1.5 %collective-permute-start.31 = (bf16[64,16,128]{2,1,0:T(8,128)(2,1)S(1)}, bf16[64,16,128]{2,1,0:T(8,128)(2,1)S(1)}, u32[]{:S(2)}, u32[]{:S(2)}) collective-permute-start(bf16[64,16,128]{2,1,0:T(8,128)(2,1)S(1)} %collective-permute-done.28.refs_11_), channel_id=1, source_target_pairs={{0,1},{1,0},{2,3},{3,2},{4,5},{5,4},{6,7},{7,6},{8,9},{9,8},{10,11... | collective-permute-start | bytes 786440 | tf_op jit(solution)/shard_map/ppermute | solution.py:174
  (2 other events, 91.6 us)

commit v3 on v2

--- a/solution.py
+++ b/solution.py
@@ -103,94 +103,143 @@
     return out_sess[session_ids].astype(jnp.bfloat16)
 
 
-def norm_pack_kernel(own, z1, z2, z3, gain, low, high, full):
-    width = own.shape[1]
+def norm_kernel(tokens, gain, main, rest):
+    width = tokens.shape[1]
+    values = tokens[...].astype(jnp.float32)
+    meansq = jnp.sum(values * values, axis=-1, keepdims=True) * (1.0 / width)
+    scale = lax.rsqrt(meansq + 1e-05)
     blocks = width // LANES
-    pieces = (own, z1, z2, z3)
-    scales = []
-    for piece in pieces:
-        values = piece[...].astype(jnp.float32)
-        meansq = jnp.sum(values * values, axis=-1, keepdims=True) * (1.0 / width)
-        scales.append(lax.rsqrt(meansq + 1e-05))
-    for block in range(blocks):
-        lanes = slice(block * LANES, (block + 1) * LANES)
-        factor = gain[:, lanes]
-        rows = jnp.concatenate(
-            [piece[:, lanes].astype(jnp.float32) * scale * factor for piece, scale in zip(pieces, scales)],
-            axis=0,
-        ).astype(jnp.bfloat16)
-        full[block] = rows
-        if block < blocks // 2:
-            low[block] = rows
+    split = main.shape[0] // PIECE
+    for first in range(0, blocks, 4):
+        tile = []
+        for block in range(first, first + 4):
+            lanes = slice(block * LANES, (block + 1) * LANES)
+            tile.append(tokens[:, lanes].astype(jnp.float32) * scale * gain[:, lanes])
+        tile = jnp.concatenate(tile, axis=0).astype(jnp.bfloat16)
+        if first < split:
+            main[first * PIECE : (first + 4) * PIECE, :] = tile
         else:
-            high[block - blocks // 2] = rows
-
-
-def pack_kernel(own, z1, z2, z3, low, high, full):
-    blocks = own.shape[0] // PIECE
-    pieces = (own, z1, z2, z3)
+            rest[(first - split) * PIECE : (first - split + 4) * PIECE, :] = tile
+
+
+def split_shapes(blocks):
+    rest = blocks * 3 // 16
+    return tuple(
+        jax.ShapeDtypeStruct((count * PIECE, LANES), jnp.bfloat16) for count in (blocks - rest, rest)
+    )
+
+
+def norm(tokens, gain):
+    return pl.pallas_call(
+        norm_kernel,
+        out_shape=split_shapes(tokens.shape[1] // LANES),
+        compiler_params=pltpu.CompilerParams(vmem_limit_bytes=8 * MIB),
+        cost_estimate=pl.CostEstimate(flops=500_000, bytes_accessed=400_000, transcendentals=0),
+    )(
+        pltpu.with_memory_space_constraint(tokens, pltpu.HBM),
+        pltpu.with_memory_space_constraint(gain[None, :], pltpu.HBM),
+    )
+
+
+def pack_planes_kernel(*refs):
+    pieces, out = refs[0], refs[-1]
+    here = lax.axis_index("wide") // 2 % 4
+    for first in range(0, out.shape[0], 4):
+        tiles = [
+            pieces[here ^ plane, first * PIECE : (first + 4) * PIECE, :].astype(jnp.float32)
+            for plane in range(4)
+        ]
+        for at in range(4):
+            rows = [tile[at * PIECE : (at + 1) * PIECE, :] for tile in tiles]
+            out[first + at] = jnp.concatenate(rows, axis=0).astype(jnp.bfloat16)
+
+
+def pack_planes(pieces, after):
+    blocks = pieces.shape[1] // PIECE
+    return pl.pallas_call(
+        pack_planes_kernel,
+        in_specs=[pl.BlockSpec(memory_space=pltpu.VMEM)] + [pl.BlockSpec(memory_space=pl.ANY)] * len(after),
+        out_shape=jax.ShapeDtypeStruct((blocks, TILE, LANES), jnp.bfloat16),
+        compiler_params=pltpu.CompilerParams(vmem_limit_bytes=8 * MIB),
+        cost_estimate=pl.CostEstimate(flops=300_000, bytes_accessed=300_000, transcendentals=0),
+    )(pieces, *after)
+
+
+def pack_kernel(*refs, count, after):
+    outs = refs[count + after :]
+    blocks = outs[0].shape[0]
+    held = blocks * PIECE
+    pieces = [(ref, base) for ref in refs[:count] for base in range(0, ref.shape[0], held)]
     for first in range(0, blocks, 4):
         tiles = [
-            piece[first * PIECE : (first + 4) * PIECE, :].astype(jnp.float32) for piece in pieces
+            ref[base + first * PIECE : base + (first + 4) * PIECE, :].astype(jnp.float32)
+            for ref, base in pieces
         ]
         for at in range(4):
             block = first + at
             rows = jnp.concatenate(
                 [tile[at * PIECE : (at + 1) * PIECE, :] for tile in tiles], axis=0
             ).astype(jnp.bfloat16)
-            full[block] = rows
-            if block < blocks // 2:
-                low[block] = rows
-            else:
-                high[block - blocks // 2] = rows
-
-
-def packed_shapes(blocks):
-    half = jax.ShapeDtypeStruct((blocks // 2, TILE, LANES), jnp.bfloat16)
-    return (half, half, jax.ShapeDtypeStruct((blocks, TILE, LANES), jnp.bfloat16))
-
-
-def norm_pack(own, z1, z2, z3, gain):
-    blocks = own.shape[1] // LANES
+            outs[0][block] = rows
+            half = outs[1].shape[0]
+            outs[1 + block // half][block % half] = rows
+
+
+def pack(pieces, after):
+    blocks = sum(piece.shape[0] for piece in pieces) // TILE
+    counts = (blocks, blocks // 2, blocks // 2)
     return pl.pallas_call(
-        norm_pack_kernel,
-        out_shape=packed_shapes(blocks),
+        functools.partial(pack_kernel, count=len(pieces), after=len(after)),
+        in_specs=[pl.BlockSpec(memory_space=pltpu.VMEM)] * len(pieces)
+        + [pl.BlockSpec(memory_space=pl.ANY)] * len(after),
+        out_shape=[jax.ShapeDtypeStruct((count, TILE, LANES), jnp.bfloat16) for count in counts],
         compiler_params=pltpu.CompilerParams(vmem_limit_bytes=8 * MIB),
-        cost_estimate=pl.CostEstimate(flops=4_000_000, bytes_accessed=2_000_000, transcendentals=0),
-    )(own, z1, z2, z3, gain[None, :])
-
-
-def pack(own, z1, z2, z3):
-    blocks = own.shape[0] // PIECE
-    return pl.pallas_call(
-        pack_kernel,
-        out_shape=packed_shapes(blocks),
-        compiler_params=pltpu.CompilerParams(vmem_limit_bytes=8 * MIB),
-        cost_estimate=pl.CostEstimate(flops=1_000_000, bytes_accessed=2_000_000, transcendentals=0),
-    )(own, z1, z2, z3)
+        cost_estimate=pl.CostEstimate(flops=1_000_000, bytes_accessed=1_000_000, transcendentals=0),
+    )(*pieces, *after)
 
 
 def swapped(array, mask, devices):
     return lax.ppermute(array, "wide", [(i, i ^ mask) for i in range(devices)])
 
 
-def gather_rows(piece, near, pack_pieces, devices):
+def gather_rows(main, rest, devices, weights=()):
     swap = functools.partial(swapped, devices=devices)
-    z2, z3, z1 = swap(piece, 16), swap(piece, 24), swap(piece, 8)
-    low, high, full = pack_pieces(near, z1, z2, z3)
+    z1, z2, z3 = swap(main, 8), swap(main, 16), swap(main, 24)
+    planes = [
+        [first + 2 * plane for plane in range(4)] for first in range(devices) if first // 2 % 4 == 0
+    ]
+    rests = lax.all_gather(rest, "wide", axis_index_groups=planes)
+    near_weights = prefetch(weights, ()) if weights else ()
+    tail = pack_planes(rests, (z1, z2, z3, *near_weights[-1:]))
+    tails = jnp.concatenate([tail, swap(tail, 8)], axis=0)
+    full, low, high = pack((main, z1, z2, z3), near_weights[-1:])
+    later_high, later_low, tails = lax.optimization_barrier((high, low, tails))
     x_low, y_high = swap(low, 2), swap(high, 4)
-    x_high, y_low = swap(high, 2), swap(low, 4)
+    x_high, y_low = swap(later_high, 2), swap(later_low, 4)
     d_low, d_high = swap(x_low, 4), swap(y_high, 2)
+    x_high, y_low, full, near_tails, x_near, y_near = lax.optimization_barrier(
+        (x_high, y_low, full, tails, x_low, y_high)
+    )
     other = swap(full, 1)
-    mine = [(low, high), (x_low, x_high), (y_low, y_high), (d_low, d_high)]
-    theirs = [(swap(a, 1), swap(b, 1)) for a, b in mine[1:]]
-    return mine, other, theirs
-
-
-def prefetch_kernel(*refs):
-    count = len(refs) // 3
+    far_tails = swap(tails, 16)
+    mine = [low, x_low, y_low, d_low, high, x_high, y_high, d_high]
+    theirs = [other] + [swap(array, 1) for array in (x_near, y_low, d_low, x_high, y_near, d_high)]
+    both = [tails, far_tails, swap(near_tails, 1), swap(far_tails, 1)]
+    return mine + theirs + both, near_weights
+
+
+RUNS = (
+    ((0, 0), (1, 0), (2, 0), (3, 0), (8, 0), (9, 0), (10, 0), (11, 0)),
+    ((4, 0), (5, 0), (6, 0), (7, 0), (8, 1), (12, 0), (13, 0), (14, 0)),
+    ((15, 0), (15, 1), (16, 0), (16, 1), (17, 0), (17, 1), (18, 0), (18, 1)),
+)
+GATHERED = 19
+
+
+def prefetch_kernel(*refs, count, after):
+    outs, signals = refs[count + after : 2 * count + after], refs[2 * count + after :]
     copies = [
-        pltpu.make_async_copy(refs[at], refs[count + at], refs[2 * count + at]) for at in range(count)
+        pltpu.make_async_copy(refs[at], outs[at], signals[at]) for at in range(count)
     ]
     for copy in copies:
         copy.start()
@@ -198,22 +247,22 @@
         copy.wait()
 
 
-def prefetch(far, near=()):
-    arrays = (*far, *near)
+def prefetch(arrays, after):
+    count = len(arrays)
     return pl.pallas_call(
-        prefetch_kernel,
-        in_specs=[pl.BlockSpec(memory_space=pltpu.HBM)] * len(far)
-        + [pl.BlockSpec(memory_space=pl.ANY)] * len(near),
-        out_specs=[pl.BlockSpec(memory_space=pl.ANY)] * len(arrays),
+        functools.partial(prefetch_kernel, count=count, after=len(after)),
+        in_specs=[pl.BlockSpec(memory_space=pltpu.HBM)] * count
+        + [pl.BlockSpec(memory_space=pl.ANY)] * len(after),
+        out_specs=[pl.BlockSpec(memory_space=pl.ANY)] * count,
         out_shape=[pltpu.VMEM(array.shape, array.dtype) for array in arrays],
-        scratch_shapes=[pltpu.SemaphoreType.DMA] * len(arrays),
+        scratch_shapes=[pltpu.SemaphoreType.DMA] * count,
         compiler_params=pltpu.CompilerParams(vmem_limit_bytes=MIB),
         cost_estimate=pl.CostEstimate(
             flops=0,
             bytes_accessed=sum(array.size * array.dtype.itemsize for array in arrays),
             transcendentals=0,
         ),
-    )(*[pltpu.with_memory_space_constraint(array, pltpu.HBM) for array in far], *near)
+    )(*[pltpu.with_memory_space_constraint(array, pltpu.HBM) for array in arrays], *after)
 
 
 def source_rows(me, rows):
@@ -224,36 +273,49 @@
     return (me ^ (core + 2 * plane + 8 * column)) * PIECE + at % PIECE
 
 
-COUNT = 16
-
-
-def multiply(refs, weight, total, weight_kv=None, total_kv=None):
-    low, high = refs[0:8], refs[8:16]
-    total[...] = jnp.zeros_like(total)
-    if weight_kv is not None:
-        total_kv[...] = jnp.zeros_like(total_kv)
-    half = low[0].shape[0]
-    blocks = 2 * half
-    for parts, base in ((low, 0), (high, half)):
-
-        def add(step, _, parts=parts, base=base):
-            first = step * COUNT
+MOST = 26
+
+
+def multiply(refs, totals, rests):
+    base = 0
+    counts = (refs[0].shape[0], refs[4].shape[0], refs[15].shape[0] // 2)
+    for run, count in enumerate(counts):
+        steps = -(-count // MOST)
+        width = count // steps
+        parts = [(refs[at], offset * count) for at, offset in RUNS[run]]
+        sums = rests if run == 2 else totals
+        if run != 1:
+            for total, _, _ in sums:
+                total[...] = jnp.zeros_like(total)
+
+        def add(step, _, parts=parts, base=base, width=width, sums=sums):
+            first = step * width
             columns = []
-            for at in range(COUNT):
-                column = []
-                for ref in parts:
-                    offset = base if ref.shape[0] == blocks else 0
-                    column.append(ref[first + at + offset])
-                columns.append(jnp.concatenate(column, axis=0))
+            for at in range(width):
+                columns.append(
+                    jnp.concatenate([ref[first + at + offset] for ref, offset in parts], axis=0)
+                )
             rows = jnp.concatenate(columns, axis=1)
-            depth = pl.ds(pl.multiple_of((base + first) * LANES, COUNT * LANES), COUNT * LANES)
-            total[...] += jnp.dot(rows, weight[depth, :], preferred_element_type=jnp.float32)
-            if weight_kv is not None:
-                total_kv[...] += lax.dot_general(
-                    rows, weight_kv[:, depth], (((1,), (1,)), ((), ())), preferred_element_type=jnp.float32
-                )
-
-        lax.fori_loop(0, half // COUNT, add, None)
+            depth = pl.ds(pl.multiple_of((base + first) * LANES, 2 * LANES), width * LANES)
+            for total, weight, turned in sums:
+                if turned:
+                    total[...] += lax.dot_general(
+                        rows, weight[:, depth], (((1,), (1,)), ((), ())), preferred_element_type=jnp.float32
+                    )
+                else:
+                    total[...] += jnp.dot(rows, weight[depth, :], preferred_element_type=jnp.float32)
+
+        lax.fori_loop(0, steps, add, None)
+        base += count
+    for (total, _, _), (rest, _, _) in zip(totals, rests):
+        for core in range(2):
+            for plane in range(4):
+                for pair in range(0, 4, 2):
+                    low = core * 64 + plane * TILE + pair * PIECE
+                    there = core * 64 + pair * TILE + plane * PIECE
+                    total[low : low + 8, :] += jnp.concatenate(
+                        [rest[there : there + 4, :], rest[there + TILE : there + TILE + 4, :]], axis=0
+                    )
 
 
 def one_hot(equal):
@@ -267,9 +329,13 @@
 
 
 def query_kernel(*refs):
-    weight, weight_kv, sessions, out, total, total_kv = refs[16:]
+    weight, weight_kv, sessions, out, total, total_kv, rest, rest_kv = refs[GATHERED:]
     me = lax.axis_index("wide")
-    multiply(refs, weight, total, weight_kv, total_kv)
+    multiply(
+        refs,
+        ((total, weight, False), (total_kv, weight_kv, True)),
+        ((rest, weight, False), (rest_kv, weight_kv, True)),
+    )
     rows, width = total.shape
     heads = width // LANES
     devices = rows // PIECE
@@ -297,8 +363,8 @@
 
 
 def out_kernel(*refs):
-    weight, sessions, out, total = refs[16:]
-    multiply(refs, weight, total)
+    weight, sessions, out, total, rest = refs[GATHERED:]
+    multiply(refs, ((total, weight, False),), ((rest, weight, False),))
     rows = total.shape[0]
     source = source_rows(lax.axis_index("wide"), rows)
     chosen = one_hot(as_column(sessions) == source)
@@ -306,16 +372,8 @@
     out[...] = jnp.dot(chosen, rounded, preferred_element_type=jnp.float32).astype(jnp.bfloat16)
 
 
-def gathered_operands(gathered):
-    mine, other, theirs = gathered
-    operands = []
-    for half in range(2):
-        operands += [pair[half] for pair in mine] + [other] + [pair[half] for pair in theirs]
-    return operands
-
-
 def project(kernel, gathered, weights, session_ids, out_shape, scratch):
-    operands = gathered_operands(gathered) + list(weights) + [session_ids[None, :]]
+    operands = list(gathered) + list(weights) + [session_ids[None, :]]
     whole = pl.BlockSpec(memory_space=pltpu.VMEM)
     rows = session_ids.shape[0]
     depth = weights[0].shape[0]
@@ -325,7 +383,7 @@
         in_specs=[whole] * len(operands),
         out_specs=whole,
         out_shape=jax.ShapeDtypeStruct(out_shape, jnp.bfloat16),
-        scratch_shapes=[pltpu.VMEM((rows, width), jnp.float32) for width in scratch],
+        scratch_shapes=[pltpu.VMEM((rows, width), jnp.float32) for width in 2 * scratch],
         compiler_params=pltpu.CompilerParams(vmem_limit_bytes=PROJECT_MIB * MIB),
         cost_estimate=pl.CostEstimate(
             flops=2 * rows * depth * columns, bytes_accessed=2 * depth * (columns + rows), transcendentals=0
@@ -336,7 +394,7 @@
 PROJECT_MIB = 8
 
 
-def attend_kernel(received, keys, values, lengths, out):
+def attend_kernel(received, keys, values, lengths, main, rest):
     sessions, kv_heads, cache_len, width = keys.shape
     devices = received.shape[0]
     per_group = devices // kv_heads
@@ -403,7 +461,14 @@
         own_weights = (own_exp / total).astype(jnp.bfloat16)
         attended = jnp.dot(weights, group_values, preferred_element_type=jnp.float32)
         attended += jnp.dot(own_weights, own_value, preferred_element_type=jnp.float32)
-        out[group * rows : (group + 1) * rows, :] = attended.astype(jnp.bfloat16)
+        attended = attended.astype(jnp.bfloat16)
+        first = group * rows
+        kept = min(max(main.shape[0] - first, 0), rows)
+        if kept:
+            main[first : first + kept, :] = attended[0:kept, :]
+        if kept < rows:
+            first = max(first - main.shape[0], 0)
+            rest[first : first + rows - kept, :] = attended[kept:, :]
 
 
 def attend(received, keys, values, lengths):
@@ -412,7 +477,7 @@
     return pl.pallas_call(
         attend_kernel,
         in_specs=[whole] * 3 + [pl.BlockSpec(memory_space=pltpu.SMEM)],
-        out_shape=jax.ShapeDtypeStruct((devices * TILE, width), jnp.bfloat16),
+        out_shape=split_shapes(devices * TILE // PIECE),
         compiler_params=pltpu.CompilerParams(vmem_limit_bytes=8 * MIB),
         cost_estimate=pl.CostEstimate(
             flops=150_000_000, bytes_accessed=3_000_000, transcendentals=300_000
@@ -428,11 +493,8 @@
     tokens, norm_gain, w_query, w_keyval, w_out, cache_keys, cache_values, session_ids, lengths, devices
 ):
     rows = devices * PIECE
-    near, gain, near_query, near_keyval, near_keys, near_values = prefetch(
-        (tokens, norm_gain, w_query, w_keyval, cache_keys, cache_values)
-    )
-    pack_tokens = functools.partial(norm_pack, gain=gain)
-    gathered = gather_rows(tokens, near, pack_tokens, devices)
+    main, rest = norm(tokens, norm_gain)
+    gathered, (near_query, near_keyval) = gather_rows(main, rest, devices, (w_query, w_keyval))
     local = project(
         query_kernel,
         gathered,
@@ -442,9 +504,8 @@
         (w_query.shape[1], w_keyval.shape[0]),
     )
     received = lax.all_to_all(local, "wide", split_axis=0, concat_axis=0, tiled=True)
-    attended = attend(received, inside(near_keys), inside(near_values), lengths)
-    near_out, near = prefetch((w_out,), (attended,))
-    gathered = gather_rows(attended, near, pack, devices)
+    main, rest = attend(received, inside(cache_keys), inside(cache_values), lengths)
+    gathered, (near_out,) = gather_rows(main, rest, devices, (w_out,))
     return project(
         out_kernel, gathered, (inside(near_out),), session_ids, (rows, w_out.shape[1]), (w_out.shape[1],)
     )

time: 108 us -> 115 us (1.065)
  waiting for transfers between devices: 41.9 us -> 25.6 us
  blocking collectives: 14.7 us -> 30.7 us
  starting transfers between devices: 24.3 us -> 32.5 us
  Pallas kernels: 27 us -> 25.8 us
    all_gather x0 -> x2, blocking collectives: none -> 16.5 us  [gather_rows(): rests = lax.all_gather(rest, 'wide', axis_index_groups=planes)]
    ppermute x32 -> x40, waiting for transfers between devices: 41.9 us -> 25.6 us  [swapped(): return lax.ppermute(array, 'wide', [(i, i ^ mask) for i in range(devices)])]
    ppermute x32 -> x40, starting transfers between devices: 24.3 us -> 32.5 us  [swapped(): return lax.ppermute(array, 'wide', [(i, i ^ mask) for i in range(devices)])]
    pallas_call x2, Pallas kernels: 9.73 us -> 8.45 us  [project(): pl.pallas_call(kernel, in_specs=[whole] * len(operands), out_specs=whole,...]
    pallas_call x4 -> x7, Pallas kernels: 13.6 us -> 13.7 us  [the longest x2 12.2 us: prefetch(): pl.pallas_call(functools.partial(prefetch_kernel, count=count, after=len(...]
  transfers between devices with their start and end apart: 32 -> 40, of which waited for: 14 -> 20; matrix products, arithmetic and copies ran while one was open for 0% -> 0% of each run, Pallas kernels for 12% -> 11%
where the time goes in v3:
time: 115 us
  starting transfers between devices  32.5 us (28%)
  blocking collectives  30.7 us (27%)
  Pallas kernels  25.8 us (22%)
  waiting for transfers between devices  25.6 us (22%)
    ppermute x40, starting transfers between devices, swapped(): return lax.ppermute(array, 'wide', [(i, i ^ mask) for i in range(devices)])  32.5 us
    ppermute x40, waiting for transfers between devices, swapped(): return lax.ppermute(array, 'wide', [(i, i ^ mask) for i in range(devices)])  25.6 us
    all_gather x2, blocking collectives, gather_rows(): rests = lax.all_gather(rest, 'wide', axis_index_groups=planes)  16.5 us
    all_to_all x1, blocking collectives, on_block(): lax.all_to_all(local, 'wide', split_axis=0, concat_axis=0, tiled=True)  14.2 us
    pallas_call x2, Pallas kernels, prefetch(): pl.pallas_call(functools.partial(prefetch_kernel, count=count, after=len(...  12.2 us
    pallas_call x2, Pallas kernels, project(): pl.pallas_call(kernel, in_specs=[whole] * len(operands), out_specs=whole,...  8.45 us
    pallas_call x1, Pallas kernels, attend(): pl.pallas_call(attend_kernel, in_specs=[whole] * 3 + [pl.BlockSpec(memory...  3.67 us
  transfers between devices with their start and end apart: 40, of which 20 were waited for; matrix products, arithmetic and copies ran while one was open for 0% of the time, Pallas kernels for 11%

profile of v3, /device:TPU:0, one launch (start us, length us, event | category | flops | bytes accessed | tf_op | source)
XLA Modules:
  0.0 114.8 jit_solution(15917368406400719336)
XLA Ops:
  0.0 1.2 %shard_map.91 = (bf16[416,128]{1,0:T(8,128)(2,1)S(1)}, bf16[96,128]{1,0:T(8,128)(2,1)S(1)}) custom-call(bf16[4,16384]{1,0:T(4,128)(2,1)} %tokens.1, f32[1,16384]{1,0:T(1,128)} %bitcast.8), custom_call_target="tpu_custom_call" | custom-call | flops 500000 | bytes 400000 | tf_op jit(solution)/shard_map/pallas_call | solution.py:133
  1.2 3.1 %collective-permute-start = (bf16[416,128]{1,0:T(8,128)(2,1)S(1)}, bf16[416,128]{1,0:T(8,128)(2,1)S(1)}, u32[]{:S(2)}, u32[]{:S(2)}) collective-permute-start(bf16[416,128]{1,0:T(8,128)(2,1)S(1)} %get-tuple-element.35.refs_0_), channel_id=1, source_target_pairs={{0,8},{1,9},{2,10},{3,11},{4,12},{5,13},{6,14},{7,15},{8,0},{9,1},... | collective-permute-start | bytes 319496 | tf_op jit(solution)/shard_map/ppermute | solution.py:202
  4.3 2.6 %collective-permute-start.1 = (bf16[416,128]{1,0:T(8,128)(2,1)S(1)}, bf16[416,128]{1,0:T(8,128)(2,1)S(1)}, u32[]{:S(2)}, u32[]{:S(2)}) collective-permute-start(bf16[416,128]{1,0:T(8,128)(2,1)S(1)} %get-tuple-element.35.refs_0_), channel_id=1, source_target_pairs={{0,16},{1,17},{2,18},{3,19},{4,20},{5,21},{6,22},{7,23},{8,24},{9,... | collective-permute-start | bytes 319496 | tf_op jit(solution)/shard_map/ppermute | solution.py:202
  6.9 6.4 %shard_map.92 = (bf16[16384,512]{1,0:T(8,128)(2,1)S(1)}, bf16[64,16384]{1,0:T(8,128)(2,1)S(1)}) custom-call(bf16[16384,512]{1,0:T(8,128)(2,1)} %refs_0_.2, bf16[64,16384]{1,0:T(8,128)(2,1)} %refs_1_.1), custom_call_target="tpu_custom_call" | custom-call | bytes 18874368 | tf_op jit(solution)/shard_map/pallas_call | solution.py:252
  13.3 8.7 %all-gather = bf16[384,128]{1,0:T(8,128)(2,1)S(1)} all-gather(bf16[96,128]{1,0:T(8,128)(2,1)S(1)} %get-tuple-element.39), channel_id=2, replica_groups={{0,2,4,6},{1,3,5,7},{8,10,12,14},{9,11,13,15},{16,18,20,22},{17,19,21,2..., dimensions={0}, use_global_device_ids=true | all-gather | bytes 122880 | tf_op jit(solution)/shard_map/all_gather | solution.py:211
  23.0 1.6 %collective-permute-start.3 = (bf16[52,16,128]{2,1,0:T(8,128)(2,1)S(1)}, bf16[52,16,128]{2,1,0:T(8,128)(2,1)S(1)}, u32[]{:S(2)}, u32[]{:S(2)}) collective-permute-start(bf16[52,16,128]{2,1,0:T(8,128)(2,1)S(1)} %get-tuple-element.41.refs_0_), channel_id=1, source_target_pairs={{0,2},{1,3},{2,0},{3,1},{4,6},{5,7},{6,4},{7,5},{8,10},{9,11},{10,... | collective-permute-start | bytes 638984 | tf_op jit(solution)/shard_map/ppermute | solution.py:202
  25.1 1.7 %collective-permute-done.4 = bf16[24,16,128]{2,1,0:T(8,128)(2,1)S(1)} collective-permute-done((bf16[24,16,128]{2,1,0:T(8,128)(2,1)S(1)}, bf16[24,16,128]{2,1,0:T(8,128)(2,1)S(1)}, u32[]{:S(2)}, u32[]{:S(2)}) %collective-permute-start.4) | collective-permute-done | bytes 98336 | tf_op jit(solution)/shard_map/ppermute | solution.py:202
  26.8 1.6 %collective-permute-start.5 = (bf16[52,16,128]{2,1,0:T(8,128)(2,1)S(1)}, bf16[52,16,128]{2,1,0:T(8,128)(2,1)S(1)}, u32[]{:S(2)}, u32[]{:S(2)}) collective-permute-start(bf16[52,16,128]{2,1,0:T(8,128)(2,1)S(1)} %get-tuple-element.40.refs_4_), channel_id=1, source_target_pairs={{0,2},{1,3},{2,0},{3,1},{4,6},{5,7},{6,4},{7,5},{8,10},{9,11},{10,... | collective-permute-start | bytes 638984 | tf_op jit(solution)/shard_map/ppermute | solution.py:202
  28.9 2.3 %collective-permute-done.3.refs_1_ = bf16[52,16,128]{2,1,0:T(8,128)(2,1)S(1)} collective-permute-done((bf16[52,16,128]{2,1,0:T(8,128)(2,1)S(1)}, bf16[52,16,128]{2,1,0:T(8,128)(2,1)S(1)}, u32[]{:S(2)}, u32[]{:S(2)}) %collective-permute-start.3) | collective-permute-done | bytes 213024 | tf_op jit(solution)/shard_map/ppermute | solution.py:202
  31.2 1.5 %collective-permute-start.8 = (bf16[52,16,128]{2,1,0:T(8,128)(2,1)S(1)}, bf16[52,16,128]{2,1,0:T(8,128)(2,1)S(1)}, u32[]{:S(2)}, u32[]{:S(2)}) collective-permute-start(bf16[52,16,128]{2,1,0:T(8,128)(2,1)S(1)} %collective-permute-done.3.refs_1_), channel_id=1, source_target_pairs={{0,4},{1,5},{2,6},{3,7},{4,0},{5,1},{6,2},{7,3},{8,12},{9,13},{10,... | collective-permute-start | bytes 638984 | tf_op jit(solution)/shard_map/ppermute | solution.py:202
  33.3 3.4 %collective-permute-start.17 = (bf16[48,16,128]{2,1,0:T(8,128)(2,1)S(1)}, bf16[48,16,128]{2,1,0:T(8,128)(2,1)S(1)}, u32[]{:S(2)}, u32[]{:S(2)}) collective-permute-start(bf16[48,16,128]{2,1,0:T(8,128)(2,1)S(1)} %pad_maximum_fusion.refs_15_), channel_id=1, source_target_pairs={{0,16},{1,17},{2,18},{3,19},{4,20},{5,21},{6,22},{7,23},{8,24},{9,... | collective-permute-start | bytes 589832 | tf_op jit(solution)/shard_map/ppermute | solution.py:202
  37.2 5.2 %collective-permute-done.17.refs_16_ = bf16[48,16,128]{2,1,0:T(8,128)(2,1)S(1)} collective-permute-done((bf16[48,16,128]{2,1,0:T(8,128)(2,1)S(1)}, bf16[48,16,128]{2,1,0:T(8,128)(2,1)S(1)}, u32[]{:S(2)}, u32[]{:S(2)}) %collective-permute-start.17) | collective-permute-done | bytes 196640 | tf_op jit(solution)/shard_map/ppermute | solution.py:202
  43.0 1.5 %collective-permute-done.19.refs_18_ = bf16[48,16,128]{2,1,0:T(8,128)(2,1)S(1)} collective-permute-done((bf16[48,16,128]{2,1,0:T(8,128)(2,1)S(1)}, bf16[48,16,128]{2,1,0:T(8,128)(2,1)S(1)}, u32[]{:S(2)}, u32[]{:S(2)}) %collective-permute-start.19) | collective-permute-done | bytes 196640 | tf_op jit(solution)/shard_map/ppermute | solution.py:202
  46.9 4.6 %shard_map.95 = bf16[32,32,128]{2,1,0:T(8,128)(2,1)S(1)} custom-call(bf16[52,16,128]{2,1,0:T(8,128)(2,1)S(1)} %get-tuple-element.41.refs_0_, bf16[52,16,128]{2,1,0:T(8,128)(2,1)S(1)} %collective-permute-done.3.refs_1_, bf16[52,16,128]{2,1,0:T(8,128)(2,1)S(1)} %collective-permute-done.6.refs_2_, bf16[52,16,128]{2,1,0:T(8,128)(2,1)S(1)} %collective-permute-done.8.refs_3_, ...), custom_call_target="tpu_custom_call" | custom-call | flops 2415919104 | bytes 23068672 | tf_op jit(solution)/shard_map/pallas_call | solution.py:381
  51.4 14.2 %all_to_all.5.received = bf16[32,32,128]{2,1,0:T(8,128)(2,1)S(1)} all-to-all(bf16[32,32,128]{2,1,0:T(8,128)(2,1)S(1)} %shard_map.95), channel_id=1, replica_groups=mesh['groups'=1,'wide'=32] {'wide'}, dimensions={0} | all-to-all | bytes 524288 | tf_op jit(solution)/shard_map/all_to_all | solution.py:506
  65.6 3.7 %shard_map.96 = (bf16[416,128]{1,0:T(8,128)(2,1)S(1)}, bf16[96,128]{1,0:T(8,128)(2,1)S(1)}) custom-call(bf16[32,32,128]{2,1,0:T(8,128)(2,1)S(1)} %all_to_all.5.received, bf16[4,8,128,128]{3,2,1,0:T(8,128)(2,1)S(1)} %copy-done, bf16[4,8,128,128]{3,2,1,0:T(8,128)(2,1)S(1)} %copy-done.1, s32[4]{0:T(128)S(1)} %copy-done.3), custom_call_target="tpu_custom_call" | custom-call | flops 150000000 | bytes 3000000 | tf_op jit(solution)/shard_map/pallas_call | solution.py:477
  69.3 1.0 collective-permute-start.20
  70.3 1.0 collective-permute-start.21
  71.3 2.5 %collective-permute-start.22 = (bf16[416,128]{1,0:T(8,128)(2,1)S(1)}, bf16[416,128]{1,0:T(8,128)(2,1)S(1)}, u32[]{:S(2)}, u32[]{:S(2)}) collective-permute-start(bf16[416,128]{1,0:T(8,128)(2,1)S(1)} %get-tuple-element.51.refs_0_), channel_id=1, source_target_pairs={{0,24},{1,25},{2,26},{3,27},{4,28},{5,29},{6,30},{7,31},{8,16},{9,... | collective-permute-start | bytes 319496 | tf_op jit(solution)/shard_map/ppermute | solution.py:202
  73.7 5.8 %shard_map.97.refs_4_.refs_19_ = bf16[16384,512]{1,0:T(8,128)(2,1)S(1)} custom-call(bf16[16384,512]{1,0:T(8,128)(2,1)} %refs_0_.3), custom_call_target="tpu_custom_call" | custom-call | bytes 16777216 | tf_op jit(solution)/shard_map/pallas_call | solution.py:252
  79.5 7.8 %all-gather.1 = bf16[384,128]{1,0:T(8,128)(2,1)S(1)} all-gather(bf16[96,128]{1,0:T(8,128)(2,1)S(1)} %get-tuple-element.54), channel_id=3, replica_groups={{0,2,4,6},{1,3,5,7},{8,10,12,14},{9,11,13,15},{16,18,20,22},{17,19,21,2..., dimensions={0}, use_global_device_ids=true | all-gather | bytes 122880 | tf_op jit(solution)/shard_map/all_gather | solution.py:211
  87.6 1.2 %collective-permute-start.23 = (bf16[52,16,128]{2,1,0:T(8,128)(2,1)S(1)}, bf16[52,16,128]{2,1,0:T(8,128)(2,1)S(1)}, u32[]{:S(2)}, u32[]{:S(2)}) collective-permute-start(bf16[52,16,128]{2,1,0:T(8,128)(2,1)S(1)} %get-tuple-element.56.refs_0_), channel_id=1, source_target_pairs={{0,2},{1,3},{2,0},{3,1},{4,6},{5,7},{6,4},{7,5},{8,10},{9,11},{10,... | collective-permute-start | bytes 638984 | tf_op jit(solution)/shard_map/ppermute | solution.py:202
  88.9 0.8 collective-permute-start.27
  89.7 2.4 %collective-permute-done.24 = bf16[24,16,128]{2,1,0:T(8,128)(2,1)S(1)} collective-permute-done((bf16[24,16,128]{2,1,0:T(8,128)(2,1)S(1)}, bf16[24,16,128]{2,1,0:T(8,128)(2,1)S(1)}, u32[]{:S(2)}, u32[]{:S(2)}) %collective-permute-start.24) | collective-permute-done | bytes 98336 | tf_op jit(solution)/shard_map/ppermute | solution.py:202
  92.1 1.2 %collective-permute-start.25 = (bf16[52,16,128]{2,1,0:T(8,128)(2,1)S(1)}, bf16[52,16,128]{2,1,0:T(8,128)(2,1)S(1)}, u32[]{:S(2)}, u32[]{:S(2)}) collective-permute-start(bf16[52,16,128]{2,1,0:T(8,128)(2,1)S(1)} %get-tuple-element.55.refs_4_), channel_id=1, source_target_pairs={{0,2},{1,3},{2,0},{3,1},{4,6},{5,7},{6,4},{7,5},{8,10},{9,11},{10,... | collective-permute-start | bytes 638984 | tf_op jit(solution)/shard_map/ppermute | solution.py:202
  94.2 1.6 %collective-permute-done.23.refs_1_ = bf16[52,16,128]{2,1,0:T(8,128)(2,1)S(1)} collective-permute-done((bf16[52,16,128]{2,1,0:T(8,128)(2,1)S(1)}, bf16[52,16,128]{2,1,0:T(8,128)(2,1)S(1)}, u32[]{:S(2)}, u32[]{:S(2)}) %collective-permute-start.23) | collective-permute-done | bytes 213024 | tf_op jit(solution)/shard_map/ppermute | solution.py:202
  95.8 1.1 collective-permute-start.28
  96.9 0.9 collective-permute-start.29
  97.8 1.8 %collective-permute-start.37 = (bf16[48,16,128]{2,1,0:T(8,128)(2,1)S(1)}, bf16[48,16,128]{2,1,0:T(8,128)(2,1)S(1)}, u32[]{:S(2)}, u32[]{:S(2)}) collective-permute-start(bf16[48,16,128]{2,1,0:T(8,128)(2,1)S(1)} %pad_maximum_fusion.1.refs_15_), channel_id=1, source_target_pairs={{0,16},{1,17},{2,18},{3,19},{4,20},{5,21},{6,22},{7,23},{8,24},{9,... | collective-permute-start | bytes 589832 | tf_op jit(solution)/shard_map/ppermute | solution.py:202
  101.3 5.2 %collective-permute-done.37.refs_16_ = bf16[48,16,128]{2,1,0:T(8,128)(2,1)S(1)} collective-permute-done((bf16[48,16,128]{2,1,0:T(8,128)(2,1)S(1)}, bf16[48,16,128]{2,1,0:T(8,128)(2,1)S(1)}, u32[]{:S(2)}, u32[]{:S(2)}) %collective-permute-start.37) | collective-permute-done | bytes 196640 | tf_op jit(solution)/shard_map/ppermute | solution.py:202
  107.1 1.5 %collective-permute-done.39.refs_18_ = bf16[48,16,128]{2,1,0:T(8,128)(2,1)S(1)} collective-permute-done((bf16[48,16,128]{2,1,0:T(8,128)(2,1)S(1)}, bf16[48,16,128]{2,1,0:T(8,128)(2,1)S(1)}, u32[]{:S(2)}, u32[]{:S(2)}) %collective-permute-start.39) | collective-permute-done | bytes 196640 | tf_op jit(solution)/shard_map/ppermute | solution.py:202
  110.9 3.9 %shard_map.100 = bf16[128,512]{1,0:T(8,128)(2,1)} custom-call(bf16[52,16,128]{2,1,0:T(8,128)(2,1)S(1)} %get-tuple-element.56.refs_0_, bf16[52,16,128]{2,1,0:T(8,128)(2,1)S(1)} %collective-permute-done.23.refs_1_, bf16[52,16,128]{2,1,0:T(8,128)(2,1)S(1)} %collective-permute-done.26.refs_2_, bf16[52,16,128]{2,1,0:T(8,128)(2,1)S(1)} %collective-permute-done.28.refs_3_, ...), custom_call_target="tpu_custom_call" | custom-call | flops 2147483648 | bytes 20971520 | tf_op jit(solution)/shard_map/pallas_call | solution.py:381
  (71 shorter events, 11.8 us)
Async XLA Ops:
  1.2 20.8 %collective-permute-start = (bf16[416,128]{1,0:T(8,128)(2,1)S(1)}, bf16[416,128]{1,0:T(8,128)(2,1)S(1)}, u32[]{:S(2)}, u32[]{:S(2)}) collective-permute-start(bf16[416,128]{1,0:T(8,128)(2,1)S(1)} %get-tuple-element.35.refs_0_), channel_id=1, source_target_pairs={{0,8},{1,9},{2,10},{3,11},{4,12},{5,13},{6,14},{7,15},{8,0},{9,1},... | collective-permute-start | bytes 319496 | tf_op jit(solution)/shard_map/ppermute | solution.py:202
  4.3 17.7 %collective-permute-start.1 = (bf16[416,128]{1,0:T(8,128)(2,1)S(1)}, bf16[416,128]{1,0:T(8,128)(2,1)S(1)}, u32[]{:S(2)}, u32[]{:S(2)}) collective-permute-start(bf16[416,128]{1,0:T(8,128)(2,1)S(1)} %get-tuple-element.35.refs_0_), channel_id=1, source_target_pairs={{0,16},{1,17},{2,18},{3,19},{4,20},{5,21},{6,22},{7,23},{8,24},{9,... | collective-permute-start | bytes 319496 | tf_op jit(solution)/shard_map/ppermute | solution.py:202
  6.9 15.2 %collective-permute-start.2 = (bf16[416,128]{1,0:T(8,128)(2,1)S(1)}, bf16[416,128]{1,0:T(8,128)(2,1)S(1)}, u32[]{:S(2)}, u32[]{:S(2)}) collective-permute-start(bf16[416,128]{1,0:T(8,128)(2,1)S(1)} %get-tuple-element.35.refs_0_), channel_id=1, source_target_pairs={{0,24},{1,25},{2,26},{3,27},{4,28},{5,29},{6,30},{7,31},{8,16},{9,... | collective-permute-start | bytes 319496 | tf_op jit(solution)/shard_map/ppermute | solution.py:202
  22.1 4.7 %collective-permute-start.4 = (bf16[24,16,128]{2,1,0:T(8,128)(2,1)S(1)}, bf16[24,16,128]{2,1,0:T(8,128)(2,1)S(1)}, u32[]{:S(2)}, u32[]{:S(2)}) collective-permute-start(bf16[24,16,128]{2,1,0:T(8,128)(2,1)S(1)} %shard_map.94), channel_id=1, source_target_pairs={{0,8},{1,9},{2,10},{3,11},{4,12},{5,13},{6,14},{7,15},{8,0},{9,1},... | collective-permute-start | bytes 294920 | tf_op jit(solution)/shard_map/ppermute | solution.py:202
  23.0 8.2 %collective-permute-start.3 = (bf16[52,16,128]{2,1,0:T(8,128)(2,1)S(1)}, bf16[52,16,128]{2,1,0:T(8,128)(2,1)S(1)}, u32[]{:S(2)}, u32[]{:S(2)}) collective-permute-start(bf16[52,16,128]{2,1,0:T(8,128)(2,1)S(1)} %get-tuple-element.41.refs_0_), channel_id=1, source_target_pairs={{0,2},{1,3},{2,0},{3,1},{4,6},{5,7},{6,4},{7,5},{8,10},{9,11},{10,... | collective-permute-start | bytes 638984 | tf_op jit(solution)/shard_map/ppermute | solution.py:202
  24.5 8.2 %collective-permute-start.7 = (bf16[52,16,128]{2,1,0:T(8,128)(2,1)S(1)}, bf16[52,16,128]{2,1,0:T(8,128)(2,1)S(1)}, u32[]{:S(2)}, u32[]{:S(2)}) collective-permute-start(bf16[52,16,128]{2,1,0:T(8,128)(2,1)S(1)} %get-tuple-element.40.refs_4_), channel_id=1, source_target_pairs={{0,4},{1,5},{2,6},{3,7},{4,0},{5,1},{6,2},{7,3},{8,12},{9,13},{10,... | collective-permute-start | bytes 638984 | tf_op jit(solution)/shard_map/ppermute | solution.py:202
  26.8 9.8 %collective-permute-start.5 = (bf16[52,16,128]{2,1,0:T(8,128)(2,1)S(1)}, bf16[52,16,128]{2,1,0:T(8,128)(2,1)S(1)}, u32[]{:S(2)}, u32[]{:S(2)}) collective-permute-start(bf16[52,16,128]{2,1,0:T(8,128)(2,1)S(1)} %get-tuple-element.40.refs_4_), channel_id=1, source_target_pairs={{0,2},{1,3},{2,0},{3,1},{4,6},{5,7},{6,4},{7,5},{8,10},{9,11},{10,... | collective-permute-start | bytes 638984 | tf_op jit(solution)/shard_map/ppermute | solution.py:202
  28.4 8.3 %collective-permute-start.6 = (bf16[52,16,128]{2,1,0:T(8,128)(2,1)S(1)}, bf16[52,16,128]{2,1,0:T(8,128)(2,1)S(1)}, u32[]{:S(2)}, u32[]{:S(2)}) collective-permute-start(bf16[52,16,128]{2,1,0:T(8,128)(2,1)S(1)} %get-tuple-element.41.refs_0_), channel_id=1, source_target_pairs={{0,4},{1,5},{2,6},{3,7},{4,0},{5,1},{6,2},{7,3},{8,12},{9,13},{10,... | collective-permute-start | bytes 638984 | tf_op jit(solution)/shard_map/ppermute | solution.py:202
  31.2 11.2 %collective-permute-start.8 = (bf16[52,16,128]{2,1,0:T(8,128)(2,1)S(1)}, bf16[52,16,128]{2,1,0:T(8,128)(2,1)S(1)}, u32[]{:S(2)}, u32[]{:S(2)}) collective-permute-start(bf16[52,16,128]{2,1,0:T(8,128)(2,1)S(1)} %collective-permute-done.3.refs_1_), channel_id=1, source_target_pairs={{0,4},{1,5},{2,6},{3,7},{4,0},{5,1},{6,2},{7,3},{8,12},{9,13},{10,... | collective-permute-start | bytes 638984 | tf_op jit(solution)/shard_map/ppermute | solution.py:202
  32.7 10.2 %collective-permute-start.9 = (bf16[52,16,128]{2,1,0:T(8,128)(2,1)S(1)}, bf16[52,16,128]{2,1,0:T(8,128)(2,1)S(1)}, u32[]{:S(2)}, u32[]{:S(2)}) collective-permute-start(bf16[52,16,128]{2,1,0:T(8,128)(2,1)S(1)} %collective-permute-done.7.refs_6_), channel_id=1, source_target_pairs={{0,2},{1,3},{2,0},{3,1},{4,6},{5,7},{6,4},{7,5},{8,10},{9,11},{10,... | collective-permute-start | bytes 638984 | tf_op jit(solution)/shard_map/ppermute | solution.py:202
  33.3 9.2 %collective-permute-start.17 = (bf16[48,16,128]{2,1,0:T(8,128)(2,1)S(1)}, bf16[48,16,128]{2,1,0:T(8,128)(2,1)S(1)}, u32[]{:S(2)}, u32[]{:S(2)}) collective-permute-start(bf16[48,16,128]{2,1,0:T(8,128)(2,1)S(1)} %pad_maximum_fusion.refs_15_), channel_id=1, source_target_pairs={{0,16},{1,17},{2,18},{3,19},{4,20},{5,21},{6,22},{7,23},{8,24},{9,... | collective-permute-start | bytes 589832 | tf_op jit(solution)/shard_map/ppermute | solution.py:202
  36.7 8.3 %collective-permute-start.11 = (bf16[52,16,128]{2,1,0:T(8,128)(2,1)S(1)}, bf16[52,16,128]{2,1,0:T(8,128)(2,1)S(1)}, u32[]{:S(2)}, u32[]{:S(2)}) collective-permute-start(bf16[52,16,128]{2,1,0:T(8,128)(2,1)S(1)} %collective-permute-done.3.refs_1_), channel_id=1, source_target_pairs={{0,1},{1,0},{2,3},{3,2},{4,5},{5,4},{6,7},{7,6},{8,9},{9,8},{10,11... | collective-permute-start | bytes 638984 | tf_op jit(solution)/shard_map/ppermute | solution.py:202
  36.7 8.6 %collective-permute-start.12 = (bf16[52,16,128]{2,1,0:T(8,128)(2,1)S(1)}, bf16[52,16,128]{2,1,0:T(8,128)(2,1)S(1)}, u32[]{:S(2)}, u32[]{:S(2)}) collective-permute-start(bf16[52,16,128]{2,1,0:T(8,128)(2,1)S(1)} %collective-permute-done.6.refs_2_), channel_id=1, source_target_pairs={{0,1},{1,0},{2,3},{3,2},{4,5},{5,4},{6,7},{7,6},{8,9},{9,8},{10,11... | collective-permute-start | bytes 638984 | tf_op jit(solution)/shard_map/ppermute | solution.py:202
  42.4 4.4 %collective-permute-start.10 = (bf16[104,16,128]{2,1,0:T(8,128)(2,1)S(1)}, bf16[104,16,128]{2,1,0:T(8,128)(2,1)S(1)}, u32[]{:S(2)}, u32[]{:S(2)}) collective-permute-start(bf16[104,16,128]{2,1,0:T(8,128)(2,1)S(1)} %get-tuple-element.46), channel_id=1, source_target_pairs={{0,1},{1,0},{2,3},{3,2},{4,5},{5,4},{6,7},{7,6},{8,9},{9,8},{10,11... | collective-permute-start | bytes 1277960 | tf_op jit(solution)/shard_map/ppermute | solution.py:202
  42.4 2.0 %collective-permute-start.19 = (bf16[48,16,128]{2,1,0:T(8,128)(2,1)S(1)}, bf16[48,16,128]{2,1,0:T(8,128)(2,1)S(1)}, u32[]{:S(2)}, u32[]{:S(2)}) collective-permute-start(bf16[48,16,128]{2,1,0:T(8,128)(2,1)S(1)} %collective-permute-done.17.refs_16_), channel_id=1, source_target_pairs={{0,1},{1,0},{2,3},{3,2},{4,5},{5,4},{6,7},{7,6},{8,9},{9,8},{10,11... | collective-permute-start | bytes 589832 | tf_op jit(solution)/shard_map/ppermute | solution.py:202
  42.9 1.8 %collective-permute-start.18 = (bf16[48,16,128]{2,1,0:T(8,128)(2,1)S(1)}, bf16[48,16,128]{2,1,0:T(8,128)(2,1)S(1)}, u32[]{:S(2)}, u32[]{:S(2)}) collective-permute-start(bf16[48,16,128]{2,1,0:T(8,128)(2,1)S(1)} %pad_maximum_fusion.refs_15_), channel_id=1, source_target_pairs={{0,1},{1,0},{2,3},{3,2},{4,5},{5,4},{6,7},{7,6},{8,9},{9,8},{10,11... | collective-permute-start | bytes 589832 | tf_op jit(solution)/shard_map/ppermute | solution.py:202
  69.3 18.0 %collective-permute-start.20 = (bf16[416,128]{1,0:T(8,128)(2,1)S(1)}, bf16[416,128]{1,0:T(8,128)(2,1)S(1)}, u32[]{:S(2)}, u32[]{:S(2)}) collective-permute-start(bf16[416,128]{1,0:T(8,128)(2,1)S(1)} %get-tuple-element.51.refs_0_), channel_id=1, source_target_pairs={{0,8},{1,9},{2,10},{3,11},{4,12},{5,13},{6,14},{7,15},{8,0},{9,1},... | collective-permute-start | bytes 319496 | tf_op jit(solution)/shard_map/ppermute | solution.py:202
  70.3 17.1 %collective-permute-start.21 = (bf16[416,128]{1,0:T(8,128)(2,1)S(1)}, bf16[416,128]{1,0:T(8,128)(2,1)S(1)}, u32[]{:S(2)}, u32[]{:S(2)}) collective-permute-start(bf16[416,128]{1,0:T(8,128)(2,1)S(1)} %get-tuple-element.51.refs_0_), channel_id=1, source_target_pairs={{0,16},{1,17},{2,18},{3,19},{4,20},{5,21},{6,22},{7,23},{8,24},{9,... | collective-permute-start | bytes 319496 | tf_op jit(solution)/shard_map/ppermute | solution.py:202
  71.3 16.1 %collective-permute-start.22 = (bf16[416,128]{1,0:T(8,128)(2,1)S(1)}, bf16[416,128]{1,0:T(8,128)(2,1)S(1)}, u32[]{:S(2)}, u32[]{:S(2)}) collective-permute-start(bf16[416,128]{1,0:T(8,128)(2,1)S(1)} %get-tuple-element.51.refs_0_), channel_id=1, source_target_pairs={{0,24},{1,25},{2,26},{3,27},{4,28},{5,29},{6,30},{7,31},{8,16},{9,... | collective-permute-start | bytes 319496 | tf_op jit(solution)/shard_map/ppermute | solution.py:202
  87.4 4.7 %collective-permute-start.24 = (bf16[24,16,128]{2,1,0:T(8,128)(2,1)S(1)}, bf16[24,16,128]{2,1,0:T(8,128)(2,1)S(1)}, u32[]{:S(2)}, u32[]{:S(2)}) collective-permute-start(bf16[24,16,128]{2,1,0:T(8,128)(2,1)S(1)} %shard_map.99), channel_id=1, source_target_pairs={{0,8},{1,9},{2,10},{3,11},{4,12},{5,13},{6,14},{7,15},{8,0},{9,1},... | collective-permute-start | bytes 294920 | tf_op jit(solution)/shard_map/ppermute | solution.py:202
  87.6 8.2 %collective-permute-start.23 = (bf16[52,16,128]{2,1,0:T(8,128)(2,1)S(1)}, bf16[52,16,128]{2,1,0:T(8,128)(2,1)S(1)}, u32[]{:S(2)}, u32[]{:S(2)}) collective-permute-start(bf16[52,16,128]{2,1,0:T(8,128)(2,1)S(1)} %get-tuple-element.56.refs_0_), channel_id=1, source_target_pairs={{0,2},{1,3},{2,0},{3,1},{4,6},{5,7},{6,4},{7,5},{8,10},{9,11},{10,... | collective-permute-start | bytes 638984 | tf_op jit(solution)/shard_map/ppermute | solution.py:202
  88.9 8.1 %collective-permute-start.27 = (bf16[52,16,128]{2,1,0:T(8,128)(2,1)S(1)}, bf16[52,16,128]{2,1,0:T(8,128)(2,1)S(1)}, u32[]{:S(2)}, u32[]{:S(2)}) collective-permute-start(bf16[52,16,128]{2,1,0:T(8,128)(2,1)S(1)} %get-tuple-element.55.refs_4_), channel_id=1, source_target_pairs={{0,4},{1,5},{2,6},{3,7},{4,0},{5,1},{6,2},{7,3},{8,12},{9,13},{10,... | collective-permute-start | bytes 638984 | tf_op jit(solution)/shard_map/ppermute | solution.py:202
  92.1 8.1 %collective-permute-start.25 = (bf16[52,16,128]{2,1,0:T(8,128)(2,1)S(1)}, bf16[52,16,128]{2,1,0:T(8,128)(2,1)S(1)}, u32[]{:S(2)}, u32[]{:S(2)}) collective-permute-start(bf16[52,16,128]{2,1,0:T(8,128)(2,1)S(1)} %get-tuple-element.55.refs_4_), channel_id=1, source_target_pairs={{0,2},{1,3},{2,0},{3,1},{4,6},{5,7},{6,4},{7,5},{8,10},{9,11},{10,... | collective-permute-start | bytes 638984 | tf_op jit(solution)/shard_map/ppermute | solution.py:202
  93.4 7.4 %collective-permute-start.26 = (bf16[52,16,128]{2,1,0:T(8,128)(2,1)S(1)}, bf16[52,16,128]{2,1,0:T(8,128)(2,1)S(1)}, u32[]{:S(2)}, u32[]{:S(2)}) collective-permute-start(bf16[52,16,128]{2,1,0:T(8,128)(2,1)S(1)} %get-tuple-element.56.refs_0_), channel_id=1, source_target_pairs={{0,4},{1,5},{2,6},{3,7},{4,0},{5,1},{6,2},{7,3},{8,12},{9,13},{10,... | collective-permute-start | bytes 638984 | tf_op jit(solution)/shard_map/ppermute | solution.py:202
  95.8 10.7 %collective-permute-start.28 = (bf16[52,16,128]{2,1,0:T(8,128)(2,1)S(1)}, bf16[52,16,128]{2,1,0:T(8,128)(2,1)S(1)}, u32[]{:S(2)}, u32[]{:S(2)}) collective-permute-start(bf16[52,16,128]{2,1,0:T(8,128)(2,1)S(1)} %collective-permute-done.23.refs_1_), channel_id=1, source_target_pairs={{0,4},{1,5},{2,6},{3,7},{4,0},{5,1},{6,2},{7,3},{8,12},{9,13},{10,... | collective-permute-start | bytes 638984 | tf_op jit(solution)/shard_map/ppermute | solution.py:202
  96.9 10.1 %collective-permute-start.29 = (bf16[52,16,128]{2,1,0:T(8,128)(2,1)S(1)}, bf16[52,16,128]{2,1,0:T(8,128)(2,1)S(1)}, u32[]{:S(2)}, u32[]{:S(2)}) collective-permute-start(bf16[52,16,128]{2,1,0:T(8,128)(2,1)S(1)} %collective-permute-done.27.refs_6_), channel_id=1, source_target_pairs={{0,2},{1,3},{2,0},{3,1},{4,6},{5,7},{6,4},{7,5},{8,10},{9,11},{10,... | collective-permute-start | bytes 638984 | tf_op jit(solution)/shard_map/ppermute | solution.py:202
  97.8 8.7 %collective-permute-start.37 = (bf16[48,16,128]{2,1,0:T(8,128)(2,1)S(1)}, bf16[48,16,128]{2,1,0:T(8,128)(2,1)S(1)}, u32[]{:S(2)}, u32[]{:S(2)}) collective-permute-start(bf16[48,16,128]{2,1,0:T(8,128)(2,1)S(1)} %pad_maximum_fusion.1.refs_15_), channel_id=1, source_target_pairs={{0,16},{1,17},{2,18},{3,19},{4,20},{5,21},{6,22},{7,23},{8,24},{9,... | collective-permute-start | bytes 589832 | tf_op jit(solution)/shard_map/ppermute | solution.py:202
  100.8 8.3 %collective-permute-start.31 = (bf16[52,16,128]{2,1,0:T(8,128)(2,1)S(1)}, bf16[52,16,128]{2,1,0:T(8,128)(2,1)S(1)}, u32[]{:S(2)}, u32[]{:S(2)}) collective-permute-start(bf16[52,16,128]{2,1,0:T(8,128)(2,1)S(1)} %collective-permute-done.23.refs_1_), channel_id=1, source_target_pairs={{0,1},{1,0},{2,3},{3,2},{4,5},{5,4},{6,7},{7,6},{8,9},{9,8},{10,11... | collective-permute-start | bytes 638984 | tf_op jit(solution)/shard_map/ppermute | solution.py:202
  100.8 8.6 %collective-permute-start.32 = (bf16[52,16,128]{2,1,0:T(8,128)(2,1)S(1)}, bf16[52,16,128]{2,1,0:T(8,128)(2,1)S(1)}, u32[]{:S(2)}, u32[]{:S(2)}) collective-permute-start(bf16[52,16,128]{2,1,0:T(8,128)(2,1)S(1)} %collective-permute-done.26.refs_2_), channel_id=1, source_target_pairs={{0,1},{1,0},{2,3},{3,2},{4,5},{5,4},{6,7},{7,6},{8,9},{9,8},{10,11... | collective-permute-start | bytes 638984 | tf_op jit(solution)/shard_map/ppermute | solution.py:202
  106.5 4.4 %collective-permute-start.30 = (bf16[104,16,128]{2,1,0:T(8,128)(2,1)S(1)}, bf16[104,16,128]{2,1,0:T(8,128)(2,1)S(1)}, u32[]{:S(2)}, u32[]{:S(2)}) collective-permute-start(bf16[104,16,128]{2,1,0:T(8,128)(2,1)S(1)} %get-tuple-element.61), channel_id=1, source_target_pairs={{0,1},{1,0},{2,3},{3,2},{4,5},{5,4},{6,7},{7,6},{8,9},{9,8},{10,11... | collective-permute-start | bytes 1277960 | tf_op jit(solution)/shard_map/ppermute | solution.py:202
  106.5 2.0 %collective-permute-start.39 = (bf16[48,16,128]{2,1,0:T(8,128)(2,1)S(1)}, bf16[48,16,128]{2,1,0:T(8,128)(2,1)S(1)}, u32[]{:S(2)}, u32[]{:S(2)}) collective-permute-start(bf16[48,16,128]{2,1,0:T(8,128)(2,1)S(1)} %collective-permute-done.37.refs_16_), channel_id=1, source_target_pairs={{0,1},{1,0},{2,3},{3,2},{4,5},{5,4},{6,7},{7,6},{8,9},{9,8},{10,11... | collective-permute-start | bytes 589832 | tf_op jit(solution)/shard_map/ppermute | solution.py:202
  107.0 1.8 %collective-permute-start.38 = (bf16[48,16,128]{2,1,0:T(8,128)(2,1)S(1)}, bf16[48,16,128]{2,1,0:T(8,128)(2,1)S(1)}, u32[]{:S(2)}, u32[]{:S(2)}) collective-permute-start(bf16[48,16,128]{2,1,0:T(8,128)(2,1)S(1)} %pad_maximum_fusion.1.refs_15_), channel_id=1, source_target_pairs={{0,1},{1,0},{2,3},{3,2},{4,5},{5,4},{6,7},{7,6},{8,9},{9,8},{10,11... | collective-permute-start | bytes 589832 | tf_op jit(solution)/shard_map/ppermute | solution.py:202
  (12 other events, 216.0 us)

commit v4 on v2

--- a/solution.py
+++ b/solution.py
@@ -179,8 +179,8 @@
     z2, z3, z1 = swap(piece, 16), swap(piece, 24), swap(piece, 8)
     low, high, full = pack_pieces(near, z1, z2, z3)
     x_low, y_high = swap(low, 2), swap(high, 4)
+    d_low, d_high = swap(x_low, 4), swap(y_high, 2)
     x_high, y_low = swap(high, 2), swap(low, 4)
-    d_low, d_high = swap(x_low, 4), swap(y_high, 2)
     other = swap(full, 1)
     mine = [(low, high), (x_low, x_high), (y_low, y_high), (d_low, d_high)]
     theirs = [(swap(a, 1), swap(b, 1)) for a, b in mine[1:]]
@@ -228,7 +228,8 @@
 
 
 def multiply(refs, weight, total, weight_kv=None, total_kv=None):
-    low, high = refs[0:8], refs[8:16]
+    placed = [refs[ORDER.index(at)] for at in range(16)]
+    low, high = placed[0:8], placed[8:16]
     total[...] = jnp.zeros_like(total)
     if weight_kv is not None:
         total_kv[...] = jnp.zeros_like(total_kv)
@@ -306,12 +307,15 @@
     out[...] = jnp.dot(chosen, rounded, preferred_element_type=jnp.float32).astype(jnp.bfloat16)
 
 
+ORDER = (3, 11, 7, 15, 0, 1, 8, 10, 2, 9, 4, 5, 6, 12, 13, 14)
+
+
 def gathered_operands(gathered):
     mine, other, theirs = gathered
     operands = []
     for half in range(2):
         operands += [pair[half] for pair in mine] + [other] + [pair[half] for pair in theirs]
-    return operands
+    return [operands[at] for at in ORDER]
 
 
 def project(kernel, gathered, weights, session_ids, out_shape, scratch):
@@ -399,8 +403,9 @@
         total = jnp.sum(cached_exp, axis=-1, keepdims=True) + jnp.sum(
             own_exp, axis=-1, keepdims=True
         )
-        weights = (cached_exp / total).astype(jnp.bfloat16)
-        own_weights = (own_exp / total).astype(jnp.bfloat16)
+        share = 1.0 / total
+        weights = (cached_exp * share).astype(jnp.bfloat16)
+        own_weights = (own_exp * share).astype(jnp.bfloat16)
         attended = jnp.dot(weights, group_values, preferred_element_type=jnp.float32)
         attended += jnp.dot(own_weights, own_value, preferred_element_type=jnp.float32)
         out[group * rows : (group + 1) * rows, :] = attended.astype(jnp.bfloat16)

time: 108 us -> 103 us (0.954)
  waiting for transfers between devices: 41.9 us -> 33.6 us
  starting transfers between devices: 24.3 us -> 26.3 us
    ppermute x32, waiting for transfers between devices: 41.9 us -> 33.6 us  [swapped(): return lax.ppermute(array, 'wide', [(i, i ^ mask) for i in range(devices)])]
    ppermute x32, starting transfers between devices: 24.3 us -> 26.3 us  [swapped(): return lax.ppermute(array, 'wide', [(i, i ^ mask) for i in range(devices)])]
  transfers between devices with their start and end apart: 32 -> 32, of which waited for: 14 -> 18; matrix products, arithmetic and copies ran while one was open for 0% -> 0% of each run, Pallas kernels for 12% -> 13%
where the time goes in v4:
time: 103 us; the launch traced here: 102 us
  waiting for transfers between devices  33.6 us (33%)
  Pallas kernels  27 us (26%)
  starting transfers between devices  26.3 us (26%)
  blocking collectives  15.1 us (15%)
    ppermute x32, waiting for transfers between devices, swapped(): return lax.ppermute(array, 'wide', [(i, i ^ mask) for i in range(devices)])  33.6 us
    ppermute x32, starting transfers between devices, swapped(): return lax.ppermute(array, 'wide', [(i, i ^ mask) for i in range(devices)])  26.3 us
    all_to_all x1, blocking collectives, on_block(): lax.all_to_all(local, 'wide', split_axis=0, concat_axis=0, tiled=True)  15.1 us
    pallas_call x2, Pallas kernels, prefetch(): pl.pallas_call(prefetch_kernel, in_specs=[pl.BlockSpec(memory_space=pltpu...  12.8 us
    pallas_call x2, Pallas kernels, project(): pl.pallas_call(kernel, in_specs=[whole] * len(operands), out_specs=whole,...  9.74 us
    pallas_call x1, Pallas kernels, attend(): pl.pallas_call(attend_kernel, in_specs=[whole] * 3 + [pl.BlockSpec(memory...  3.67 us
  transfers between devices with their start and end apart: 32, of which 18 were waited for; matrix products, arithmetic and copies ran while one was open for 0% of the time, Pallas kernels for 13%

profile of v4, /device:TPU:0, one launch (start us, length us, event | category | flops | bytes accessed | tf_op | source)
XLA Modules:
  0.0 102.2 jit_solution(10596862346719074703)
XLA Ops:
  0.0 3.0 %collective-permute-start = (bf16[4,16384]{1,0:T(4,128)(2,1)}, bf16[4,16384]{1,0:T(4,128)(2,1)S(1)}, u32[]{:S(2)}, u32[]{:S(2)}) collective-permute-start(bf16[4,16384]{1,0:T(4,128)(2,1)} %refs_0_.2), channel_id=1, source_target_pairs={{0,8},{1,9},{2,10},{3,11},{4,12},{5,13},{6,14},{7,15},{8,0},{9,1},... | collective-permute-start | bytes 393224 | tf_op jit(solution)/shard_map/ppermute | solution.py:174
  3.0 2.6 %collective-permute-start.1 = (bf16[4,16384]{1,0:T(4,128)(2,1)}, bf16[4,16384]{1,0:T(4,128)(2,1)S(1)}, u32[]{:S(2)}, u32[]{:S(2)}) collective-permute-start(bf16[4,16384]{1,0:T(4,128)(2,1)} %refs_0_.2), channel_id=1, source_target_pairs={{0,16},{1,17},{2,18},{3,19},{4,20},{5,21},{6,22},{7,23},{8,24},{9,... | collective-permute-start | bytes 393224 | tf_op jit(solution)/shard_map/ppermute | solution.py:174
  5.6 7.1 %shard_map.91 = (bf16[4,16384]{1,0:T(4,128)(2,1)S(1)}, f32[16384]{0:T(1024)S(1)}, bf16[16384,512]{1,0:T(8,128)(2,1)S(1)}, bf16[64,16384]{1,0:T(8,128)(2,1)S(1)},...) custom-call(bf16[4,16384]{1,0:T(4,128)(2,1)} %refs_0_.2, f32[16384]{0:T(1024)} %refs_1_.1, ...), custom_call_target="tpu_custom_call" | custom-call | bytes 21168128 | tf_op jit(solution)/shard_map/pallas_call | solution.py:203
  12.7 3.5 %collective-permute-done.1.z2 = bf16[4,16384]{1,0:T(4,128)(2,1)S(1)} collective-permute-done((bf16[4,16384]{1,0:T(4,128)(2,1)}, bf16[4,16384]{1,0:T(4,128)(2,1)S(1)}, u32[]{:S(2)}, u32[]{:S(2)}) %collective-permute-start.1) | collective-permute-done | bytes 131104 | tf_op jit(solution)/shard_map/ppermute | solution.py:174
  16.2 0.6 shard_map.92
  16.8 1.6 %collective-permute-start.3 = (bf16[64,16,128]{2,1,0:T(8,128)(2,1)S(1)}, bf16[64,16,128]{2,1,0:T(8,128)(2,1)S(1)}, u32[]{:S(2)}, u32[]{:S(2)}) collective-permute-start(bf16[64,16,128]{2,1,0:T(8,128)(2,1)S(1)} %get-tuple-element.21.refs_4_), channel_id=1, source_target_pairs={{0,2},{1,3},{2,0},{3,1},{4,6},{5,7},{6,4},{7,5},{8,10},{9,11},{10,... | collective-permute-start | bytes 786440 | tf_op jit(solution)/shard_map/ppermute | solution.py:174
  18.4 1.5 %collective-permute-start.5 = (bf16[64,16,128]{2,1,0:T(8,128)(2,1)S(1)}, bf16[64,16,128]{2,1,0:T(8,128)(2,1)S(1)}, u32[]{:S(2)}, u32[]{:S(2)}) collective-permute-start(bf16[64,16,128]{2,1,0:T(8,128)(2,1)S(1)} %get-tuple-element.22.refs_6_), channel_id=1, source_target_pairs={{0,4},{1,5},{2,6},{3,7},{4,0},{5,1},{6,2},{7,3},{8,12},{9,13},{10,... | collective-permute-start | bytes 786440 | tf_op jit(solution)/shard_map/ppermute | solution.py:174
  20.4 0.5 collective-permute-start.10
  20.9 2.3 %collective-permute-done.3.refs_5_ = bf16[64,16,128]{2,1,0:T(8,128)(2,1)S(1)} collective-permute-done((bf16[64,16,128]{2,1,0:T(8,128)(2,1)S(1)}, bf16[64,16,128]{2,1,0:T(8,128)(2,1)S(1)}, u32[]{:S(2)}, u32[]{:S(2)}) %collective-permute-start.3) | collective-permute-done | bytes 262176 | tf_op jit(solution)/shard_map/ppermute | solution.py:174
  23.2 1.5 %collective-permute-start.4 = (bf16[64,16,128]{2,1,0:T(8,128)(2,1)S(1)}, bf16[64,16,128]{2,1,0:T(8,128)(2,1)S(1)}, u32[]{:S(2)}, u32[]{:S(2)}) collective-permute-start(bf16[64,16,128]{2,1,0:T(8,128)(2,1)S(1)} %collective-permute-done.3.refs_5_), channel_id=1, source_target_pairs={{0,4},{1,5},{2,6},{3,7},{4,0},{5,1},{6,2},{7,3},{8,12},{9,13},{10,... | collective-permute-start | bytes 786440 | tf_op jit(solution)/shard_map/ppermute | solution.py:174
  24.8 1.8 %collective-permute-done.5.refs_7_ = bf16[64,16,128]{2,1,0:T(8,128)(2,1)S(1)} collective-permute-done((bf16[64,16,128]{2,1,0:T(8,128)(2,1)S(1)}, bf16[64,16,128]{2,1,0:T(8,128)(2,1)S(1)}, u32[]{:S(2)}, u32[]{:S(2)}) %collective-permute-start.5) | collective-permute-done | bytes 262176 | tf_op jit(solution)/shard_map/ppermute | solution.py:174
  26.5 0.6 collective-permute-start.6
  27.2 5.0 %collective-permute-done.9.refs_8_ = bf16[64,16,128]{2,1,0:T(8,128)(2,1)S(1)} collective-permute-done((bf16[64,16,128]{2,1,0:T(8,128)(2,1)S(1)}, bf16[64,16,128]{2,1,0:T(8,128)(2,1)S(1)}, u32[]{:S(2)}, u32[]{:S(2)}) %collective-permute-start.9) | collective-permute-done | bytes 262176 | tf_op jit(solution)/shard_map/ppermute | solution.py:174
  32.7 3.3 %collective-permute-done.4.refs_0_ = bf16[64,16,128]{2,1,0:T(8,128)(2,1)S(1)} collective-permute-done((bf16[64,16,128]{2,1,0:T(8,128)(2,1)S(1)}, bf16[64,16,128]{2,1,0:T(8,128)(2,1)S(1)}, u32[]{:S(2)}, u32[]{:S(2)}) %collective-permute-start.4) | collective-permute-done | bytes 262176 | tf_op jit(solution)/shard_map/ppermute | solution.py:174
  38.6 5.3 %shard_map.93 = bf16[32,32,128]{2,1,0:T(8,128)(2,1)S(1)} custom-call(bf16[64,16,128]{2,1,0:T(8,128)(2,1)S(1)} %collective-permute-done.4.refs_0_, bf16[64,16,128]{2,1,0:T(8,128)(2,1)S(1)} %collective-permute-done.6.refs_1_, bf16[64,16,128]{2,1,0:T(8,128)(2,1)S(1)} %collective-permute-done.7.refs_2_, bf16[64,16,128]{2,1,0:T(8,128)(2,1)S(1)} %collective-permute-done.8.refs_3_, ...), custom_call_target="tpu_custom_call" | custom-call | flops 2415919104 | bytes 23068672 | tf_op jit(solution)/shard_map/pallas_call | solution.py:327
  43.9 15.1 %all_to_all.5.received = bf16[32,32,128]{2,1,0:T(8,128)(2,1)S(1)} all-to-all(bf16[32,32,128]{2,1,0:T(8,128)(2,1)S(1)} %shard_map.93), channel_id=1, replica_groups=mesh['groups'=1,'wide'=32] {'wide'}, dimensions={0} | all-to-all | bytes 524288 | tf_op jit(solution)/shard_map/all_to_all | solution.py:449
  59.0 3.7 %shard_map.94.refs_1_ = bf16[512,128]{1,0:T(8,128)(2,1)S(1)} custom-call(bf16[32,32,128]{2,1,0:T(8,128)(2,1)S(1)} %all_to_all.5.received, bf16[4,8,128,128]{3,2,1,0:T(8,128)(2,1)S(1)} %get-tuple-element.26.keys, bf16[4,8,128,128]{3,2,1,0:T(8,128)(2,1)S(1)} %get-tuple-element.27.values, s32[4]{0:T(128)S(1)} %copy-done.1), custom_call_target="tpu_custom_call" | custom-call | flops 150000000 | bytes 3000000 | tf_op jit(solution)/shard_map/pallas_call | solution.py:417
  62.7 1.0 collective-permute-start.16
  63.7 1.0 collective-permute-start.17
  64.7 2.5 %collective-permute-start.18 = (bf16[512,128]{1,0:T(8,128)(2,1)S(1)}, bf16[512,128]{1,0:T(8,128)(2,1)S(1)}, u32[]{:S(2)}, u32[]{:S(2)}) collective-permute-start(bf16[512,128]{1,0:T(8,128)(2,1)S(1)} %shard_map.94.refs_1_), channel_id=1, source_target_pairs={{0,24},{1,25},{2,26},{3,27},{4,28},{5,29},{6,30},{7,31},{8,16},{9,... | collective-permute-start | bytes 393224 | tf_op jit(solution)/shard_map/ppermute | solution.py:174
  67.2 5.8 %shard_map.95 = (bf16[16384,512]{1,0:T(8,128)(2,1)S(1)}, bf16[512,128]{1,0:T(8,128)(2,1)S(1)}) custom-call(bf16[16384,512]{1,0:T(8,128)(2,1)} %refs_0_.3, bf16[512,128]{1,0:T(8,128)(2,1)S(1)} %shard_map.94.refs_1_), custom_call_target="tpu_custom_call" | custom-call | bytes 16908288 | tf_op jit(solution)/shard_map/pallas_call | solution.py:203
  73.0 3.2 %collective-permute-done.17.z2 = bf16[512,128]{1,0:T(8,128)(2,1)S(1)} collective-permute-done((bf16[512,128]{1,0:T(8,128)(2,1)S(1)}, bf16[512,128]{1,0:T(8,128)(2,1)S(1)}, u32[]{:S(2)}, u32[]{:S(2)}) %collective-permute-start.17) | collective-permute-done | bytes 131104 | tf_op jit(solution)/shard_map/ppermute | solution.py:174
  76.4 1.4 %collective-permute-start.21 = (bf16[64,16,128]{2,1,0:T(8,128)(2,1)S(1)}, bf16[64,16,128]{2,1,0:T(8,128)(2,1)S(1)}, u32[]{:S(2)}, u32[]{:S(2)}) collective-permute-start(bf16[64,16,128]{2,1,0:T(8,128)(2,1)S(1)} %get-tuple-element.30.refs_6_), channel_id=1, source_target_pairs={{0,4},{1,5},{2,6},{3,7},{4,0},{5,1},{6,2},{7,3},{8,12},{9,13},{10,... | collective-permute-start | bytes 786440 | tf_op jit(solution)/shard_map/ppermute | solution.py:174
  77.8 0.6 collective-permute-start.25
  78.4 1.9 %collective-permute-start.26 = (bf16[64,16,128]{2,1,0:T(8,128)(2,1)S(1)}, bf16[64,16,128]{2,1,0:T(8,128)(2,1)S(1)}, u32[]{:S(2)}, u32[]{:S(2)}) collective-permute-start(bf16[64,16,128]{2,1,0:T(8,128)(2,1)S(1)} %get-tuple-element.30.refs_6_), channel_id=1, source_target_pairs={{0,2},{1,3},{2,0},{3,1},{4,6},{5,7},{6,4},{7,5},{8,10},{9,11},{10,... | collective-permute-start | bytes 786440 | tf_op jit(solution)/shard_map/ppermute | solution.py:174
  80.4 3.5 %collective-permute-done.19.refs_5_ = bf16[64,16,128]{2,1,0:T(8,128)(2,1)S(1)} collective-permute-done((bf16[64,16,128]{2,1,0:T(8,128)(2,1)S(1)}, bf16[64,16,128]{2,1,0:T(8,128)(2,1)S(1)}, u32[]{:S(2)}, u32[]{:S(2)}) %collective-permute-start.19) | collective-permute-done | bytes 262176 | tf_op jit(solution)/shard_map/ppermute | solution.py:174
  83.9 0.9 collective-permute-start.20
  84.8 0.9 collective-permute-done.21.refs_7_
  85.7 1.9 %collective-permute-start.22 = (bf16[64,16,128]{2,1,0:T(8,128)(2,1)S(1)}, bf16[64,16,128]{2,1,0:T(8,128)(2,1)S(1)}, u32[]{:S(2)}, u32[]{:S(2)}) collective-permute-start(bf16[64,16,128]{2,1,0:T(8,128)(2,1)S(1)} %collective-permute-done.21.refs_7_), channel_id=1, source_target_pairs={{0,2},{1,3},{2,0},{3,1},{4,6},{5,7},{6,4},{7,5},{8,10},{9,11},{10,... | collective-permute-start | bytes 786440 | tf_op jit(solution)/shard_map/ppermute | solution.py:174
  87.5 3.7 %collective-permute-done.25.refs_8_ = bf16[64,16,128]{2,1,0:T(8,128)(2,1)S(1)} collective-permute-done((bf16[64,16,128]{2,1,0:T(8,128)(2,1)S(1)}, bf16[64,16,128]{2,1,0:T(8,128)(2,1)S(1)}, u32[]{:S(2)}, u32[]{:S(2)}) %collective-permute-start.25) | collective-permute-done | bytes 262176 | tf_op jit(solution)/shard_map/ppermute | solution.py:174
  91.8 3.2 %collective-permute-done.20.refs_0_ = bf16[64,16,128]{2,1,0:T(8,128)(2,1)S(1)} collective-permute-done((bf16[64,16,128]{2,1,0:T(8,128)(2,1)S(1)}, bf16[64,16,128]{2,1,0:T(8,128)(2,1)S(1)}, u32[]{:S(2)}, u32[]{:S(2)}) %collective-permute-start.20) | collective-permute-done | bytes 262176 | tf_op jit(solution)/shard_map/ppermute | solution.py:174
  97.7 4.5 %shard_map.97 = bf16[128,512]{1,0:T(8,128)(2,1)} custom-call(bf16[64,16,128]{2,1,0:T(8,128)(2,1)S(1)} %collective-permute-done.20.refs_0_, bf16[64,16,128]{2,1,0:T(8,128)(2,1)S(1)} %collective-permute-done.22.refs_1_, bf16[64,16,128]{2,1,0:T(8,128)(2,1)S(1)} %collective-permute-done.23.refs_2_, bf16[64,16,128]{2,1,0:T(8,128)(2,1)S(1)} %collective-permute-done.24.refs_3_, ...), custom_call_target="tpu_custom_call" | custom-call | flops 2147483648 | bytes 20971520 | tf_op jit(solution)/shard_map/pallas_call | solution.py:327
  (44 shorter events, 7.1 us)
Async XLA Ops:
  0.0 12.7 %collective-permute-start = (bf16[4,16384]{1,0:T(4,128)(2,1)}, bf16[4,16384]{1,0:T(4,128)(2,1)S(1)}, u32[]{:S(2)}, u32[]{:S(2)}) collective-permute-start(bf16[4,16384]{1,0:T(4,128)(2,1)} %refs_0_.2), channel_id=1, source_target_pairs={{0,8},{1,9},{2,10},{3,11},{4,12},{5,13},{6,14},{7,15},{8,0},{9,1},... | collective-permute-start | bytes 393224 | tf_op jit(solution)/shard_map/ppermute | solution.py:174
  3.0 13.2 %collective-permute-start.1 = (bf16[4,16384]{1,0:T(4,128)(2,1)}, bf16[4,16384]{1,0:T(4,128)(2,1)S(1)}, u32[]{:S(2)}, u32[]{:S(2)}) collective-permute-start(bf16[4,16384]{1,0:T(4,128)(2,1)} %refs_0_.2), channel_id=1, source_target_pairs={{0,16},{1,17},{2,18},{3,19},{4,20},{5,21},{6,22},{7,23},{8,24},{9,... | collective-permute-start | bytes 393224 | tf_op jit(solution)/shard_map/ppermute | solution.py:174
  5.6 10.6 %collective-permute-start.2 = (bf16[4,16384]{1,0:T(4,128)(2,1)}, bf16[4,16384]{1,0:T(4,128)(2,1)S(1)}, u32[]{:S(2)}, u32[]{:S(2)}) collective-permute-start(bf16[4,16384]{1,0:T(4,128)(2,1)} %refs_0_.2), channel_id=1, source_target_pairs={{0,24},{1,25},{2,26},{3,27},{4,28},{5,29},{6,30},{7,31},{8,16},{9,... | collective-permute-start | bytes 393224 | tf_op jit(solution)/shard_map/ppermute | solution.py:174
  16.8 6.4 %collective-permute-start.3 = (bf16[64,16,128]{2,1,0:T(8,128)(2,1)S(1)}, bf16[64,16,128]{2,1,0:T(8,128)(2,1)S(1)}, u32[]{:S(2)}, u32[]{:S(2)}) collective-permute-start(bf16[64,16,128]{2,1,0:T(8,128)(2,1)S(1)} %get-tuple-element.21.refs_4_), channel_id=1, source_target_pairs={{0,2},{1,3},{2,0},{3,1},{4,6},{5,7},{6,4},{7,5},{8,10},{9,11},{10,... | collective-permute-start | bytes 786440 | tf_op jit(solution)/shard_map/ppermute | solution.py:174
  18.4 8.2 %collective-permute-start.5 = (bf16[64,16,128]{2,1,0:T(8,128)(2,1)S(1)}, bf16[64,16,128]{2,1,0:T(8,128)(2,1)S(1)}, u32[]{:S(2)}, u32[]{:S(2)}) collective-permute-start(bf16[64,16,128]{2,1,0:T(8,128)(2,1)S(1)} %get-tuple-element.22.refs_6_), channel_id=1, source_target_pairs={{0,4},{1,5},{2,6},{3,7},{4,0},{5,1},{6,2},{7,3},{8,12},{9,13},{10,... | collective-permute-start | bytes 786440 | tf_op jit(solution)/shard_map/ppermute | solution.py:174
  19.9 16.6 %collective-permute-start.11 = (bf16[128,16,128]{2,1,0:T(8,128)(2,1)S(1)}, bf16[128,16,128]{2,1,0:T(8,128)(2,1)S(1)}, u32[]{:S(2)}, u32[]{:S(2)}) collective-permute-start(bf16[128,16,128]{2,1,0:T(8,128)(2,1)S(1)} %get-tuple-element.23), channel_id=1, source_target_pairs={{0,1},{1,0},{2,3},{3,2},{4,5},{5,4},{6,7},{7,6},{8,9},{9,8},{10,11... | collective-permute-start | bytes 1572872 | tf_op jit(solution)/shard_map/ppermute | solution.py:174
  19.9 12.3 %collective-permute-start.9 = (bf16[64,16,128]{2,1,0:T(8,128)(2,1)S(1)}, bf16[64,16,128]{2,1,0:T(8,128)(2,1)S(1)}, u32[]{:S(2)}, u32[]{:S(2)}) collective-permute-start(bf16[64,16,128]{2,1,0:T(8,128)(2,1)S(1)} %get-tuple-element.21.refs_4_), channel_id=1, source_target_pairs={{0,4},{1,5},{2,6},{3,7},{4,0},{5,1},{6,2},{7,3},{8,12},{9,13},{10,... | collective-permute-start | bytes 786440 | tf_op jit(solution)/shard_map/ppermute | solution.py:174
  20.4 11.8 %collective-permute-start.10 = (bf16[64,16,128]{2,1,0:T(8,128)(2,1)S(1)}, bf16[64,16,128]{2,1,0:T(8,128)(2,1)S(1)}, u32[]{:S(2)}, u32[]{:S(2)}) collective-permute-start(bf16[64,16,128]{2,1,0:T(8,128)(2,1)S(1)} %get-tuple-element.22.refs_6_), channel_id=1, source_target_pairs={{0,2},{1,3},{2,0},{3,1},{4,6},{5,7},{6,4},{7,5},{8,10},{9,11},{10,... | collective-permute-start | bytes 786440 | tf_op jit(solution)/shard_map/ppermute | solution.py:174
  23.2 12.7 %collective-permute-start.4 = (bf16[64,16,128]{2,1,0:T(8,128)(2,1)S(1)}, bf16[64,16,128]{2,1,0:T(8,128)(2,1)S(1)}, u32[]{:S(2)}, u32[]{:S(2)}) collective-permute-start(bf16[64,16,128]{2,1,0:T(8,128)(2,1)S(1)} %collective-permute-done.3.refs_5_), channel_id=1, source_target_pairs={{0,4},{1,5},{2,6},{3,7},{4,0},{5,1},{6,2},{7,3},{8,12},{9,13},{10,... | collective-permute-start | bytes 786440 | tf_op jit(solution)/shard_map/ppermute | solution.py:174
  26.5 9.4 %collective-permute-start.6 = (bf16[64,16,128]{2,1,0:T(8,128)(2,1)S(1)}, bf16[64,16,128]{2,1,0:T(8,128)(2,1)S(1)}, u32[]{:S(2)}, u32[]{:S(2)}) collective-permute-start(bf16[64,16,128]{2,1,0:T(8,128)(2,1)S(1)} %collective-permute-done.5.refs_7_), channel_id=1, source_target_pairs={{0,2},{1,3},{2,0},{3,1},{4,6},{5,7},{6,4},{7,5},{8,10},{9,11},{10,... | collective-permute-start | bytes 786440 | tf_op jit(solution)/shard_map/ppermute | solution.py:174
  32.1 4.4 %collective-permute-start.12 = (bf16[64,16,128]{2,1,0:T(8,128)(2,1)S(1)}, bf16[64,16,128]{2,1,0:T(8,128)(2,1)S(1)}, u32[]{:S(2)}, u32[]{:S(2)}) collective-permute-start(bf16[64,16,128]{2,1,0:T(8,128)(2,1)S(1)} %collective-permute-done.3.refs_5_), channel_id=1, source_target_pairs={{0,1},{1,0},{2,3},{3,2},{4,5},{5,4},{6,7},{7,6},{8,9},{9,8},{10,11... | collective-permute-start | bytes 786440 | tf_op jit(solution)/shard_map/ppermute | solution.py:174
  32.1 5.7 %collective-permute-start.15 = (bf16[64,16,128]{2,1,0:T(8,128)(2,1)S(1)}, bf16[64,16,128]{2,1,0:T(8,128)(2,1)S(1)}, u32[]{:S(2)}, u32[]{:S(2)}) collective-permute-start(bf16[64,16,128]{2,1,0:T(8,128)(2,1)S(1)} %collective-permute-done.5.refs_7_), channel_id=1, source_target_pairs={{0,1},{1,0},{2,3},{3,2},{4,5},{5,4},{6,7},{7,6},{8,9},{9,8},{10,11... | collective-permute-start | bytes 786440 | tf_op jit(solution)/shard_map/ppermute | solution.py:174
  36.0 1.5 %collective-permute-start.13 = (bf16[64,16,128]{2,1,0:T(8,128)(2,1)S(1)}, bf16[64,16,128]{2,1,0:T(8,128)(2,1)S(1)}, u32[]{:S(2)}, u32[]{:S(2)}) collective-permute-start(bf16[64,16,128]{2,1,0:T(8,128)(2,1)S(1)} %collective-permute-done.9.refs_8_), channel_id=1, source_target_pairs={{0,1},{1,0},{2,3},{3,2},{4,5},{5,4},{6,7},{7,6},{8,9},{9,8},{10,11... | collective-permute-start | bytes 786440 | tf_op jit(solution)/shard_map/ppermute | solution.py:174
  36.0 1.9 %collective-permute-start.14 = (bf16[64,16,128]{2,1,0:T(8,128)(2,1)S(1)}, bf16[64,16,128]{2,1,0:T(8,128)(2,1)S(1)}, u32[]{:S(2)}, u32[]{:S(2)}) collective-permute-start(bf16[64,16,128]{2,1,0:T(8,128)(2,1)S(1)} %collective-permute-done.10.refs_9_), channel_id=1, source_target_pairs={{0,1},{1,0},{2,3},{3,2},{4,5},{5,4},{6,7},{7,6},{8,9},{9,8},{10,11... | collective-permute-start | bytes 786440 | tf_op jit(solution)/shard_map/ppermute | solution.py:174
  36.5 1.8 %collective-permute-start.7 = (bf16[64,16,128]{2,1,0:T(8,128)(2,1)S(1)}, bf16[64,16,128]{2,1,0:T(8,128)(2,1)S(1)}, u32[]{:S(2)}, u32[]{:S(2)}) collective-permute-start(bf16[64,16,128]{2,1,0:T(8,128)(2,1)S(1)} %collective-permute-done.4.refs_0_), channel_id=1, source_target_pairs={{0,1},{1,0},{2,3},{3,2},{4,5},{5,4},{6,7},{7,6},{8,9},{9,8},{10,11... | collective-permute-start | bytes 786440 | tf_op jit(solution)/shard_map/ppermute | solution.py:174
  36.6 2.1 %collective-permute-start.8 = (bf16[64,16,128]{2,1,0:T(8,128)(2,1)S(1)}, bf16[64,16,128]{2,1,0:T(8,128)(2,1)S(1)}, u32[]{:S(2)}, u32[]{:S(2)}) collective-permute-start(bf16[64,16,128]{2,1,0:T(8,128)(2,1)S(1)} %collective-permute-done.6.refs_1_), channel_id=1, source_target_pairs={{0,1},{1,0},{2,3},{3,2},{4,5},{5,4},{6,7},{7,6},{8,9},{9,8},{10,11... | collective-permute-start | bytes 786440 | tf_op jit(solution)/shard_map/ppermute | solution.py:174
  62.7 10.3 %collective-permute-start.16 = (bf16[512,128]{1,0:T(8,128)(2,1)S(1)}, bf16[512,128]{1,0:T(8,128)(2,1)S(1)}, u32[]{:S(2)}, u32[]{:S(2)}) collective-permute-start(bf16[512,128]{1,0:T(8,128)(2,1)S(1)} %shard_map.94.refs_1_), channel_id=1, source_target_pairs={{0,8},{1,9},{2,10},{3,11},{4,12},{5,13},{6,14},{7,15},{8,0},{9,1},... | collective-permute-start | bytes 393224 | tf_op jit(solution)/shard_map/ppermute | solution.py:174
  63.7 12.4 %collective-permute-start.17 = (bf16[512,128]{1,0:T(8,128)(2,1)S(1)}, bf16[512,128]{1,0:T(8,128)(2,1)S(1)}, u32[]{:S(2)}, u32[]{:S(2)}) collective-permute-start(bf16[512,128]{1,0:T(8,128)(2,1)S(1)} %shard_map.94.refs_1_), channel_id=1, source_target_pairs={{0,16},{1,17},{2,18},{3,19},{4,20},{5,21},{6,22},{7,23},{8,24},{9,... | collective-permute-start | bytes 393224 | tf_op jit(solution)/shard_map/ppermute | solution.py:174
  64.7 11.5 %collective-permute-start.18 = (bf16[512,128]{1,0:T(8,128)(2,1)S(1)}, bf16[512,128]{1,0:T(8,128)(2,1)S(1)}, u32[]{:S(2)}, u32[]{:S(2)}) collective-permute-start(bf16[512,128]{1,0:T(8,128)(2,1)S(1)} %shard_map.94.refs_1_), channel_id=1, source_target_pairs={{0,24},{1,25},{2,26},{3,27},{4,28},{5,29},{6,30},{7,31},{8,16},{9,... | collective-permute-start | bytes 393224 | tf_op jit(solution)/shard_map/ppermute | solution.py:174
  76.3 7.6 %collective-permute-start.19 = (bf16[64,16,128]{2,1,0:T(8,128)(2,1)S(1)}, bf16[64,16,128]{2,1,0:T(8,128)(2,1)S(1)}, u32[]{:S(2)}, u32[]{:S(2)}) collective-permute-start(bf16[64,16,128]{2,1,0:T(8,128)(2,1)S(1)} %get-tuple-element.29.refs_4_), channel_id=1, source_target_pairs={{0,2},{1,3},{2,0},{3,1},{4,6},{5,7},{6,4},{7,5},{8,10},{9,11},{10,... | collective-permute-start | bytes 786440 | tf_op jit(solution)/shard_map/ppermute | solution.py:174
  76.4 9.2 %collective-permute-start.21 = (bf16[64,16,128]{2,1,0:T(8,128)(2,1)S(1)}, bf16[64,16,128]{2,1,0:T(8,128)(2,1)S(1)}, u32[]{:S(2)}, u32[]{:S(2)}) collective-permute-start(bf16[64,16,128]{2,1,0:T(8,128)(2,1)S(1)} %get-tuple-element.30.refs_6_), channel_id=1, source_target_pairs={{0,4},{1,5},{2,6},{3,7},{4,0},{5,1},{6,2},{7,3},{8,12},{9,13},{10,... | collective-permute-start | bytes 786440 | tf_op jit(solution)/shard_map/ppermute | solution.py:174
  77.8 17.7 %collective-permute-start.27 = (bf16[128,16,128]{2,1,0:T(8,128)(2,1)S(1)}, bf16[128,16,128]{2,1,0:T(8,128)(2,1)S(1)}, u32[]{:S(2)}, u32[]{:S(2)}) collective-permute-start(bf16[128,16,128]{2,1,0:T(8,128)(2,1)S(1)} %get-tuple-element.31), channel_id=1, source_target_pairs={{0,1},{1,0},{2,3},{3,2},{4,5},{5,4},{6,7},{7,6},{8,9},{9,8},{10,11... | collective-permute-start | bytes 1572872 | tf_op jit(solution)/shard_map/ppermute | solution.py:174
  77.8 13.4 %collective-permute-start.25 = (bf16[64,16,128]{2,1,0:T(8,128)(2,1)S(1)}, bf16[64,16,128]{2,1,0:T(8,128)(2,1)S(1)}, u32[]{:S(2)}, u32[]{:S(2)}) collective-permute-start(bf16[64,16,128]{2,1,0:T(8,128)(2,1)S(1)} %get-tuple-element.29.refs_4_), channel_id=1, source_target_pairs={{0,4},{1,5},{2,6},{3,7},{4,0},{5,1},{6,2},{7,3},{8,12},{9,13},{10,... | collective-permute-start | bytes 786440 | tf_op jit(solution)/shard_map/ppermute | solution.py:174
  78.4 12.8 %collective-permute-start.26 = (bf16[64,16,128]{2,1,0:T(8,128)(2,1)S(1)}, bf16[64,16,128]{2,1,0:T(8,128)(2,1)S(1)}, u32[]{:S(2)}, u32[]{:S(2)}) collective-permute-start(bf16[64,16,128]{2,1,0:T(8,128)(2,1)S(1)} %get-tuple-element.30.refs_6_), channel_id=1, source_target_pairs={{0,2},{1,3},{2,0},{3,1},{4,6},{5,7},{6,4},{7,5},{8,10},{9,11},{10,... | collective-permute-start | bytes 786440 | tf_op jit(solution)/shard_map/ppermute | solution.py:174
  83.9 11.2 %collective-permute-start.20 = (bf16[64,16,128]{2,1,0:T(8,128)(2,1)S(1)}, bf16[64,16,128]{2,1,0:T(8,128)(2,1)S(1)}, u32[]{:S(2)}, u32[]{:S(2)}) collective-permute-start(bf16[64,16,128]{2,1,0:T(8,128)(2,1)S(1)} %collective-permute-done.19.refs_5_), channel_id=1, source_target_pairs={{0,4},{1,5},{2,6},{3,7},{4,0},{5,1},{6,2},{7,3},{8,12},{9,13},{10,... | collective-permute-start | bytes 786440 | tf_op jit(solution)/shard_map/ppermute | solution.py:174
  85.7 9.4 %collective-permute-start.22 = (bf16[64,16,128]{2,1,0:T(8,128)(2,1)S(1)}, bf16[64,16,128]{2,1,0:T(8,128)(2,1)S(1)}, u32[]{:S(2)}, u32[]{:S(2)}) collective-permute-start(bf16[64,16,128]{2,1,0:T(8,128)(2,1)S(1)} %collective-permute-done.21.refs_7_), channel_id=1, source_target_pairs={{0,2},{1,3},{2,0},{3,1},{4,6},{5,7},{6,4},{7,5},{8,10},{9,11},{10,... | collective-permute-start | bytes 786440 | tf_op jit(solution)/shard_map/ppermute | solution.py:174
  91.3 4.3 %collective-permute-start.28 = (bf16[64,16,128]{2,1,0:T(8,128)(2,1)S(1)}, bf16[64,16,128]{2,1,0:T(8,128)(2,1)S(1)}, u32[]{:S(2)}, u32[]{:S(2)}) collective-permute-start(bf16[64,16,128]{2,1,0:T(8,128)(2,1)S(1)} %collective-permute-done.19.refs_5_), channel_id=1, source_target_pairs={{0,1},{1,0},{2,3},{3,2},{4,5},{5,4},{6,7},{7,6},{8,9},{9,8},{10,11... | collective-permute-start | bytes 786440 | tf_op jit(solution)/shard_map/ppermute | solution.py:174
  91.3 5.7 %collective-permute-start.31 = (bf16[64,16,128]{2,1,0:T(8,128)(2,1)S(1)}, bf16[64,16,128]{2,1,0:T(8,128)(2,1)S(1)}, u32[]{:S(2)}, u32[]{:S(2)}) collective-permute-start(bf16[64,16,128]{2,1,0:T(8,128)(2,1)S(1)} %collective-permute-done.21.refs_7_), channel_id=1, source_target_pairs={{0,1},{1,0},{2,3},{3,2},{4,5},{5,4},{6,7},{7,6},{8,9},{9,8},{10,11... | collective-permute-start | bytes 786440 | tf_op jit(solution)/shard_map/ppermute | solution.py:174
  95.0 1.5 %collective-permute-start.29 = (bf16[64,16,128]{2,1,0:T(8,128)(2,1)S(1)}, bf16[64,16,128]{2,1,0:T(8,128)(2,1)S(1)}, u32[]{:S(2)}, u32[]{:S(2)}) collective-permute-start(bf16[64,16,128]{2,1,0:T(8,128)(2,1)S(1)} %collective-permute-done.25.refs_8_), channel_id=1, source_target_pairs={{0,1},{1,0},{2,3},{3,2},{4,5},{5,4},{6,7},{7,6},{8,9},{9,8},{10,11... | collective-permute-start | bytes 786440 | tf_op jit(solution)/shard_map/ppermute | solution.py:174
  95.0 1.9 %collective-permute-start.30 = (bf16[64,16,128]{2,1,0:T(8,128)(2,1)S(1)}, bf16[64,16,128]{2,1,0:T(8,128)(2,1)S(1)}, u32[]{:S(2)}, u32[]{:S(2)}) collective-permute-start(bf16[64,16,128]{2,1,0:T(8,128)(2,1)S(1)} %collective-permute-done.26.refs_9_), channel_id=1, source_target_pairs={{0,1},{1,0},{2,3},{3,2},{4,5},{5,4},{6,7},{7,6},{8,9},{9,8},{10,11... | collective-permute-start | bytes 786440 | tf_op jit(solution)/shard_map/ppermute | solution.py:174
  95.5 1.8 %collective-permute-start.23 = (bf16[64,16,128]{2,1,0:T(8,128)(2,1)S(1)}, bf16[64,16,128]{2,1,0:T(8,128)(2,1)S(1)}, u32[]{:S(2)}, u32[]{:S(2)}) collective-permute-start(bf16[64,16,128]{2,1,0:T(8,128)(2,1)S(1)} %collective-permute-done.20.refs_0_), channel_id=1, source_target_pairs={{0,1},{1,0},{2,3},{3,2},{4,5},{5,4},{6,7},{7,6},{8,9},{9,8},{10,11... | collective-permute-start | bytes 786440 | tf_op jit(solution)/shard_map/ppermute | solution.py:174
  95.6 2.1 %collective-permute-start.24 = (bf16[64,16,128]{2,1,0:T(8,128)(2,1)S(1)}, bf16[64,16,128]{2,1,0:T(8,128)(2,1)S(1)}, u32[]{:S(2)}, u32[]{:S(2)}) collective-permute-start(bf16[64,16,128]{2,1,0:T(8,128)(2,1)S(1)} %collective-permute-done.22.refs_1_), channel_id=1, source_target_pairs={{0,1},{1,0},{2,3},{3,2},{4,5},{5,4},{6,7},{7,6},{8,9},{9,8},{10,11... | collective-permute-start | bytes 786440 | tf_op jit(solution)/shard_map/ppermute | solution.py:174
  (2 other events, 85.0 us)

commit v5 on v4

--- a/solution.py
+++ b/solution.py
@@ -17,6 +17,7 @@
 LANES = 128
 PIECE = 4
 TILE = 16
+EXTRA = 8
 MIB = 1 << 20
 
 
@@ -224,7 +225,7 @@
     return (me ^ (core + 2 * plane + 8 * column)) * PIECE + at % PIECE
 
 
-COUNT = 16
+COUNT = 64
 
 
 def multiply(refs, weight, total, weight_kv=None, total_kv=None):
@@ -286,15 +287,15 @@
     query = jnp.dot(one_hot(wanted == codes), stacked, preferred_element_type=jnp.float32)
     out[:, 0:TILE, :] = query.astype(jnp.bfloat16).reshape(devices, TILE, LANES)
     columns = total_kv.shape[1]
-    at = lax.broadcasted_iota(jnp.int32, (devices * TILE, rows), 0)
-    wanted = jnp.where(at % TILE < PIECE, (at // TILE) * PIECE + at % TILE, -1)
+    at = lax.broadcasted_iota(jnp.int32, (devices * EXTRA, rows), 0)
+    wanted = jnp.where(at % EXTRA < PIECE, (at // EXTRA) * PIECE + at % EXTRA, -1)
     keyval = total_kv[...].astype(jnp.bfloat16)
     ordered = jnp.dot(one_hot(wanted == session), keyval, preferred_element_type=jnp.float32)
     here = lax.broadcasted_iota(jnp.int32, (columns, LANES), 0)
     there = lax.broadcasted_iota(jnp.int32, (columns, LANES), 1)
     place = one_hot(there == here + (me % 2) * columns)
     placed = jnp.dot(ordered.astype(jnp.bfloat16), place, preferred_element_type=jnp.float32)
-    out[:, TILE : 2 * TILE, :] = placed.astype(jnp.bfloat16).reshape(devices, TILE, LANES)
+    out[:, TILE : TILE + EXTRA, :] = placed.astype(jnp.bfloat16).reshape(devices, EXTRA, LANES)
 
 
 def out_kernel(*refs):
@@ -367,12 +368,11 @@
     def rotate(vectors):
         return (vectors * cosine + pltpu.roll(vectors, halfway, 1) * sine).astype(jnp.bfloat16)
 
-    own = received[:, TILE : 2 * TILE, :].astype(jnp.float32)
+    own = received[:, TILE : TILE + EXTRA, :].astype(jnp.float32)
     pairs = devices // 2
-    own = own.reshape(pairs, 2, TILE, width)
+    own = own.reshape(pairs, 2, EXTRA, width)
     own = own[:, 0] + own[:, 1]
-    own = own[:, 0:8]
-    own_rows = kv_heads * 8
+    own_rows = kv_heads * EXTRA
     own_key = rotate(own[0:kv_heads].reshape(own_rows, width))
     own_value = own[kv_heads:].reshape(own_rows, width).astype(jnp.bfloat16)
 
@@ -381,34 +381,59 @@
     valid = (column // cache_len == session) & (column % cache_len < limits)
     own_session = lax.broadcasted_iota(jnp.int32, (rows, own_rows), 0) % PIECE
     own_column = lax.broadcasted_iota(jnp.int32, (rows, own_rows), 1)
-    for group in range(kv_heads):
-        query = received[group * per_group : (group + 1) * per_group, 0:TILE, :]
-        query = rotate(query.reshape(rows, width).astype(jnp.float32))
-        group_keys = keys[:, group].reshape(sessions * cache_len, width)
-        group_values = values[:, group].reshape(sessions * cache_len, width)
-        contract = (((1,), (1,)), ((), ()))
-        scores = (
-            lax.dot_general(query, group_keys, contract, preferred_element_type=jnp.float32) * scale
-        )
-        scores = jnp.where(valid, scores, -jnp.inf)
-        own_scores = (
-            lax.dot_general(query, own_key, contract, preferred_element_type=jnp.float32) * scale
-        )
-        own_scores = jnp.where(own_column == group * 8 + own_session, own_scores, -jnp.inf)
-        highest = jnp.maximum(
-            jnp.max(scores, axis=-1, keepdims=True), jnp.max(own_scores, axis=-1, keepdims=True)
-        )
-        cached_exp = jnp.exp(scores - highest)
-        own_exp = jnp.exp(own_scores - highest)
-        total = jnp.sum(cached_exp, axis=-1, keepdims=True) + jnp.sum(
-            own_exp, axis=-1, keepdims=True
-        )
-        share = 1.0 / total
-        weights = (cached_exp * share).astype(jnp.bfloat16)
-        own_weights = (own_exp * share).astype(jnp.bfloat16)
-        attended = jnp.dot(weights, group_values, preferred_element_type=jnp.float32)
-        attended += jnp.dot(own_weights, own_value, preferred_element_type=jnp.float32)
-        out[group * rows : (group + 1) * rows, :] = attended.astype(jnp.bfloat16)
+    contract = (((1,), (1,)), ((), ()))
+    for first in range(0, kv_heads, 8):
+        groups = range(first, first + 8)
+        queries = [
+            rotate(
+                received[group * per_group : (group + 1) * per_group, 0:TILE, :]
+                .reshape(rows, width)
+                .astype(jnp.float32)
+            )
+            for group in groups
+        ]
+        scores = [
+            jnp.where(
+                valid,
+                lax.dot_general(
+                    query,
+                    keys[:, group].reshape(sessions * cache_len, width),
+                    contract,
+                    preferred_element_type=jnp.float32,
+                )
+                * scale,
+                -jnp.inf,
+            )
+            for query, group in zip(queries, groups)
+        ]
+        own_scores = [
+            jnp.where(
+                own_column == group * EXTRA + own_session,
+                lax.dot_general(query, own_key, contract, preferred_element_type=jnp.float32) * scale,
+                -jnp.inf,
+            )
+            for query, group in zip(queries, groups)
+        ]
+        highest = [
+            jnp.maximum(jnp.max(cached, axis=-1, keepdims=True), jnp.max(own, axis=-1, keepdims=True))
+            for cached, own in zip(scores, own_scores)
+        ]
+        scores = [jnp.exp(cached - high) for cached, high in zip(scores, highest)]
+        own_scores = [jnp.exp(own - high) for own, high in zip(own_scores, highest)]
+        shares = [
+            1.0 / (jnp.sum(cached, axis=-1, keepdims=True) + jnp.sum(own, axis=-1, keepdims=True))
+            for cached, own in zip(scores, own_scores)
+        ]
+        for cached, own, share, group in zip(scores, own_scores, shares, groups):
+            attended = jnp.dot(
+                (cached * share).astype(jnp.bfloat16),
+                values[:, group].reshape(sessions * cache_len, width),
+                preferred_element_type=jnp.float32,
+            )
+            attended += jnp.dot(
+                (own * share).astype(jnp.bfloat16), own_value, preferred_element_type=jnp.float32
+            )
+            out[group * rows : (group + 1) * rows, :] = attended.astype(jnp.bfloat16)
 
 
 def attend(received, keys, values, lengths):
@@ -443,7 +468,7 @@
         gathered,
         (inside(near_query), inside(near_keyval)),
         session_ids,
-        (devices, 2 * TILE, LANES),
+        (devices, TILE + EXTRA, LANES),
         (w_query.shape[1], w_keyval.shape[0]),
     )
     received = lax.all_to_all(local, "wide", split_axis=0, concat_axis=0, tiled=True)

time: 103 us -> 96.7 us (0.939)
  Pallas kernels: 27 us -> 22.2 us
  blocking collectives: 15.1 us -> 13.4 us
  waiting for transfers between devices: 33.6 us -> 34.7 us
    pallas_call x2, Pallas kernels: 9.74 us -> 6.91 us  [project(): pl.pallas_call(kernel, in_specs=[whole] * len(operands), out_specs=whole,...]
    pallas_call x1, Pallas kernels: 3.67 us -> 1.72 us  [attend(): pl.pallas_call(attend_kernel, in_specs=[whole] * 3 + [pl.BlockSpec(memory...]
    all_to_all x1, blocking collectives: 15.1 us -> 13.4 us  [on_block(): lax.all_to_all(local, 'wide', split_axis=0, concat_axis=0, tiled=True)]
    ppermute x32, waiting for transfers between devices: 33.6 us -> 34.7 us  [swapped(): return lax.ppermute(array, 'wide', [(i, i ^ mask) for i in range(devices)])]
  transfers between devices with their start and end apart: 32 -> 32, of which waited for: 18 -> 17; matrix products, arithmetic and copies ran while one was open for 0% -> 0% of each run, Pallas kernels for 13% -> 13%
where the time goes in v5:
time: 96.7 us; the launch traced here: 95.9 us
  waiting for transfers between devices  34.7 us (36%)
  starting transfers between devices  25.5 us (26%)
  Pallas kernels  22.2 us (23%)
  blocking collectives  13.4 us (14%)
    ppermute x32, waiting for transfers between devices, swapped(): return lax.ppermute(array, 'wide', [(i, i ^ mask) for i in range(devices)])  34.7 us
    ppermute x32, starting transfers between devices, swapped(): return lax.ppermute(array, 'wide', [(i, i ^ mask) for i in range(devices)])  25.5 us
    all_to_all x1, blocking collectives, on_block(): lax.all_to_all(local, 'wide', split_axis=0, concat_axis=0, tiled=True)  13.4 us
    pallas_call x2, Pallas kernels, prefetch(): pl.pallas_call(prefetch_kernel, in_specs=[pl.BlockSpec(memory_space=pltpu...  12.8 us
    pallas_call x2, Pallas kernels, project(): pl.pallas_call(kernel, in_specs=[whole] * len(operands), out_specs=whole,...  6.91 us
  transfers between devices with their start and end apart: 32, of which 17 were waited for; matrix products, arithmetic and copies ran while one was open for 0% of the time, Pallas kernels for 13%

profile of v5, /device:TPU:0, one launch (start us, length us, event | category | flops | bytes accessed | tf_op | source)
XLA Modules:
  0.0 95.9 jit_solution(12472146454392773951)
XLA Ops:
  0.0 3.0 %collective-permute-start = (bf16[4,16384]{1,0:T(4,128)(2,1)}, bf16[4,16384]{1,0:T(4,128)(2,1)S(1)}, u32[]{:S(2)}, u32[]{:S(2)}) collective-permute-start(bf16[4,16384]{1,0:T(4,128)(2,1)} %refs_0_.2), channel_id=1, source_target_pairs={{0,8},{1,9},{2,10},{3,11},{4,12},{5,13},{6,14},{7,15},{8,0},{9,1},... | collective-permute-start | bytes 393224 | tf_op jit(solution)/shard_map/ppermute | solution.py:175
  3.0 2.6 %collective-permute-start.1 = (bf16[4,16384]{1,0:T(4,128)(2,1)}, bf16[4,16384]{1,0:T(4,128)(2,1)S(1)}, u32[]{:S(2)}, u32[]{:S(2)}) collective-permute-start(bf16[4,16384]{1,0:T(4,128)(2,1)} %refs_0_.2), channel_id=1, source_target_pairs={{0,16},{1,17},{2,18},{3,19},{4,20},{5,21},{6,22},{7,23},{8,24},{9,... | collective-permute-start | bytes 393224 | tf_op jit(solution)/shard_map/ppermute | solution.py:175
  5.6 7.1 %shard_map.91 = (bf16[4,16384]{1,0:T(4,128)(2,1)S(1)}, f32[16384]{0:T(1024)S(1)}, bf16[16384,512]{1,0:T(8,128)(2,1)S(1)}, bf16[64,16384]{1,0:T(8,128)(2,1)S(1)},...) custom-call(bf16[4,16384]{1,0:T(4,128)(2,1)} %refs_0_.2, f32[16384]{0:T(1024)} %refs_1_.1, ...), custom_call_target="tpu_custom_call" | custom-call | bytes 21168128 | tf_op jit(solution)/shard_map/pallas_call | solution.py:204
  12.7 3.5 %collective-permute-done.1.z2 = bf16[4,16384]{1,0:T(4,128)(2,1)S(1)} collective-permute-done((bf16[4,16384]{1,0:T(4,128)(2,1)}, bf16[4,16384]{1,0:T(4,128)(2,1)S(1)}, u32[]{:S(2)}, u32[]{:S(2)}) %collective-permute-start.1) | collective-permute-done | bytes 131104 | tf_op jit(solution)/shard_map/ppermute | solution.py:175
  16.2 0.6 shard_map.92
  16.8 1.6 %collective-permute-start.3 = (bf16[64,16,128]{2,1,0:T(8,128)(2,1)S(1)}, bf16[64,16,128]{2,1,0:T(8,128)(2,1)S(1)}, u32[]{:S(2)}, u32[]{:S(2)}) collective-permute-start(bf16[64,16,128]{2,1,0:T(8,128)(2,1)S(1)} %get-tuple-element.21.refs_4_), channel_id=1, source_target_pairs={{0,2},{1,3},{2,0},{3,1},{4,6},{5,7},{6,4},{7,5},{8,10},{9,11},{10,... | collective-permute-start | bytes 786440 | tf_op jit(solution)/shard_map/ppermute | solution.py:175
  18.4 1.5 %collective-permute-start.5 = (bf16[64,16,128]{2,1,0:T(8,128)(2,1)S(1)}, bf16[64,16,128]{2,1,0:T(8,128)(2,1)S(1)}, u32[]{:S(2)}, u32[]{:S(2)}) collective-permute-start(bf16[64,16,128]{2,1,0:T(8,128)(2,1)S(1)} %get-tuple-element.22.refs_6_), channel_id=1, source_target_pairs={{0,4},{1,5},{2,6},{3,7},{4,0},{5,1},{6,2},{7,3},{8,12},{9,13},{10,... | collective-permute-start | bytes 786440 | tf_op jit(solution)/shard_map/ppermute | solution.py:175
  20.4 0.5 collective-permute-start.10
  20.9 2.3 %collective-permute-done.3.refs_5_ = bf16[64,16,128]{2,1,0:T(8,128)(2,1)S(1)} collective-permute-done((bf16[64,16,128]{2,1,0:T(8,128)(2,1)S(1)}, bf16[64,16,128]{2,1,0:T(8,128)(2,1)S(1)}, u32[]{:S(2)}, u32[]{:S(2)}) %collective-permute-start.3) | collective-permute-done | bytes 262176 | tf_op jit(solution)/shard_map/ppermute | solution.py:175
  23.2 1.5 %collective-permute-start.4 = (bf16[64,16,128]{2,1,0:T(8,128)(2,1)S(1)}, bf16[64,16,128]{2,1,0:T(8,128)(2,1)S(1)}, u32[]{:S(2)}, u32[]{:S(2)}) collective-permute-start(bf16[64,16,128]{2,1,0:T(8,128)(2,1)S(1)} %collective-permute-done.3.refs_5_), channel_id=1, source_target_pairs={{0,4},{1,5},{2,6},{3,7},{4,0},{5,1},{6,2},{7,3},{8,12},{9,13},{10,... | collective-permute-start | bytes 786440 | tf_op jit(solution)/shard_map/ppermute | solution.py:175
  24.8 1.8 %collective-permute-done.5.refs_7_ = bf16[64,16,128]{2,1,0:T(8,128)(2,1)S(1)} collective-permute-done((bf16[64,16,128]{2,1,0:T(8,128)(2,1)S(1)}, bf16[64,16,128]{2,1,0:T(8,128)(2,1)S(1)}, u32[]{:S(2)}, u32[]{:S(2)}) %collective-permute-start.5) | collective-permute-done | bytes 262176 | tf_op jit(solution)/shard_map/ppermute | solution.py:175
  26.5 0.6 collective-permute-start.6
  27.2 5.0 %collective-permute-done.9.refs_8_ = bf16[64,16,128]{2,1,0:T(8,128)(2,1)S(1)} collective-permute-done((bf16[64,16,128]{2,1,0:T(8,128)(2,1)S(1)}, bf16[64,16,128]{2,1,0:T(8,128)(2,1)S(1)}, u32[]{:S(2)}, u32[]{:S(2)}) %collective-permute-start.9) | collective-permute-done | bytes 262176 | tf_op jit(solution)/shard_map/ppermute | solution.py:175
  32.1 0.5 collective-permute-start.15
  32.7 3.3 %collective-permute-done.4.refs_0_ = bf16[64,16,128]{2,1,0:T(8,128)(2,1)S(1)} collective-permute-done((bf16[64,16,128]{2,1,0:T(8,128)(2,1)S(1)}, bf16[64,16,128]{2,1,0:T(8,128)(2,1)S(1)}, u32[]{:S(2)}, u32[]{:S(2)}) %collective-permute-start.4) | collective-permute-done | bytes 262176 | tf_op jit(solution)/shard_map/ppermute | solution.py:175
  38.6 3.8 %shard_map.93 = bf16[32,24,128]{2,1,0:T(8,128)(2,1)S(1)} custom-call(bf16[64,16,128]{2,1,0:T(8,128)(2,1)S(1)} %collective-permute-done.4.refs_0_, bf16[64,16,128]{2,1,0:T(8,128)(2,1)S(1)} %collective-permute-done.6.refs_1_, bf16[64,16,128]{2,1,0:T(8,128)(2,1)S(1)} %collective-permute-done.7.refs_2_, bf16[64,16,128]{2,1,0:T(8,128)(2,1)S(1)} %collective-permute-done.8.refs_3_, ...), custom_call_target="tpu_custom_call" | custom-call | flops 2415919104 | bytes 23068672 | tf_op jit(solution)/shard_map/pallas_call | solution.py:328
  42.4 13.4 %all_to_all.5.received = bf16[32,24,128]{2,1,0:T(8,128)(2,1)S(1)} all-to-all(bf16[32,24,128]{2,1,0:T(8,128)(2,1)S(1)} %shard_map.93), channel_id=1, replica_groups=mesh['groups'=1,'wide'=32] {'wide'}, dimensions={0} | all-to-all | bytes 393216 | tf_op jit(solution)/shard_map/all_to_all | solution.py:474
  55.8 1.7 %shard_map.94.refs_1_ = bf16[512,128]{1,0:T(8,128)(2,1)S(1)} custom-call(bf16[32,24,128]{2,1,0:T(8,128)(2,1)S(1)} %all_to_all.5.received, bf16[4,8,128,128]{3,2,1,0:T(8,128)(2,1)S(1)} %get-tuple-element.26.keys, bf16[4,8,128,128]{3,2,1,0:T(8,128)(2,1)S(1)} %get-tuple-element.27.values, s32[4]{0:T(128)S(1)} %copy-done.1), custom_call_target="tpu_custom_call" | custom-call | flops 150000000 | bytes 3000000 | tf_op jit(solution)/shard_map/pallas_call | solution.py:442
  57.5 1.1 %collective-permute-start.16 = (bf16[512,128]{1,0:T(8,128)(2,1)S(1)}, bf16[512,128]{1,0:T(8,128)(2,1)S(1)}, u32[]{:S(2)}, u32[]{:S(2)}) collective-permute-start(bf16[512,128]{1,0:T(8,128)(2,1)S(1)} %shard_map.94.refs_1_), channel_id=1, source_target_pairs={{0,8},{1,9},{2,10},{3,11},{4,12},{5,13},{6,14},{7,15},{8,0},{9,1},... | collective-permute-start | bytes 393224 | tf_op jit(solution)/shard_map/ppermute | solution.py:175
  58.6 1.4 %collective-permute-start.17 = (bf16[512,128]{1,0:T(8,128)(2,1)S(1)}, bf16[512,128]{1,0:T(8,128)(2,1)S(1)}, u32[]{:S(2)}, u32[]{:S(2)}) collective-permute-start(bf16[512,128]{1,0:T(8,128)(2,1)S(1)} %shard_map.94.refs_1_), channel_id=1, source_target_pairs={{0,16},{1,17},{2,18},{3,19},{4,20},{5,21},{6,22},{7,23},{8,24},{9,... | collective-permute-start | bytes 393224 | tf_op jit(solution)/shard_map/ppermute | solution.py:175
  60.0 2.0 %collective-permute-start.18 = (bf16[512,128]{1,0:T(8,128)(2,1)S(1)}, bf16[512,128]{1,0:T(8,128)(2,1)S(1)}, u32[]{:S(2)}, u32[]{:S(2)}) collective-permute-start(bf16[512,128]{1,0:T(8,128)(2,1)S(1)} %shard_map.94.refs_1_), channel_id=1, source_target_pairs={{0,24},{1,25},{2,26},{3,27},{4,28},{5,29},{6,30},{7,31},{8,16},{9,... | collective-permute-start | bytes 393224 | tf_op jit(solution)/shard_map/ppermute | solution.py:175
  62.0 5.8 %shard_map.95 = (bf16[16384,512]{1,0:T(8,128)(2,1)S(1)}, bf16[512,128]{1,0:T(8,128)(2,1)S(1)}) custom-call(bf16[16384,512]{1,0:T(8,128)(2,1)} %refs_0_.3, bf16[512,128]{1,0:T(8,128)(2,1)S(1)} %shard_map.94.refs_1_), custom_call_target="tpu_custom_call" | custom-call | bytes 16908288 | tf_op jit(solution)/shard_map/pallas_call | solution.py:204
  67.8 3.7 %collective-permute-done.17.z2 = bf16[512,128]{1,0:T(8,128)(2,1)S(1)} collective-permute-done((bf16[512,128]{1,0:T(8,128)(2,1)S(1)}, bf16[512,128]{1,0:T(8,128)(2,1)S(1)}, u32[]{:S(2)}, u32[]{:S(2)}) %collective-permute-start.17) | collective-permute-done | bytes 131104 | tf_op jit(solution)/shard_map/ppermute | solution.py:175
  71.7 1.4 %collective-permute-start.21 = (bf16[64,16,128]{2,1,0:T(8,128)(2,1)S(1)}, bf16[64,16,128]{2,1,0:T(8,128)(2,1)S(1)}, u32[]{:S(2)}, u32[]{:S(2)}) collective-permute-start(bf16[64,16,128]{2,1,0:T(8,128)(2,1)S(1)} %get-tuple-element.30.refs_6_), channel_id=1, source_target_pairs={{0,4},{1,5},{2,6},{3,7},{4,0},{5,1},{6,2},{7,3},{8,12},{9,13},{10,... | collective-permute-start | bytes 786440 | tf_op jit(solution)/shard_map/ppermute | solution.py:175
  73.1 0.7 collective-permute-start.25
  73.8 1.9 %collective-permute-start.26 = (bf16[64,16,128]{2,1,0:T(8,128)(2,1)S(1)}, bf16[64,16,128]{2,1,0:T(8,128)(2,1)S(1)}, u32[]{:S(2)}, u32[]{:S(2)}) collective-permute-start(bf16[64,16,128]{2,1,0:T(8,128)(2,1)S(1)} %get-tuple-element.30.refs_6_), channel_id=1, source_target_pairs={{0,2},{1,3},{2,0},{3,1},{4,6},{5,7},{6,4},{7,5},{8,10},{9,11},{10,... | collective-permute-start | bytes 786440 | tf_op jit(solution)/shard_map/ppermute | solution.py:175
  75.7 5.0 %collective-permute-done.19.refs_5_ = bf16[64,16,128]{2,1,0:T(8,128)(2,1)S(1)} collective-permute-done((bf16[64,16,128]{2,1,0:T(8,128)(2,1)S(1)}, bf16[64,16,128]{2,1,0:T(8,128)(2,1)S(1)}, u32[]{:S(2)}, u32[]{:S(2)}) %collective-permute-start.19) | collective-permute-done | bytes 262176 | tf_op jit(solution)/shard_map/ppermute | solution.py:175
  81.0 1.9 %collective-permute-start.22 = (bf16[64,16,128]{2,1,0:T(8,128)(2,1)S(1)}, bf16[64,16,128]{2,1,0:T(8,128)(2,1)S(1)}, u32[]{:S(2)}, u32[]{:S(2)}) collective-permute-start(bf16[64,16,128]{2,1,0:T(8,128)(2,1)S(1)} %collective-permute-done.21.refs_7_), channel_id=1, source_target_pairs={{0,2},{1,3},{2,0},{3,1},{4,6},{5,7},{6,4},{7,5},{8,10},{9,11},{10,... | collective-permute-start | bytes 786440 | tf_op jit(solution)/shard_map/ppermute | solution.py:175
  82.9 3.7 %collective-permute-done.25.refs_8_ = bf16[64,16,128]{2,1,0:T(8,128)(2,1)S(1)} collective-permute-done((bf16[64,16,128]{2,1,0:T(8,128)(2,1)S(1)}, bf16[64,16,128]{2,1,0:T(8,128)(2,1)S(1)}, u32[]{:S(2)}, u32[]{:S(2)}) %collective-permute-start.25) | collective-permute-done | bytes 262176 | tf_op jit(solution)/shard_map/ppermute | solution.py:175
  87.1 3.0 %collective-permute-done.20.refs_0_ = bf16[64,16,128]{2,1,0:T(8,128)(2,1)S(1)} collective-permute-done((bf16[64,16,128]{2,1,0:T(8,128)(2,1)S(1)}, bf16[64,16,128]{2,1,0:T(8,128)(2,1)S(1)}, u32[]{:S(2)}, u32[]{:S(2)}) %collective-permute-start.20) | collective-permute-done | bytes 262176 | tf_op jit(solution)/shard_map/ppermute | solution.py:175
  91.2 0.9 collective-permute-done.30.refs_14_
  92.8 3.1 %shard_map.97 = bf16[128,512]{1,0:T(8,128)(2,1)} custom-call(bf16[64,16,128]{2,1,0:T(8,128)(2,1)S(1)} %collective-permute-done.20.refs_0_, bf16[64,16,128]{2,1,0:T(8,128)(2,1)S(1)} %collective-permute-done.22.refs_1_, bf16[64,16,128]{2,1,0:T(8,128)(2,1)S(1)} %collective-permute-done.23.refs_2_, bf16[64,16,128]{2,1,0:T(8,128)(2,1)S(1)} %collective-permute-done.24.refs_3_, ...), custom_call_target="tpu_custom_call" | custom-call | flops 2147483648 | bytes 20971520 | tf_op jit(solution)/shard_map/pallas_call | solution.py:328
  (44 shorter events, 5.9 us)
Async XLA Ops:
  0.0 12.7 %collective-permute-start = (bf16[4,16384]{1,0:T(4,128)(2,1)}, bf16[4,16384]{1,0:T(4,128)(2,1)S(1)}, u32[]{:S(2)}, u32[]{:S(2)}) collective-permute-start(bf16[4,16384]{1,0:T(4,128)(2,1)} %refs_0_.2), channel_id=1, source_target_pairs={{0,8},{1,9},{2,10},{3,11},{4,12},{5,13},{6,14},{7,15},{8,0},{9,1},... | collective-permute-start | bytes 393224 | tf_op jit(solution)/shard_map/ppermute | solution.py:175
  3.0 13.2 %collective-permute-start.1 = (bf16[4,16384]{1,0:T(4,128)(2,1)}, bf16[4,16384]{1,0:T(4,128)(2,1)S(1)}, u32[]{:S(2)}, u32[]{:S(2)}) collective-permute-start(bf16[4,16384]{1,0:T(4,128)(2,1)} %refs_0_.2), channel_id=1, source_target_pairs={{0,16},{1,17},{2,18},{3,19},{4,20},{5,21},{6,22},{7,23},{8,24},{9,... | collective-permute-start | bytes 393224 | tf_op jit(solution)/shard_map/ppermute | solution.py:175
  5.6 10.6 %collective-permute-start.2 = (bf16[4,16384]{1,0:T(4,128)(2,1)}, bf16[4,16384]{1,0:T(4,128)(2,1)S(1)}, u32[]{:S(2)}, u32[]{:S(2)}) collective-permute-start(bf16[4,16384]{1,0:T(4,128)(2,1)} %refs_0_.2), channel_id=1, source_target_pairs={{0,24},{1,25},{2,26},{3,27},{4,28},{5,29},{6,30},{7,31},{8,16},{9,... | collective-permute-start | bytes 393224 | tf_op jit(solution)/shard_map/ppermute | solution.py:175
  16.8 6.4 %collective-permute-start.3 = (bf16[64,16,128]{2,1,0:T(8,128)(2,1)S(1)}, bf16[64,16,128]{2,1,0:T(8,128)(2,1)S(1)}, u32[]{:S(2)}, u32[]{:S(2)}) collective-permute-start(bf16[64,16,128]{2,1,0:T(8,128)(2,1)S(1)} %get-tuple-element.21.refs_4_), channel_id=1, source_target_pairs={{0,2},{1,3},{2,0},{3,1},{4,6},{5,7},{6,4},{7,5},{8,10},{9,11},{10,... | collective-permute-start | bytes 786440 | tf_op jit(solution)/shard_map/ppermute | solution.py:175
  18.4 8.2 %collective-permute-start.5 = (bf16[64,16,128]{2,1,0:T(8,128)(2,1)S(1)}, bf16[64,16,128]{2,1,0:T(8,128)(2,1)S(1)}, u32[]{:S(2)}, u32[]{:S(2)}) collective-permute-start(bf16[64,16,128]{2,1,0:T(8,128)(2,1)S(1)} %get-tuple-element.22.refs_6_), channel_id=1, source_target_pairs={{0,4},{1,5},{2,6},{3,7},{4,0},{5,1},{6,2},{7,3},{8,12},{9,13},{10,... | collective-permute-start | bytes 786440 | tf_op jit(solution)/shard_map/ppermute | solution.py:175
  19.9 16.6 %collective-permute-start.11 = (bf16[128,16,128]{2,1,0:T(8,128)(2,1)S(1)}, bf16[128,16,128]{2,1,0:T(8,128)(2,1)S(1)}, u32[]{:S(2)}, u32[]{:S(2)}) collective-permute-start(bf16[128,16,128]{2,1,0:T(8,128)(2,1)S(1)} %get-tuple-element.23), channel_id=1, source_target_pairs={{0,1},{1,0},{2,3},{3,2},{4,5},{5,4},{6,7},{7,6},{8,9},{9,8},{10,11... | collective-permute-start | bytes 1572872 | tf_op jit(solution)/shard_map/ppermute | solution.py:175
  19.9 12.3 %collective-permute-start.9 = (bf16[64,16,128]{2,1,0:T(8,128)(2,1)S(1)}, bf16[64,16,128]{2,1,0:T(8,128)(2,1)S(1)}, u32[]{:S(2)}, u32[]{:S(2)}) collective-permute-start(bf16[64,16,128]{2,1,0:T(8,128)(2,1)S(1)} %get-tuple-element.21.refs_4_), channel_id=1, source_target_pairs={{0,4},{1,5},{2,6},{3,7},{4,0},{5,1},{6,2},{7,3},{8,12},{9,13},{10,... | collective-permute-start | bytes 786440 | tf_op jit(solution)/shard_map/ppermute | solution.py:175
  20.4 11.8 %collective-permute-start.10 = (bf16[64,16,128]{2,1,0:T(8,128)(2,1)S(1)}, bf16[64,16,128]{2,1,0:T(8,128)(2,1)S(1)}, u32[]{:S(2)}, u32[]{:S(2)}) collective-permute-start(bf16[64,16,128]{2,1,0:T(8,128)(2,1)S(1)} %get-tuple-element.22.refs_6_), channel_id=1, source_target_pairs={{0,2},{1,3},{2,0},{3,1},{4,6},{5,7},{6,4},{7,5},{8,10},{9,11},{10,... | collective-permute-start | bytes 786440 | tf_op jit(solution)/shard_map/ppermute | solution.py:175
  23.2 12.7 %collective-permute-start.4 = (bf16[64,16,128]{2,1,0:T(8,128)(2,1)S(1)}, bf16[64,16,128]{2,1,0:T(8,128)(2,1)S(1)}, u32[]{:S(2)}, u32[]{:S(2)}) collective-permute-start(bf16[64,16,128]{2,1,0:T(8,128)(2,1)S(1)} %collective-permute-done.3.refs_5_), channel_id=1, source_target_pairs={{0,4},{1,5},{2,6},{3,7},{4,0},{5,1},{6,2},{7,3},{8,12},{9,13},{10,... | collective-permute-start | bytes 786440 | tf_op jit(solution)/shard_map/ppermute | solution.py:175
  26.5 9.4 %collective-permute-start.6 = (bf16[64,16,128]{2,1,0:T(8,128)(2,1)S(1)}, bf16[64,16,128]{2,1,0:T(8,128)(2,1)S(1)}, u32[]{:S(2)}, u32[]{:S(2)}) collective-permute-start(bf16[64,16,128]{2,1,0:T(8,128)(2,1)S(1)} %collective-permute-done.5.refs_7_), channel_id=1, source_target_pairs={{0,2},{1,3},{2,0},{3,1},{4,6},{5,7},{6,4},{7,5},{8,10},{9,11},{10,... | collective-permute-start | bytes 786440 | tf_op jit(solution)/shard_map/ppermute | solution.py:175
  32.1 4.4 %collective-permute-start.12 = (bf16[64,16,128]{2,1,0:T(8,128)(2,1)S(1)}, bf16[64,16,128]{2,1,0:T(8,128)(2,1)S(1)}, u32[]{:S(2)}, u32[]{:S(2)}) collective-permute-start(bf16[64,16,128]{2,1,0:T(8,128)(2,1)S(1)} %collective-permute-done.3.refs_5_), channel_id=1, source_target_pairs={{0,1},{1,0},{2,3},{3,2},{4,5},{5,4},{6,7},{7,6},{8,9},{9,8},{10,11... | collective-permute-start | bytes 786440 | tf_op jit(solution)/shard_map/ppermute | solution.py:175
  32.1 5.7 %collective-permute-start.15 = (bf16[64,16,128]{2,1,0:T(8,128)(2,1)S(1)}, bf16[64,16,128]{2,1,0:T(8,128)(2,1)S(1)}, u32[]{:S(2)}, u32[]{:S(2)}) collective-permute-start(bf16[64,16,128]{2,1,0:T(8,128)(2,1)S(1)} %collective-permute-done.5.refs_7_), channel_id=1, source_target_pairs={{0,1},{1,0},{2,3},{3,2},{4,5},{5,4},{6,7},{7,6},{8,9},{9,8},{10,11... | collective-permute-start | bytes 786440 | tf_op jit(solution)/shard_map/ppermute | solution.py:175
  36.0 1.5 %collective-permute-start.13 = (bf16[64,16,128]{2,1,0:T(8,128)(2,1)S(1)}, bf16[64,16,128]{2,1,0:T(8,128)(2,1)S(1)}, u32[]{:S(2)}, u32[]{:S(2)}) collective-permute-start(bf16[64,16,128]{2,1,0:T(8,128)(2,1)S(1)} %collective-permute-done.9.refs_8_), channel_id=1, source_target_pairs={{0,1},{1,0},{2,3},{3,2},{4,5},{5,4},{6,7},{7,6},{8,9},{9,8},{10,11... | collective-permute-start | bytes 786440 | tf_op jit(solution)/shard_map/ppermute | solution.py:175
  36.0 1.9 %collective-permute-start.14 = (bf16[64,16,128]{2,1,0:T(8,128)(2,1)S(1)}, bf16[64,16,128]{2,1,0:T(8,128)(2,1)S(1)}, u32[]{:S(2)}, u32[]{:S(2)}) collective-permute-start(bf16[64,16,128]{2,1,0:T(8,128)(2,1)S(1)} %collective-permute-done.10.refs_9_), channel_id=1, source_target_pairs={{0,1},{1,0},{2,3},{3,2},{4,5},{5,4},{6,7},{7,6},{8,9},{9,8},{10,11... | collective-permute-start | bytes 786440 | tf_op jit(solution)/shard_map/ppermute | solution.py:175
  36.5 1.8 %collective-permute-start.7 = (bf16[64,16,128]{2,1,0:T(8,128)(2,1)S(1)}, bf16[64,16,128]{2,1,0:T(8,128)(2,1)S(1)}, u32[]{:S(2)}, u32[]{:S(2)}) collective-permute-start(bf16[64,16,128]{2,1,0:T(8,128)(2,1)S(1)} %collective-permute-done.4.refs_0_), channel_id=1, source_target_pairs={{0,1},{1,0},{2,3},{3,2},{4,5},{5,4},{6,7},{7,6},{8,9},{9,8},{10,11... | collective-permute-start | bytes 786440 | tf_op jit(solution)/shard_map/ppermute | solution.py:175
  36.6 2.1 %collective-permute-start.8 = (bf16[64,16,128]{2,1,0:T(8,128)(2,1)S(1)}, bf16[64,16,128]{2,1,0:T(8,128)(2,1)S(1)}, u32[]{:S(2)}, u32[]{:S(2)}) collective-permute-start(bf16[64,16,128]{2,1,0:T(8,128)(2,1)S(1)} %collective-permute-done.6.refs_1_), channel_id=1, source_target_pairs={{0,1},{1,0},{2,3},{3,2},{4,5},{5,4},{6,7},{7,6},{8,9},{9,8},{10,11... | collective-permute-start | bytes 786440 | tf_op jit(solution)/shard_map/ppermute | solution.py:175
  57.5 10.3 %collective-permute-start.16 = (bf16[512,128]{1,0:T(8,128)(2,1)S(1)}, bf16[512,128]{1,0:T(8,128)(2,1)S(1)}, u32[]{:S(2)}, u32[]{:S(2)}) collective-permute-start(bf16[512,128]{1,0:T(8,128)(2,1)S(1)} %shard_map.94.refs_1_), channel_id=1, source_target_pairs={{0,8},{1,9},{2,10},{3,11},{4,12},{5,13},{6,14},{7,15},{8,0},{9,1},... | collective-permute-start | bytes 393224 | tf_op jit(solution)/shard_map/ppermute | solution.py:175
  58.6 12.8 %collective-permute-start.17 = (bf16[512,128]{1,0:T(8,128)(2,1)S(1)}, bf16[512,128]{1,0:T(8,128)(2,1)S(1)}, u32[]{:S(2)}, u32[]{:S(2)}) collective-permute-start(bf16[512,128]{1,0:T(8,128)(2,1)S(1)} %shard_map.94.refs_1_), channel_id=1, source_target_pairs={{0,16},{1,17},{2,18},{3,19},{4,20},{5,21},{6,22},{7,23},{8,24},{9,... | collective-permute-start | bytes 393224 | tf_op jit(solution)/shard_map/ppermute | solution.py:175
  60.0 11.5 %collective-permute-start.18 = (bf16[512,128]{1,0:T(8,128)(2,1)S(1)}, bf16[512,128]{1,0:T(8,128)(2,1)S(1)}, u32[]{:S(2)}, u32[]{:S(2)}) collective-permute-start(bf16[512,128]{1,0:T(8,128)(2,1)S(1)} %shard_map.94.refs_1_), channel_id=1, source_target_pairs={{0,24},{1,25},{2,26},{3,27},{4,28},{5,29},{6,30},{7,31},{8,16},{9,... | collective-permute-start | bytes 393224 | tf_op jit(solution)/shard_map/ppermute | solution.py:175
  71.6 9.2 %collective-permute-start.19 = (bf16[64,16,128]{2,1,0:T(8,128)(2,1)S(1)}, bf16[64,16,128]{2,1,0:T(8,128)(2,1)S(1)}, u32[]{:S(2)}, u32[]{:S(2)}) collective-permute-start(bf16[64,16,128]{2,1,0:T(8,128)(2,1)S(1)} %get-tuple-element.29.refs_4_), channel_id=1, source_target_pairs={{0,2},{1,3},{2,0},{3,1},{4,6},{5,7},{6,4},{7,5},{8,10},{9,11},{10,... | collective-permute-start | bytes 786440 | tf_op jit(solution)/shard_map/ppermute | solution.py:175
  71.7 9.3 %collective-permute-start.21 = (bf16[64,16,128]{2,1,0:T(8,128)(2,1)S(1)}, bf16[64,16,128]{2,1,0:T(8,128)(2,1)S(1)}, u32[]{:S(2)}, u32[]{:S(2)}) collective-permute-start(bf16[64,16,128]{2,1,0:T(8,128)(2,1)S(1)} %get-tuple-element.30.refs_6_), channel_id=1, source_target_pairs={{0,4},{1,5},{2,6},{3,7},{4,0},{5,1},{6,2},{7,3},{8,12},{9,13},{10,... | collective-permute-start | bytes 786440 | tf_op jit(solution)/shard_map/ppermute | solution.py:175
  73.1 13.5 %collective-permute-start.25 = (bf16[64,16,128]{2,1,0:T(8,128)(2,1)S(1)}, bf16[64,16,128]{2,1,0:T(8,128)(2,1)S(1)}, u32[]{:S(2)}, u32[]{:S(2)}) collective-permute-start(bf16[64,16,128]{2,1,0:T(8,128)(2,1)S(1)} %get-tuple-element.29.refs_4_), channel_id=1, source_target_pairs={{0,4},{1,5},{2,6},{3,7},{4,0},{5,1},{6,2},{7,3},{8,12},{9,13},{10,... | collective-permute-start | bytes 786440 | tf_op jit(solution)/shard_map/ppermute | solution.py:175
  73.8 12.8 %collective-permute-start.26 = (bf16[64,16,128]{2,1,0:T(8,128)(2,1)S(1)}, bf16[64,16,128]{2,1,0:T(8,128)(2,1)S(1)}, u32[]{:S(2)}, u32[]{:S(2)}) collective-permute-start(bf16[64,16,128]{2,1,0:T(8,128)(2,1)S(1)} %get-tuple-element.30.refs_6_), channel_id=1, source_target_pairs={{0,2},{1,3},{2,0},{3,1},{4,6},{5,7},{6,4},{7,5},{8,10},{9,11},{10,... | collective-permute-start | bytes 786440 | tf_op jit(solution)/shard_map/ppermute | solution.py:175
  75.7 16.3 %collective-permute-start.27 = (bf16[128,16,128]{2,1,0:T(8,128)(2,1)S(1)}, bf16[128,16,128]{2,1,0:T(8,128)(2,1)S(1)}, u32[]{:S(2)}, u32[]{:S(2)}) collective-permute-start(bf16[128,16,128]{2,1,0:T(8,128)(2,1)S(1)} %get-tuple-element.31), channel_id=1, source_target_pairs={{0,1},{1,0},{2,3},{3,2},{4,5},{5,4},{6,7},{7,6},{8,9},{9,8},{10,11... | collective-permute-start | bytes 1572872 | tf_op jit(solution)/shard_map/ppermute | solution.py:175
  80.8 9.4 %collective-permute-start.20 = (bf16[64,16,128]{2,1,0:T(8,128)(2,1)S(1)}, bf16[64,16,128]{2,1,0:T(8,128)(2,1)S(1)}, u32[]{:S(2)}, u32[]{:S(2)}) collective-permute-start(bf16[64,16,128]{2,1,0:T(8,128)(2,1)S(1)} %collective-permute-done.19.refs_5_), channel_id=1, source_target_pairs={{0,4},{1,5},{2,6},{3,7},{4,0},{5,1},{6,2},{7,3},{8,12},{9,13},{10,... | collective-permute-start | bytes 786440 | tf_op jit(solution)/shard_map/ppermute | solution.py:175
  81.0 9.1 %collective-permute-start.22 = (bf16[64,16,128]{2,1,0:T(8,128)(2,1)S(1)}, bf16[64,16,128]{2,1,0:T(8,128)(2,1)S(1)}, u32[]{:S(2)}, u32[]{:S(2)}) collective-permute-start(bf16[64,16,128]{2,1,0:T(8,128)(2,1)S(1)} %collective-permute-done.21.refs_7_), channel_id=1, source_target_pairs={{0,2},{1,3},{2,0},{3,1},{4,6},{5,7},{6,4},{7,5},{8,10},{9,11},{10,... | collective-permute-start | bytes 786440 | tf_op jit(solution)/shard_map/ppermute | solution.py:175
  86.6 4.0 %collective-permute-start.28 = (bf16[64,16,128]{2,1,0:T(8,128)(2,1)S(1)}, bf16[64,16,128]{2,1,0:T(8,128)(2,1)S(1)}, u32[]{:S(2)}, u32[]{:S(2)}) collective-permute-start(bf16[64,16,128]{2,1,0:T(8,128)(2,1)S(1)} %collective-permute-done.19.refs_5_), channel_id=1, source_target_pairs={{0,1},{1,0},{2,3},{3,2},{4,5},{5,4},{6,7},{7,6},{8,9},{9,8},{10,11... | collective-permute-start | bytes 786440 | tf_op jit(solution)/shard_map/ppermute | solution.py:175
  86.6 4.1 %collective-permute-start.29 = (bf16[64,16,128]{2,1,0:T(8,128)(2,1)S(1)}, bf16[64,16,128]{2,1,0:T(8,128)(2,1)S(1)}, u32[]{:S(2)}, u32[]{:S(2)}) collective-permute-start(bf16[64,16,128]{2,1,0:T(8,128)(2,1)S(1)} %collective-permute-done.25.refs_8_), channel_id=1, source_target_pairs={{0,1},{1,0},{2,3},{3,2},{4,5},{5,4},{6,7},{7,6},{8,9},{9,8},{10,11... | collective-permute-start | bytes 786440 | tf_op jit(solution)/shard_map/ppermute | solution.py:175
  90.1 1.9 %collective-permute-start.31 = (bf16[64,16,128]{2,1,0:T(8,128)(2,1)S(1)}, bf16[64,16,128]{2,1,0:T(8,128)(2,1)S(1)}, u32[]{:S(2)}, u32[]{:S(2)}) collective-permute-start(bf16[64,16,128]{2,1,0:T(8,128)(2,1)S(1)} %collective-permute-done.21.refs_7_), channel_id=1, source_target_pairs={{0,1},{1,0},{2,3},{3,2},{4,5},{5,4},{6,7},{7,6},{8,9},{9,8},{10,11... | collective-permute-start | bytes 786440 | tf_op jit(solution)/shard_map/ppermute | solution.py:175
  90.1 1.9 %collective-permute-start.30 = (bf16[64,16,128]{2,1,0:T(8,128)(2,1)S(1)}, bf16[64,16,128]{2,1,0:T(8,128)(2,1)S(1)}, u32[]{:S(2)}, u32[]{:S(2)}) collective-permute-start(bf16[64,16,128]{2,1,0:T(8,128)(2,1)S(1)} %collective-permute-done.26.refs_9_), channel_id=1, source_target_pairs={{0,1},{1,0},{2,3},{3,2},{4,5},{5,4},{6,7},{7,6},{8,9},{9,8},{10,11... | collective-permute-start | bytes 786440 | tf_op jit(solution)/shard_map/ppermute | solution.py:175
  90.6 1.8 %collective-permute-start.23 = (bf16[64,16,128]{2,1,0:T(8,128)(2,1)S(1)}, bf16[64,16,128]{2,1,0:T(8,128)(2,1)S(1)}, u32[]{:S(2)}, u32[]{:S(2)}) collective-permute-start(bf16[64,16,128]{2,1,0:T(8,128)(2,1)S(1)} %collective-permute-done.20.refs_0_), channel_id=1, source_target_pairs={{0,1},{1,0},{2,3},{3,2},{4,5},{5,4},{6,7},{7,6},{8,9},{9,8},{10,11... | collective-permute-start | bytes 786440 | tf_op jit(solution)/shard_map/ppermute | solution.py:175
  90.7 2.1 %collective-permute-start.24 = (bf16[64,16,128]{2,1,0:T(8,128)(2,1)S(1)}, bf16[64,16,128]{2,1,0:T(8,128)(2,1)S(1)}, u32[]{:S(2)}, u32[]{:S(2)}) collective-permute-start(bf16[64,16,128]{2,1,0:T(8,128)(2,1)S(1)} %collective-permute-done.22.refs_1_), channel_id=1, source_target_pairs={{0,1},{1,0},{2,3},{3,2},{4,5},{5,4},{6,7},{7,6},{8,9},{9,8},{10,11... | collective-permute-start | bytes 786440 | tf_op jit(solution)/shard_map/ppermute | solution.py:175
  (2 other events, 81.8 us)

commit v6 on v5

--- a/solution.py
+++ b/solution.py
@@ -225,37 +225,23 @@
     return (me ^ (core + 2 * plane + 8 * column)) * PIECE + at % PIECE
 
 
-COUNT = 64
-
-
-def multiply(refs, weight, total, weight_kv=None, total_kv=None):
+def multiply(refs, weight, weight_kv=None):
     placed = [refs[ORDER.index(at)] for at in range(16)]
-    low, high = placed[0:8], placed[8:16]
-    total[...] = jnp.zeros_like(total)
-    if weight_kv is not None:
-        total_kv[...] = jnp.zeros_like(total_kv)
-    half = low[0].shape[0]
-    blocks = 2 * half
-    for parts, base in ((low, 0), (high, half)):
-
-        def add(step, _, parts=parts, base=base):
-            first = step * COUNT
-            columns = []
-            for at in range(COUNT):
-                column = []
-                for ref in parts:
-                    offset = base if ref.shape[0] == blocks else 0
-                    column.append(ref[first + at + offset])
-                columns.append(jnp.concatenate(column, axis=0))
-            rows = jnp.concatenate(columns, axis=1)
-            depth = pl.ds(pl.multiple_of((base + first) * LANES, COUNT * LANES), COUNT * LANES)
-            total[...] += jnp.dot(rows, weight[depth, :], preferred_element_type=jnp.float32)
-            if weight_kv is not None:
-                total_kv[...] += lax.dot_general(
-                    rows, weight_kv[:, depth], (((1,), (1,)), ((), ())), preferred_element_type=jnp.float32
-                )
-
-        lax.fori_loop(0, half // COUNT, add, None)
+    half = placed[0].shape[0]
+    total = total_kv = 0.0
+    for parts, base in ((placed[0:8], 0), (placed[8:16], half)):
+        columns = []
+        for at in range(half):
+            column = [ref[at + (base if ref.shape[0] > half else 0)] for ref in parts]
+            columns.append(jnp.concatenate(column, axis=0))
+        rows = jnp.concatenate(columns, axis=1)
+        depth = slice(base * LANES, (base + half) * LANES)
+        total += jnp.dot(rows, weight[depth, :], preferred_element_type=jnp.float32)
+        if weight_kv is not None:
+            total_kv += lax.dot_general(
+                rows, weight_kv[:, depth], (((1,), (1,)), ((), ())), preferred_element_type=jnp.float32
+            )
+    return total, total_kv
 
 
 def one_hot(equal):
@@ -269,9 +255,9 @@
 
 
 def query_kernel(*refs):
-    weight, weight_kv, sessions, out, total, total_kv = refs[16:]
+    weight, weight_kv, sessions, out = refs[16:]
     me = lax.axis_index("wide")
-    multiply(refs, weight, total, weight_kv, total_kv)
+    total, total_kv = multiply(refs, weight, weight_kv)
     rows, width = total.shape
     heads = width // LANES
     devices = rows // PIECE
@@ -289,7 +275,7 @@
     columns = total_kv.shape[1]
     at = lax.broadcasted_iota(jnp.int32, (devices * EXTRA, rows), 0)
     wanted = jnp.where(at % EXTRA < PIECE, (at // EXTRA) * PIECE + at % EXTRA, -1)
-    keyval = total_kv[...].astype(jnp.bfloat16)
+    keyval = total_kv.astype(jnp.bfloat16)
     ordered = jnp.dot(one_hot(wanted == session), keyval, preferred_element_type=jnp.float32)
     here = lax.broadcasted_iota(jnp.int32, (columns, LANES), 0)
     there = lax.broadcasted_iota(jnp.int32, (columns, LANES), 1)
@@ -299,12 +285,12 @@
 
 
 def out_kernel(*refs):
-    weight, sessions, out, total = refs[16:]
-    multiply(refs, weight, total)
+    weight, sessions, out = refs[16:]
+    total, _ = multiply(refs, weight)
     rows = total.shape[0]
     source = source_rows(lax.axis_index("wide"), rows)
     chosen = one_hot(as_column(sessions) == source)
-    rounded = total[...].astype(jnp.bfloat16)
+    rounded = total.astype(jnp.bfloat16)
     out[...] = jnp.dot(chosen, rounded, preferred_element_type=jnp.float32).astype(jnp.bfloat16)
 
 
@@ -319,18 +305,16 @@
     return [operands[at] for at in ORDER]
 
 
-def project(kernel, gathered, weights, session_ids, out_shape, scratch):
+def project(kernel, gathered, weights, session_ids, out_shape, columns):
     operands = gathered_operands(gathered) + list(weights) + [session_ids[None, :]]
     whole = pl.BlockSpec(memory_space=pltpu.VMEM)
     rows = session_ids.shape[0]
     depth = weights[0].shape[0]
-    columns = sum(width for width in scratch)
     return pl.pallas_call(
         kernel,
         in_specs=[whole] * len(operands),
         out_specs=whole,
         out_shape=jax.ShapeDtypeStruct(out_shape, jnp.bfloat16),
-        scratch_shapes=[pltpu.VMEM((rows, width), jnp.float32) for width in scratch],
         compiler_params=pltpu.CompilerParams(vmem_limit_bytes=PROJECT_MIB * MIB),
         cost_estimate=pl.CostEstimate(
             flops=2 * rows * depth * columns, bytes_accessed=2 * depth * (columns + rows), transcendentals=0
@@ -469,14 +453,14 @@
         (inside(near_query), inside(near_keyval)),
         session_ids,
         (devices, TILE + EXTRA, LANES),
-        (w_query.shape[1], w_keyval.shape[0]),
+        w_query.shape[1] + w_keyval.shape[0],
     )
     received = lax.all_to_all(local, "wide", split_axis=0, concat_axis=0, tiled=True)
     attended = attend(received, inside(near_keys), inside(near_values), lengths)
     near_out, near = prefetch((w_out,), (attended,))
     gathered = gather_rows(attended, near, pack, devices)
     return project(
-        out_kernel, gathered, (inside(near_out),), session_ids, (rows, w_out.shape[1]), (w_out.shape[1],)
+        out_kernel, gathered, (inside(near_out),), session_ids, (rows, w_out.shape[1]), w_out.shape[1]
     )
 
 

time: 96.7 us -> 97.1 us (level)
  no operation moved by 1% of the time
where the time goes in v6:
time: 97.1 us; the launch traced here: 96.3 us
  waiting for transfers between devices  34.7 us (36%)
  starting transfers between devices  25.5 us (26%)
  Pallas kernels  22.6 us (23%)
  blocking collectives  13.4 us (14%)
    ppermute x32, waiting for transfers between devices, swapped(): return lax.ppermute(array, 'wide', [(i, i ^ mask) for i in range(devices)])  34.7 us
    ppermute x32, starting transfers between devices, swapped(): return lax.ppermute(array, 'wide', [(i, i ^ mask) for i in range(devices)])  25.5 us
    all_to_all x1, blocking collectives, on_block(): lax.all_to_all(local, 'wide', split_axis=0, concat_axis=0, tiled=True)  13.4 us
    pallas_call x2, Pallas kernels, prefetch(): pl.pallas_call(prefetch_kernel, in_specs=[pl.BlockSpec(memory_space=pltpu...  12.8 us
    pallas_call x2, Pallas kernels, project(): pl.pallas_call(kernel, in_specs=[whole] * len(operands), out_specs=whole,...  7.31 us
  transfers between devices with their start and end apart: 32, of which 17 were waited for; matrix products, arithmetic and copies ran while one was open for 0% of the time, Pallas kernels for 13%

profile of v6, /device:TPU:0, one launch (start us, length us, event | category | flops | bytes accessed | tf_op | source)
XLA Modules:
  0.0 96.3 jit_solution(13661961700549645110)
XLA Ops:
  0.0 3.0 %collective-permute-start = (bf16[4,16384]{1,0:T(4,128)(2,1)}, bf16[4,16384]{1,0:T(4,128)(2,1)S(1)}, u32[]{:S(2)}, u32[]{:S(2)}) collective-permute-start(bf16[4,16384]{1,0:T(4,128)(2,1)} %refs_0_.2), channel_id=1, source_target_pairs={{0,8},{1,9},{2,10},{3,11},{4,12},{5,13},{6,14},{7,15},{8,0},{9,1},... | collective-permute-start | bytes 393224 | tf_op jit(solution)/shard_map/ppermute | solution.py:175
  3.0 2.6 %collective-permute-start.1 = (bf16[4,16384]{1,0:T(4,128)(2,1)}, bf16[4,16384]{1,0:T(4,128)(2,1)S(1)}, u32[]{:S(2)}, u32[]{:S(2)}) collective-permute-start(bf16[4,16384]{1,0:T(4,128)(2,1)} %refs_0_.2), channel_id=1, source_target_pairs={{0,16},{1,17},{2,18},{3,19},{4,20},{5,21},{6,22},{7,23},{8,24},{9,... | collective-permute-start | bytes 393224 | tf_op jit(solution)/shard_map/ppermute | solution.py:175
  5.6 7.1 %shard_map.91 = (bf16[4,16384]{1,0:T(4,128)(2,1)S(1)}, f32[16384]{0:T(1024)S(1)}, bf16[16384,512]{1,0:T(8,128)(2,1)S(1)}, bf16[64,16384]{1,0:T(8,128)(2,1)S(1)},...) custom-call(bf16[4,16384]{1,0:T(4,128)(2,1)} %refs_0_.2, f32[16384]{0:T(1024)} %refs_1_.1, ...), custom_call_target="tpu_custom_call" | custom-call | bytes 21168128 | tf_op jit(solution)/shard_map/pallas_call | solution.py:204
  12.7 3.5 %collective-permute-done.1.z2 = bf16[4,16384]{1,0:T(4,128)(2,1)S(1)} collective-permute-done((bf16[4,16384]{1,0:T(4,128)(2,1)}, bf16[4,16384]{1,0:T(4,128)(2,1)S(1)}, u32[]{:S(2)}, u32[]{:S(2)}) %collective-permute-start.1) | collective-permute-done | bytes 131104 | tf_op jit(solution)/shard_map/ppermute | solution.py:175
  16.2 0.6 shard_map.92
  16.8 1.6 %collective-permute-start.3 = (bf16[64,16,128]{2,1,0:T(8,128)(2,1)S(1)}, bf16[64,16,128]{2,1,0:T(8,128)(2,1)S(1)}, u32[]{:S(2)}, u32[]{:S(2)}) collective-permute-start(bf16[64,16,128]{2,1,0:T(8,128)(2,1)S(1)} %get-tuple-element.21.refs_4_), channel_id=1, source_target_pairs={{0,2},{1,3},{2,0},{3,1},{4,6},{5,7},{6,4},{7,5},{8,10},{9,11},{10,... | collective-permute-start | bytes 786440 | tf_op jit(solution)/shard_map/ppermute | solution.py:175
  18.4 1.5 %collective-permute-start.5 = (bf16[64,16,128]{2,1,0:T(8,128)(2,1)S(1)}, bf16[64,16,128]{2,1,0:T(8,128)(2,1)S(1)}, u32[]{:S(2)}, u32[]{:S(2)}) collective-permute-start(bf16[64,16,128]{2,1,0:T(8,128)(2,1)S(1)} %get-tuple-element.22.refs_6_), channel_id=1, source_target_pairs={{0,4},{1,5},{2,6},{3,7},{4,0},{5,1},{6,2},{7,3},{8,12},{9,13},{10,... | collective-permute-start | bytes 786440 | tf_op jit(solution)/shard_map/ppermute | solution.py:175
  20.4 0.5 collective-permute-start.10
  20.9 2.3 %collective-permute-done.3.refs_5_ = bf16[64,16,128]{2,1,0:T(8,128)(2,1)S(1)} collective-permute-done((bf16[64,16,128]{2,1,0:T(8,128)(2,1)S(1)}, bf16[64,16,128]{2,1,0:T(8,128)(2,1)S(1)}, u32[]{:S(2)}, u32[]{:S(2)}) %collective-permute-start.3) | collective-permute-done | bytes 262176 | tf_op jit(solution)/shard_map/ppermute | solution.py:175
  23.2 1.5 %collective-permute-start.4 = (bf16[64,16,128]{2,1,0:T(8,128)(2,1)S(1)}, bf16[64,16,128]{2,1,0:T(8,128)(2,1)S(1)}, u32[]{:S(2)}, u32[]{:S(2)}) collective-permute-start(bf16[64,16,128]{2,1,0:T(8,128)(2,1)S(1)} %collective-permute-done.3.refs_5_), channel_id=1, source_target_pairs={{0,4},{1,5},{2,6},{3,7},{4,0},{5,1},{6,2},{7,3},{8,12},{9,13},{10,... | collective-permute-start | bytes 786440 | tf_op jit(solution)/shard_map/ppermute | solution.py:175
  24.8 1.8 %collective-permute-done.5.refs_7_ = bf16[64,16,128]{2,1,0:T(8,128)(2,1)S(1)} collective-permute-done((bf16[64,16,128]{2,1,0:T(8,128)(2,1)S(1)}, bf16[64,16,128]{2,1,0:T(8,128)(2,1)S(1)}, u32[]{:S(2)}, u32[]{:S(2)}) %collective-permute-start.5) | collective-permute-done | bytes 262176 | tf_op jit(solution)/shard_map/ppermute | solution.py:175
  26.5 0.6 collective-permute-start.6
  27.2 5.0 %collective-permute-done.9.refs_8_ = bf16[64,16,128]{2,1,0:T(8,128)(2,1)S(1)} collective-permute-done((bf16[64,16,128]{2,1,0:T(8,128)(2,1)S(1)}, bf16[64,16,128]{2,1,0:T(8,128)(2,1)S(1)}, u32[]{:S(2)}, u32[]{:S(2)}) %collective-permute-start.9) | collective-permute-done | bytes 262176 | tf_op jit(solution)/shard_map/ppermute | solution.py:175
  32.1 0.5 collective-permute-start.15
  32.7 3.3 %collective-permute-done.4.refs_0_ = bf16[64,16,128]{2,1,0:T(8,128)(2,1)S(1)} collective-permute-done((bf16[64,16,128]{2,1,0:T(8,128)(2,1)S(1)}, bf16[64,16,128]{2,1,0:T(8,128)(2,1)S(1)}, u32[]{:S(2)}, u32[]{:S(2)}) %collective-permute-start.4) | collective-permute-done | bytes 262176 | tf_op jit(solution)/shard_map/ppermute | solution.py:175
  38.6 4.2 %shard_map.93 = bf16[32,24,128]{2,1,0:T(8,128)(2,1)S(1)} custom-call(bf16[64,16,128]{2,1,0:T(8,128)(2,1)S(1)} %collective-permute-done.4.refs_0_, bf16[64,16,128]{2,1,0:T(8,128)(2,1)S(1)} %collective-permute-done.6.refs_1_, bf16[64,16,128]{2,1,0:T(8,128)(2,1)S(1)} %collective-permute-done.7.refs_2_, bf16[64,16,128]{2,1,0:T(8,128)(2,1)S(1)} %collective-permute-done.8.refs_3_, ...), custom_call_target="tpu_custom_call" | custom-call | flops 2415919104 | bytes 23068672 | tf_op jit(solution)/shard_map/pallas_call | solution.py:313
  42.8 13.4 %all_to_all.5.received = bf16[32,24,128]{2,1,0:T(8,128)(2,1)S(1)} all-to-all(bf16[32,24,128]{2,1,0:T(8,128)(2,1)S(1)} %shard_map.93), channel_id=1, replica_groups=mesh['groups'=1,'wide'=32] {'wide'}, dimensions={0} | all-to-all | bytes 393216 | tf_op jit(solution)/shard_map/all_to_all | solution.py:458
  56.2 1.7 %shard_map.94.refs_1_ = bf16[512,128]{1,0:T(8,128)(2,1)S(1)} custom-call(bf16[32,24,128]{2,1,0:T(8,128)(2,1)S(1)} %all_to_all.5.received, bf16[4,8,128,128]{3,2,1,0:T(8,128)(2,1)S(1)} %get-tuple-element.26.keys, bf16[4,8,128,128]{3,2,1,0:T(8,128)(2,1)S(1)} %get-tuple-element.27.values, s32[4]{0:T(128)S(1)} %copy-done.1), custom_call_target="tpu_custom_call" | custom-call | flops 150000000 | bytes 3000000 | tf_op jit(solution)/shard_map/pallas_call | solution.py:426
  57.9 1.1 %collective-permute-start.16 = (bf16[512,128]{1,0:T(8,128)(2,1)S(1)}, bf16[512,128]{1,0:T(8,128)(2,1)S(1)}, u32[]{:S(2)}, u32[]{:S(2)}) collective-permute-start(bf16[512,128]{1,0:T(8,128)(2,1)S(1)} %shard_map.94.refs_1_), channel_id=1, source_target_pairs={{0,8},{1,9},{2,10},{3,11},{4,12},{5,13},{6,14},{7,15},{8,0},{9,1},... | collective-permute-start | bytes 393224 | tf_op jit(solution)/shard_map/ppermute | solution.py:175
  59.0 1.4 %collective-permute-start.17 = (bf16[512,128]{1,0:T(8,128)(2,1)S(1)}, bf16[512,128]{1,0:T(8,128)(2,1)S(1)}, u32[]{:S(2)}, u32[]{:S(2)}) collective-permute-start(bf16[512,128]{1,0:T(8,128)(2,1)S(1)} %shard_map.94.refs_1_), channel_id=1, source_target_pairs={{0,16},{1,17},{2,18},{3,19},{4,20},{5,21},{6,22},{7,23},{8,24},{9,... | collective-permute-start | bytes 393224 | tf_op jit(solution)/shard_map/ppermute | solution.py:175
  60.4 2.0 %collective-permute-start.18 = (bf16[512,128]{1,0:T(8,128)(2,1)S(1)}, bf16[512,128]{1,0:T(8,128)(2,1)S(1)}, u32[]{:S(2)}, u32[]{:S(2)}) collective-permute-start(bf16[512,128]{1,0:T(8,128)(2,1)S(1)} %shard_map.94.refs_1_), channel_id=1, source_target_pairs={{0,24},{1,25},{2,26},{3,27},{4,28},{5,29},{6,30},{7,31},{8,16},{9,... | collective-permute-start | bytes 393224 | tf_op jit(solution)/shard_map/ppermute | solution.py:175
  62.4 5.8 %shard_map.95 = (bf16[16384,512]{1,0:T(8,128)(2,1)S(1)}, bf16[512,128]{1,0:T(8,128)(2,1)S(1)}) custom-call(bf16[16384,512]{1,0:T(8,128)(2,1)} %refs_0_.3, bf16[512,128]{1,0:T(8,128)(2,1)S(1)} %shard_map.94.refs_1_), custom_call_target="tpu_custom_call" | custom-call | bytes 16908288 | tf_op jit(solution)/shard_map/pallas_call | solution.py:204
  68.2 3.7 %collective-permute-done.17.z2 = bf16[512,128]{1,0:T(8,128)(2,1)S(1)} collective-permute-done((bf16[512,128]{1,0:T(8,128)(2,1)S(1)}, bf16[512,128]{1,0:T(8,128)(2,1)S(1)}, u32[]{:S(2)}, u32[]{:S(2)}) %collective-permute-start.17) | collective-permute-done | bytes 131104 | tf_op jit(solution)/shard_map/ppermute | solution.py:175
  72.1 1.4 %collective-permute-start.21 = (bf16[64,16,128]{2,1,0:T(8,128)(2,1)S(1)}, bf16[64,16,128]{2,1,0:T(8,128)(2,1)S(1)}, u32[]{:S(2)}, u32[]{:S(2)}) collective-permute-start(bf16[64,16,128]{2,1,0:T(8,128)(2,1)S(1)} %get-tuple-element.30.refs_6_), channel_id=1, source_target_pairs={{0,4},{1,5},{2,6},{3,7},{4,0},{5,1},{6,2},{7,3},{8,12},{9,13},{10,... | collective-permute-start | bytes 786440 | tf_op jit(solution)/shard_map/ppermute | solution.py:175
  73.5 0.7 collective-permute-start.25
  74.2 1.9 %collective-permute-start.26 = (bf16[64,16,128]{2,1,0:T(8,128)(2,1)S(1)}, bf16[64,16,128]{2,1,0:T(8,128)(2,1)S(1)}, u32[]{:S(2)}, u32[]{:S(2)}) collective-permute-start(bf16[64,16,128]{2,1,0:T(8,128)(2,1)S(1)} %get-tuple-element.30.refs_6_), channel_id=1, source_target_pairs={{0,2},{1,3},{2,0},{3,1},{4,6},{5,7},{6,4},{7,5},{8,10},{9,11},{10,... | collective-permute-start | bytes 786440 | tf_op jit(solution)/shard_map/ppermute | solution.py:175
  76.1 5.0 %collective-permute-done.19.refs_5_ = bf16[64,16,128]{2,1,0:T(8,128)(2,1)S(1)} collective-permute-done((bf16[64,16,128]{2,1,0:T(8,128)(2,1)S(1)}, bf16[64,16,128]{2,1,0:T(8,128)(2,1)S(1)}, u32[]{:S(2)}, u32[]{:S(2)}) %collective-permute-start.19) | collective-permute-done | bytes 262176 | tf_op jit(solution)/shard_map/ppermute | solution.py:175
  81.4 1.9 %collective-permute-start.22 = (bf16[64,16,128]{2,1,0:T(8,128)(2,1)S(1)}, bf16[64,16,128]{2,1,0:T(8,128)(2,1)S(1)}, u32[]{:S(2)}, u32[]{:S(2)}) collective-permute-start(bf16[64,16,128]{2,1,0:T(8,128)(2,1)S(1)} %collective-permute-done.21.refs_7_), channel_id=1, source_target_pairs={{0,2},{1,3},{2,0},{3,1},{4,6},{5,7},{6,4},{7,5},{8,10},{9,11},{10,... | collective-permute-start | bytes 786440 | tf_op jit(solution)/shard_map/ppermute | solution.py:175
  83.3 3.7 %collective-permute-done.25.refs_8_ = bf16[64,16,128]{2,1,0:T(8,128)(2,1)S(1)} collective-permute-done((bf16[64,16,128]{2,1,0:T(8,128)(2,1)S(1)}, bf16[64,16,128]{2,1,0:T(8,128)(2,1)S(1)}, u32[]{:S(2)}, u32[]{:S(2)}) %collective-permute-start.25) | collective-permute-done | bytes 262176 | tf_op jit(solution)/shard_map/ppermute | solution.py:175
  87.5 3.0 %collective-permute-done.20.refs_0_ = bf16[64,16,128]{2,1,0:T(8,128)(2,1)S(1)} collective-permute-done((bf16[64,16,128]{2,1,0:T(8,128)(2,1)S(1)}, bf16[64,16,128]{2,1,0:T(8,128)(2,1)S(1)}, u32[]{:S(2)}, u32[]{:S(2)}) %collective-permute-start.20) | collective-permute-done | bytes 262176 | tf_op jit(solution)/shard_map/ppermute | solution.py:175
  91.5 0.9 collective-permute-done.30.refs_14_
  93.2 3.1 %shard_map.97 = bf16[128,512]{1,0:T(8,128)(2,1)} custom-call(bf16[64,16,128]{2,1,0:T(8,128)(2,1)S(1)} %collective-permute-done.20.refs_0_, bf16[64,16,128]{2,1,0:T(8,128)(2,1)S(1)} %collective-permute-done.22.refs_1_, bf16[64,16,128]{2,1,0:T(8,128)(2,1)S(1)} %collective-permute-done.23.refs_2_, bf16[64,16,128]{2,1,0:T(8,128)(2,1)S(1)} %collective-permute-done.24.refs_3_, ...), custom_call_target="tpu_custom_call" | custom-call | flops 2147483648 | bytes 20971520 | tf_op jit(solution)/shard_map/pallas_call | solution.py:313
  (44 shorter events, 5.9 us)
Async XLA Ops:
  0.0 12.7 %collective-permute-start = (bf16[4,16384]{1,0:T(4,128)(2,1)}, bf16[4,16384]{1,0:T(4,128)(2,1)S(1)}, u32[]{:S(2)}, u32[]{:S(2)}) collective-permute-start(bf16[4,16384]{1,0:T(4,128)(2,1)} %refs_0_.2), channel_id=1, source_target_pairs={{0,8},{1,9},{2,10},{3,11},{4,12},{5,13},{6,14},{7,15},{8,0},{9,1},... | collective-permute-start | bytes 393224 | tf_op jit(solution)/shard_map/ppermute | solution.py:175
  3.0 13.2 %collective-permute-start.1 = (bf16[4,16384]{1,0:T(4,128)(2,1)}, bf16[4,16384]{1,0:T(4,128)(2,1)S(1)}, u32[]{:S(2)}, u32[]{:S(2)}) collective-permute-start(bf16[4,16384]{1,0:T(4,128)(2,1)} %refs_0_.2), channel_id=1, source_target_pairs={{0,16},{1,17},{2,18},{3,19},{4,20},{5,21},{6,22},{7,23},{8,24},{9,... | collective-permute-start | bytes 393224 | tf_op jit(solution)/shard_map/ppermute | solution.py:175
  5.6 10.6 %collective-permute-start.2 = (bf16[4,16384]{1,0:T(4,128)(2,1)}, bf16[4,16384]{1,0:T(4,128)(2,1)S(1)}, u32[]{:S(2)}, u32[]{:S(2)}) collective-permute-start(bf16[4,16384]{1,0:T(4,128)(2,1)} %refs_0_.2), channel_id=1, source_target_pairs={{0,24},{1,25},{2,26},{3,27},{4,28},{5,29},{6,30},{7,31},{8,16},{9,... | collective-permute-start | bytes 393224 | tf_op jit(solution)/shard_map/ppermute | solution.py:175
  16.8 6.4 %collective-permute-start.3 = (bf16[64,16,128]{2,1,0:T(8,128)(2,1)S(1)}, bf16[64,16,128]{2,1,0:T(8,128)(2,1)S(1)}, u32[]{:S(2)}, u32[]{:S(2)}) collective-permute-start(bf16[64,16,128]{2,1,0:T(8,128)(2,1)S(1)} %get-tuple-element.21.refs_4_), channel_id=1, source_target_pairs={{0,2},{1,3},{2,0},{3,1},{4,6},{5,7},{6,4},{7,5},{8,10},{9,11},{10,... | collective-permute-start | bytes 786440 | tf_op jit(solution)/shard_map/ppermute | solution.py:175
  18.4 8.2 %collective-permute-start.5 = (bf16[64,16,128]{2,1,0:T(8,128)(2,1)S(1)}, bf16[64,16,128]{2,1,0:T(8,128)(2,1)S(1)}, u32[]{:S(2)}, u32[]{:S(2)}) collective-permute-start(bf16[64,16,128]{2,1,0:T(8,128)(2,1)S(1)} %get-tuple-element.22.refs_6_), channel_id=1, source_target_pairs={{0,4},{1,5},{2,6},{3,7},{4,0},{5,1},{6,2},{7,3},{8,12},{9,13},{10,... | collective-permute-start | bytes 786440 | tf_op jit(solution)/shard_map/ppermute | solution.py:175
  19.9 16.6 %collective-permute-start.11 = (bf16[128,16,128]{2,1,0:T(8,128)(2,1)S(1)}, bf16[128,16,128]{2,1,0:T(8,128)(2,1)S(1)}, u32[]{:S(2)}, u32[]{:S(2)}) collective-permute-start(bf16[128,16,128]{2,1,0:T(8,128)(2,1)S(1)} %get-tuple-element.23), channel_id=1, source_target_pairs={{0,1},{1,0},{2,3},{3,2},{4,5},{5,4},{6,7},{7,6},{8,9},{9,8},{10,11... | collective-permute-start | bytes 1572872 | tf_op jit(solution)/shard_map/ppermute | solution.py:175
  19.9 12.3 %collective-permute-start.9 = (bf16[64,16,128]{2,1,0:T(8,128)(2,1)S(1)}, bf16[64,16,128]{2,1,0:T(8,128)(2,1)S(1)}, u32[]{:S(2)}, u32[]{:S(2)}) collective-permute-start(bf16[64,16,128]{2,1,0:T(8,128)(2,1)S(1)} %get-tuple-element.21.refs_4_), channel_id=1, source_target_pairs={{0,4},{1,5},{2,6},{3,7},{4,0},{5,1},{6,2},{7,3},{8,12},{9,13},{10,... | collective-permute-start | bytes 786440 | tf_op jit(solution)/shard_map/ppermute | solution.py:175
  20.4 11.8 %collective-permute-start.10 = (bf16[64,16,128]{2,1,0:T(8,128)(2,1)S(1)}, bf16[64,16,128]{2,1,0:T(8,128)(2,1)S(1)}, u32[]{:S(2)}, u32[]{:S(2)}) collective-permute-start(bf16[64,16,128]{2,1,0:T(8,128)(2,1)S(1)} %get-tuple-element.22.refs_6_), channel_id=1, source_target_pairs={{0,2},{1,3},{2,0},{3,1},{4,6},{5,7},{6,4},{7,5},{8,10},{9,11},{10,... | collective-permute-start | bytes 786440 | tf_op jit(solution)/shard_map/ppermute | solution.py:175
  23.2 12.7 %collective-permute-start.4 = (bf16[64,16,128]{2,1,0:T(8,128)(2,1)S(1)}, bf16[64,16,128]{2,1,0:T(8,128)(2,1)S(1)}, u32[]{:S(2)}, u32[]{:S(2)}) collective-permute-start(bf16[64,16,128]{2,1,0:T(8,128)(2,1)S(1)} %collective-permute-done.3.refs_5_), channel_id=1, source_target_pairs={{0,4},{1,5},{2,6},{3,7},{4,0},{5,1},{6,2},{7,3},{8,12},{9,13},{10,... | collective-permute-start | bytes 786440 | tf_op jit(solution)/shard_map/ppermute | solution.py:175
  26.5 9.4 %collective-permute-start.6 = (bf16[64,16,128]{2,1,0:T(8,128)(2,1)S(1)}, bf16[64,16,128]{2,1,0:T(8,128)(2,1)S(1)}, u32[]{:S(2)}, u32[]{:S(2)}) collective-permute-start(bf16[64,16,128]{2,1,0:T(8,128)(2,1)S(1)} %collective-permute-done.5.refs_7_), channel_id=1, source_target_pairs={{0,2},{1,3},{2,0},{3,1},{4,6},{5,7},{6,4},{7,5},{8,10},{9,11},{10,... | collective-permute-start | bytes 786440 | tf_op jit(solution)/shard_map/ppermute | solution.py:175
  32.1 4.4 %collective-permute-start.12 = (bf16[64,16,128]{2,1,0:T(8,128)(2,1)S(1)}, bf16[64,16,128]{2,1,0:T(8,128)(2,1)S(1)}, u32[]{:S(2)}, u32[]{:S(2)}) collective-permute-start(bf16[64,16,128]{2,1,0:T(8,128)(2,1)S(1)} %collective-permute-done.3.refs_5_), channel_id=1, source_target_pairs={{0,1},{1,0},{2,3},{3,2},{4,5},{5,4},{6,7},{7,6},{8,9},{9,8},{10,11... | collective-permute-start | bytes 786440 | tf_op jit(solution)/shard_map/ppermute | solution.py:175
  32.1 5.7 %collective-permute-start.15 = (bf16[64,16,128]{2,1,0:T(8,128)(2,1)S(1)}, bf16[64,16,128]{2,1,0:T(8,128)(2,1)S(1)}, u32[]{:S(2)}, u32[]{:S(2)}) collective-permute-start(bf16[64,16,128]{2,1,0:T(8,128)(2,1)S(1)} %collective-permute-done.5.refs_7_), channel_id=1, source_target_pairs={{0,1},{1,0},{2,3},{3,2},{4,5},{5,4},{6,7},{7,6},{8,9},{9,8},{10,11... | collective-permute-start | bytes 786440 | tf_op jit(solution)/shard_map/ppermute | solution.py:175
  36.0 1.5 %collective-permute-start.13 = (bf16[64,16,128]{2,1,0:T(8,128)(2,1)S(1)}, bf16[64,16,128]{2,1,0:T(8,128)(2,1)S(1)}, u32[]{:S(2)}, u32[]{:S(2)}) collective-permute-start(bf16[64,16,128]{2,1,0:T(8,128)(2,1)S(1)} %collective-permute-done.9.refs_8_), channel_id=1, source_target_pairs={{0,1},{1,0},{2,3},{3,2},{4,5},{5,4},{6,7},{7,6},{8,9},{9,8},{10,11... | collective-permute-start | bytes 786440 | tf_op jit(solution)/shard_map/ppermute | solution.py:175
  36.0 1.9 %collective-permute-start.14 = (bf16[64,16,128]{2,1,0:T(8,128)(2,1)S(1)}, bf16[64,16,128]{2,1,0:T(8,128)(2,1)S(1)}, u32[]{:S(2)}, u32[]{:S(2)}) collective-permute-start(bf16[64,16,128]{2,1,0:T(8,128)(2,1)S(1)} %collective-permute-done.10.refs_9_), channel_id=1, source_target_pairs={{0,1},{1,0},{2,3},{3,2},{4,5},{5,4},{6,7},{7,6},{8,9},{9,8},{10,11... | collective-permute-start | bytes 786440 | tf_op jit(solution)/shard_map/ppermute | solution.py:175
  36.5 1.8 %collective-permute-start.7 = (bf16[64,16,128]{2,1,0:T(8,128)(2,1)S(1)}, bf16[64,16,128]{2,1,0:T(8,128)(2,1)S(1)}, u32[]{:S(2)}, u32[]{:S(2)}) collective-permute-start(bf16[64,16,128]{2,1,0:T(8,128)(2,1)S(1)} %collective-permute-done.4.refs_0_), channel_id=1, source_target_pairs={{0,1},{1,0},{2,3},{3,2},{4,5},{5,4},{6,7},{7,6},{8,9},{9,8},{10,11... | collective-permute-start | bytes 786440 | tf_op jit(solution)/shard_map/ppermute | solution.py:175
  36.6 2.1 %collective-permute-start.8 = (bf16[64,16,128]{2,1,0:T(8,128)(2,1)S(1)}, bf16[64,16,128]{2,1,0:T(8,128)(2,1)S(1)}, u32[]{:S(2)}, u32[]{:S(2)}) collective-permute-start(bf16[64,16,128]{2,1,0:T(8,128)(2,1)S(1)} %collective-permute-done.6.refs_1_), channel_id=1, source_target_pairs={{0,1},{1,0},{2,3},{3,2},{4,5},{5,4},{6,7},{7,6},{8,9},{9,8},{10,11... | collective-permute-start | bytes 786440 | tf_op jit(solution)/shard_map/ppermute | solution.py:175
  57.9 10.3 %collective-permute-start.16 = (bf16[512,128]{1,0:T(8,128)(2,1)S(1)}, bf16[512,128]{1,0:T(8,128)(2,1)S(1)}, u32[]{:S(2)}, u32[]{:S(2)}) collective-permute-start(bf16[512,128]{1,0:T(8,128)(2,1)S(1)} %shard_map.94.refs_1_), channel_id=1, source_target_pairs={{0,8},{1,9},{2,10},{3,11},{4,12},{5,13},{6,14},{7,15},{8,0},{9,1},... | collective-permute-start | bytes 393224 | tf_op jit(solution)/shard_map/ppermute | solution.py:175
  59.0 12.8 %collective-permute-start.17 = (bf16[512,128]{1,0:T(8,128)(2,1)S(1)}, bf16[512,128]{1,0:T(8,128)(2,1)S(1)}, u32[]{:S(2)}, u32[]{:S(2)}) collective-permute-start(bf16[512,128]{1,0:T(8,128)(2,1)S(1)} %shard_map.94.refs_1_), channel_id=1, source_target_pairs={{0,16},{1,17},{2,18},{3,19},{4,20},{5,21},{6,22},{7,23},{8,24},{9,... | collective-permute-start | bytes 393224 | tf_op jit(solution)/shard_map/ppermute | solution.py:175
  60.4 11.5 %collective-permute-start.18 = (bf16[512,128]{1,0:T(8,128)(2,1)S(1)}, bf16[512,128]{1,0:T(8,128)(2,1)S(1)}, u32[]{:S(2)}, u32[]{:S(2)}) collective-permute-start(bf16[512,128]{1,0:T(8,128)(2,1)S(1)} %shard_map.94.refs_1_), channel_id=1, source_target_pairs={{0,24},{1,25},{2,26},{3,27},{4,28},{5,29},{6,30},{7,31},{8,16},{9,... | collective-permute-start | bytes 393224 | tf_op jit(solution)/shard_map/ppermute | solution.py:175
  72.0 9.2 %collective-permute-start.19 = (bf16[64,16,128]{2,1,0:T(8,128)(2,1)S(1)}, bf16[64,16,128]{2,1,0:T(8,128)(2,1)S(1)}, u32[]{:S(2)}, u32[]{:S(2)}) collective-permute-start(bf16[64,16,128]{2,1,0:T(8,128)(2,1)S(1)} %get-tuple-element.29.refs_4_), channel_id=1, source_target_pairs={{0,2},{1,3},{2,0},{3,1},{4,6},{5,7},{6,4},{7,5},{8,10},{9,11},{10,... | collective-permute-start | bytes 786440 | tf_op jit(solution)/shard_map/ppermute | solution.py:175
  72.1 9.3 %collective-permute-start.21 = (bf16[64,16,128]{2,1,0:T(8,128)(2,1)S(1)}, bf16[64,16,128]{2,1,0:T(8,128)(2,1)S(1)}, u32[]{:S(2)}, u32[]{:S(2)}) collective-permute-start(bf16[64,16,128]{2,1,0:T(8,128)(2,1)S(1)} %get-tuple-element.30.refs_6_), channel_id=1, source_target_pairs={{0,4},{1,5},{2,6},{3,7},{4,0},{5,1},{6,2},{7,3},{8,12},{9,13},{10,... | collective-permute-start | bytes 786440 | tf_op jit(solution)/shard_map/ppermute | solution.py:175
  73.5 13.5 %collective-permute-start.25 = (bf16[64,16,128]{2,1,0:T(8,128)(2,1)S(1)}, bf16[64,16,128]{2,1,0:T(8,128)(2,1)S(1)}, u32[]{:S(2)}, u32[]{:S(2)}) collective-permute-start(bf16[64,16,128]{2,1,0:T(8,128)(2,1)S(1)} %get-tuple-element.29.refs_4_), channel_id=1, source_target_pairs={{0,4},{1,5},{2,6},{3,7},{4,0},{5,1},{6,2},{7,3},{8,12},{9,13},{10,... | collective-permute-start | bytes 786440 | tf_op jit(solution)/shard_map/ppermute | solution.py:175
  74.2 12.8 %collective-permute-start.26 = (bf16[64,16,128]{2,1,0:T(8,128)(2,1)S(1)}, bf16[64,16,128]{2,1,0:T(8,128)(2,1)S(1)}, u32[]{:S(2)}, u32[]{:S(2)}) collective-permute-start(bf16[64,16,128]{2,1,0:T(8,128)(2,1)S(1)} %get-tuple-element.30.refs_6_), channel_id=1, source_target_pairs={{0,2},{1,3},{2,0},{3,1},{4,6},{5,7},{6,4},{7,5},{8,10},{9,11},{10,... | collective-permute-start | bytes 786440 | tf_op jit(solution)/shard_map/ppermute | solution.py:175
  76.1 16.3 %collective-permute-start.27 = (bf16[128,16,128]{2,1,0:T(8,128)(2,1)S(1)}, bf16[128,16,128]{2,1,0:T(8,128)(2,1)S(1)}, u32[]{:S(2)}, u32[]{:S(2)}) collective-permute-start(bf16[128,16,128]{2,1,0:T(8,128)(2,1)S(1)} %get-tuple-element.31), channel_id=1, source_target_pairs={{0,1},{1,0},{2,3},{3,2},{4,5},{5,4},{6,7},{7,6},{8,9},{9,8},{10,11... | collective-permute-start | bytes 1572872 | tf_op jit(solution)/shard_map/ppermute | solution.py:175
  81.2 9.4 %collective-permute-start.20 = (bf16[64,16,128]{2,1,0:T(8,128)(2,1)S(1)}, bf16[64,16,128]{2,1,0:T(8,128)(2,1)S(1)}, u32[]{:S(2)}, u32[]{:S(2)}) collective-permute-start(bf16[64,16,128]{2,1,0:T(8,128)(2,1)S(1)} %collective-permute-done.19.refs_5_), channel_id=1, source_target_pairs={{0,4},{1,5},{2,6},{3,7},{4,0},{5,1},{6,2},{7,3},{8,12},{9,13},{10,... | collective-permute-start | bytes 786440 | tf_op jit(solution)/shard_map/ppermute | solution.py:175
  81.4 9.1 %collective-permute-start.22 = (bf16[64,16,128]{2,1,0:T(8,128)(2,1)S(1)}, bf16[64,16,128]{2,1,0:T(8,128)(2,1)S(1)}, u32[]{:S(2)}, u32[]{:S(2)}) collective-permute-start(bf16[64,16,128]{2,1,0:T(8,128)(2,1)S(1)} %collective-permute-done.21.refs_7_), channel_id=1, source_target_pairs={{0,2},{1,3},{2,0},{3,1},{4,6},{5,7},{6,4},{7,5},{8,10},{9,11},{10,... | collective-permute-start | bytes 786440 | tf_op jit(solution)/shard_map/ppermute | solution.py:175
  87.0 4.0 %collective-permute-start.28 = (bf16[64,16,128]{2,1,0:T(8,128)(2,1)S(1)}, bf16[64,16,128]{2,1,0:T(8,128)(2,1)S(1)}, u32[]{:S(2)}, u32[]{:S(2)}) collective-permute-start(bf16[64,16,128]{2,1,0:T(8,128)(2,1)S(1)} %collective-permute-done.19.refs_5_), channel_id=1, source_target_pairs={{0,1},{1,0},{2,3},{3,2},{4,5},{5,4},{6,7},{7,6},{8,9},{9,8},{10,11... | collective-permute-start | bytes 786440 | tf_op jit(solution)/shard_map/ppermute | solution.py:175
  87.0 4.1 %collective-permute-start.29 = (bf16[64,16,128]{2,1,0:T(8,128)(2,1)S(1)}, bf16[64,16,128]{2,1,0:T(8,128)(2,1)S(1)}, u32[]{:S(2)}, u32[]{:S(2)}) collective-permute-start(bf16[64,16,128]{2,1,0:T(8,128)(2,1)S(1)} %collective-permute-done.25.refs_8_), channel_id=1, source_target_pairs={{0,1},{1,0},{2,3},{3,2},{4,5},{5,4},{6,7},{7,6},{8,9},{9,8},{10,11... | collective-permute-start | bytes 786440 | tf_op jit(solution)/shard_map/ppermute | solution.py:175
  90.5 1.9 %collective-permute-start.31 = (bf16[64,16,128]{2,1,0:T(8,128)(2,1)S(1)}, bf16[64,16,128]{2,1,0:T(8,128)(2,1)S(1)}, u32[]{:S(2)}, u32[]{:S(2)}) collective-permute-start(bf16[64,16,128]{2,1,0:T(8,128)(2,1)S(1)} %collective-permute-done.21.refs_7_), channel_id=1, source_target_pairs={{0,1},{1,0},{2,3},{3,2},{4,5},{5,4},{6,7},{7,6},{8,9},{9,8},{10,11... | collective-permute-start | bytes 786440 | tf_op jit(solution)/shard_map/ppermute | solution.py:175
  90.5 1.9 %collective-permute-start.30 = (bf16[64,16,128]{2,1,0:T(8,128)(2,1)S(1)}, bf16[64,16,128]{2,1,0:T(8,128)(2,1)S(1)}, u32[]{:S(2)}, u32[]{:S(2)}) collective-permute-start(bf16[64,16,128]{2,1,0:T(8,128)(2,1)S(1)} %collective-permute-done.26.refs_9_), channel_id=1, source_target_pairs={{0,1},{1,0},{2,3},{3,2},{4,5},{5,4},{6,7},{7,6},{8,9},{9,8},{10,11... | collective-permute-start | bytes 786440 | tf_op jit(solution)/shard_map/ppermute | solution.py:175
  91.0 1.8 %collective-permute-start.23 = (bf16[64,16,128]{2,1,0:T(8,128)(2,1)S(1)}, bf16[64,16,128]{2,1,0:T(8,128)(2,1)S(1)}, u32[]{:S(2)}, u32[]{:S(2)}) collective-permute-start(bf16[64,16,128]{2,1,0:T(8,128)(2,1)S(1)} %collective-permute-done.20.refs_0_), channel_id=1, source_target_pairs={{0,1},{1,0},{2,3},{3,2},{4,5},{5,4},{6,7},{7,6},{8,9},{9,8},{10,11... | collective-permute-start | bytes 786440 | tf_op jit(solution)/shard_map/ppermute | solution.py:175
  91.1 2.1 %collective-permute-start.24 = (bf16[64,16,128]{2,1,0:T(8,128)(2,1)S(1)}, bf16[64,16,128]{2,1,0:T(8,128)(2,1)S(1)}, u32[]{:S(2)}, u32[]{:S(2)}) collective-permute-start(bf16[64,16,128]{2,1,0:T(8,128)(2,1)S(1)} %collective-permute-done.22.refs_1_), channel_id=1, source_target_pairs={{0,1},{1,0},{2,3},{3,2},{4,5},{5,4},{6,7},{7,6},{8,9},{9,8},{10,11... | collective-permute-start | bytes 786440 | tf_op jit(solution)/shard_map/ppermute | solution.py:175
  (2 other events, 82.2 us)

commit v7 on v5

--- a/solution.py
+++ b/solution.py
@@ -184,7 +184,12 @@
     x_high, y_low = swap(high, 2), swap(low, 4)
     other = swap(full, 1)
     mine = [(low, high), (x_low, x_high), (y_low, y_high), (d_low, d_high)]
-    theirs = [(swap(a, 1), swap(b, 1)) for a, b in mine[1:]]
+    other, x_late, y_late = lax.optimization_barrier((other, x_high, y_low))
+    theirs = [
+        (swap(x_low, 1), swap(x_late, 1)),
+        (swap(y_late, 1), swap(y_high, 1)),
+        (swap(d_low, 1), swap(d_high, 1)),
+    ]
     return mine, other, theirs
 
 

time: 96.7 us -> 100 us (1.034)
  waiting for transfers between devices: 34.7 us -> 39.5 us
    ppermute x32, waiting for transfers between devices: 34.7 us -> 39.5 us  [swapped(): return lax.ppermute(array, 'wide', [(i, i ^ mask) for i in range(devices)])]
where the time goes in v7:
time: 100 us
  waiting for transfers between devices  39.5 us (40%)
  starting transfers between devices  25.5 us (26%)
  Pallas kernels  22.2 us (22%)
  blocking collectives  12.6 us (13%)
    ppermute x32, waiting for transfers between devices, swapped(): return lax.ppermute(array, 'wide', [(i, i ^ mask) for i in range(devices)])  39.5 us
    ppermute x32, starting transfers between devices, swapped(): return lax.ppermute(array, 'wide', [(i, i ^ mask) for i in range(devices)])  25.5 us
    pallas_call x2, Pallas kernels, prefetch(): pl.pallas_call(prefetch_kernel, in_specs=[pl.BlockSpec(memory_space=pltpu...  12.8 us
    all_to_all x1, blocking collectives, on_block(): lax.all_to_all(local, 'wide', split_axis=0, concat_axis=0, tiled=True)  12.6 us
    pallas_call x2, Pallas kernels, project(): pl.pallas_call(kernel, in_specs=[whole] * len(operands), out_specs=whole,...  6.91 us
  transfers between devices with their start and end apart: 32, of which 17 were waited for; matrix products, arithmetic and copies ran while one was open for 0% of the time, Pallas kernels for 13%

profile of v7, /device:TPU:0, one launch (start us, length us, event | category | flops | bytes accessed | tf_op | source)
XLA Modules:
  0.0 100.0 jit_solution(4557977805992750732)
XLA Ops:
  0.0 3.0 %collective-permute-start = (bf16[4,16384]{1,0:T(4,128)(2,1)}, bf16[4,16384]{1,0:T(4,128)(2,1)S(1)}, u32[]{:S(2)}, u32[]{:S(2)}) collective-permute-start(bf16[4,16384]{1,0:T(4,128)(2,1)} %refs_0_.2), channel_id=1, source_target_pairs={{0,8},{1,9},{2,10},{3,11},{4,12},{5,13},{6,14},{7,15},{8,0},{9,1},... | collective-permute-start | bytes 393224 | tf_op jit(solution)/shard_map/ppermute | solution.py:175
  3.0 2.5 %collective-permute-start.2 = (bf16[4,16384]{1,0:T(4,128)(2,1)}, bf16[4,16384]{1,0:T(4,128)(2,1)S(1)}, u32[]{:S(2)}, u32[]{:S(2)}) collective-permute-start(bf16[4,16384]{1,0:T(4,128)(2,1)} %refs_0_.2), channel_id=1, source_target_pairs={{0,24},{1,25},{2,26},{3,27},{4,28},{5,29},{6,30},{7,31},{8,16},{9,... | collective-permute-start | bytes 393224 | tf_op jit(solution)/shard_map/ppermute | solution.py:175
  5.6 7.1 %shard_map.91 = (bf16[4,16384]{1,0:T(4,128)(2,1)S(1)}, f32[16384]{0:T(1024)S(1)}, bf16[16384,512]{1,0:T(8,128)(2,1)S(1)}, bf16[64,16384]{1,0:T(8,128)(2,1)S(1)},...) custom-call(bf16[4,16384]{1,0:T(4,128)(2,1)} %refs_0_.2, f32[16384]{0:T(1024)} %refs_1_.1, ...), custom_call_target="tpu_custom_call" | custom-call | bytes 21168128 | tf_op jit(solution)/shard_map/pallas_call | solution.py:209
  13.0 4.5 %collective-permute-done.1.z2 = bf16[4,16384]{1,0:T(4,128)(2,1)S(1)} collective-permute-done((bf16[4,16384]{1,0:T(4,128)(2,1)}, bf16[4,16384]{1,0:T(4,128)(2,1)S(1)}, u32[]{:S(2)}, u32[]{:S(2)}) %collective-permute-start.1) | collective-permute-done | bytes 131104 | tf_op jit(solution)/shard_map/ppermute | solution.py:175
  17.5 0.6 shard_map.92
  18.2 1.6 %collective-permute-start.3 = (bf16[64,16,128]{2,1,0:T(8,128)(2,1)S(1)}, bf16[64,16,128]{2,1,0:T(8,128)(2,1)S(1)}, u32[]{:S(2)}, u32[]{:S(2)}) collective-permute-start(bf16[64,16,128]{2,1,0:T(8,128)(2,1)S(1)} %get-tuple-element.27.refs_4_), channel_id=1, source_target_pairs={{0,2},{1,3},{2,0},{3,1},{4,6},{5,7},{6,4},{7,5},{8,10},{9,11},{10,... | collective-permute-start | bytes 786440 | tf_op jit(solution)/shard_map/ppermute | solution.py:175
  19.7 1.6 %collective-permute-start.5 = (bf16[64,16,128]{2,1,0:T(8,128)(2,1)S(1)}, bf16[64,16,128]{2,1,0:T(8,128)(2,1)S(1)}, u32[]{:S(2)}, u32[]{:S(2)}) collective-permute-start(bf16[64,16,128]{2,1,0:T(8,128)(2,1)S(1)} %get-tuple-element.28.refs_6_), channel_id=1, source_target_pairs={{0,4},{1,5},{2,6},{3,7},{4,0},{5,1},{6,2},{7,3},{8,12},{9,13},{10,... | collective-permute-start | bytes 786440 | tf_op jit(solution)/shard_map/ppermute | solution.py:175
  21.8 0.5 collective-permute-start.10
  22.3 5.1 %collective-permute-done.3.refs_5_ = bf16[64,16,128]{2,1,0:T(8,128)(2,1)S(1)} collective-permute-done((bf16[64,16,128]{2,1,0:T(8,128)(2,1)S(1)}, bf16[64,16,128]{2,1,0:T(8,128)(2,1)S(1)}, u32[]{:S(2)}, u32[]{:S(2)}) %collective-permute-start.3) | collective-permute-done | bytes 262176 | tf_op jit(solution)/shard_map/ppermute | solution.py:175
  27.4 1.5 %collective-permute-start.4 = (bf16[64,16,128]{2,1,0:T(8,128)(2,1)S(1)}, bf16[64,16,128]{2,1,0:T(8,128)(2,1)S(1)}, u32[]{:S(2)}, u32[]{:S(2)}) collective-permute-start(bf16[64,16,128]{2,1,0:T(8,128)(2,1)S(1)} %collective-permute-done.3.refs_5_), channel_id=1, source_target_pairs={{0,4},{1,5},{2,6},{3,7},{4,0},{5,1},{6,2},{7,3},{8,12},{9,13},{10,... | collective-permute-start | bytes 786440 | tf_op jit(solution)/shard_map/ppermute | solution.py:175
  28.9 1.5 %collective-permute-start.6 = (bf16[64,16,128]{2,1,0:T(8,128)(2,1)S(1)}, bf16[64,16,128]{2,1,0:T(8,128)(2,1)S(1)}, u32[]{:S(2)}, u32[]{:S(2)}) collective-permute-start(bf16[64,16,128]{2,1,0:T(8,128)(2,1)S(1)} %collective-permute-done.5.refs_7_), channel_id=1, source_target_pairs={{0,2},{1,3},{2,0},{3,1},{4,6},{5,7},{6,4},{7,5},{8,10},{9,11},{10,... | collective-permute-start | bytes 786440 | tf_op jit(solution)/shard_map/ppermute | solution.py:175
  30.4 4.1 %collective-permute-done.9.refs_8_ = bf16[64,16,128]{2,1,0:T(8,128)(2,1)S(1)} collective-permute-done((bf16[64,16,128]{2,1,0:T(8,128)(2,1)S(1)}, bf16[64,16,128]{2,1,0:T(8,128)(2,1)S(1)}, u32[]{:S(2)}, u32[]{:S(2)}) %collective-permute-start.9) | collective-permute-done | bytes 262176 | tf_op jit(solution)/shard_map/ppermute | solution.py:175
  35.1 4.3 %collective-permute-done.4.refs_0_ = bf16[64,16,128]{2,1,0:T(8,128)(2,1)S(1)} collective-permute-done((bf16[64,16,128]{2,1,0:T(8,128)(2,1)S(1)}, bf16[64,16,128]{2,1,0:T(8,128)(2,1)S(1)}, u32[]{:S(2)}, u32[]{:S(2)}) %collective-permute-start.4) | collective-permute-done | bytes 262176 | tf_op jit(solution)/shard_map/ppermute | solution.py:175
  40.0 0.9 collective-permute-done.7.refs_2_
  41.7 3.8 %shard_map.93 = bf16[32,24,128]{2,1,0:T(8,128)(2,1)S(1)} custom-call(bf16[64,16,128]{2,1,0:T(8,128)(2,1)S(1)} %collective-permute-done.4.refs_0_, bf16[64,16,128]{2,1,0:T(8,128)(2,1)S(1)} %collective-permute-done.6.refs_1_, bf16[64,16,128]{2,1,0:T(8,128)(2,1)S(1)} %collective-permute-done.7.refs_2_, bf16[64,16,128]{2,1,0:T(8,128)(2,1)S(1)} %collective-permute-done.8.refs_3_, ...), custom_call_target="tpu_custom_call" | custom-call | flops 2415919104 | bytes 23068672 | tf_op jit(solution)/shard_map/pallas_call | solution.py:333
  45.4 12.6 %all_to_all.5.received = bf16[32,24,128]{2,1,0:T(8,128)(2,1)S(1)} all-to-all(bf16[32,24,128]{2,1,0:T(8,128)(2,1)S(1)} %shard_map.93), channel_id=1, replica_groups=mesh['groups'=1,'wide'=32] {'wide'}, dimensions={0} | all-to-all | bytes 393216 | tf_op jit(solution)/shard_map/all_to_all | solution.py:479
  58.1 1.7 %shard_map.94.refs_1_ = bf16[512,128]{1,0:T(8,128)(2,1)S(1)} custom-call(bf16[32,24,128]{2,1,0:T(8,128)(2,1)S(1)} %all_to_all.5.received, bf16[4,8,128,128]{3,2,1,0:T(8,128)(2,1)S(1)} %get-tuple-element.35.keys, bf16[4,8,128,128]{3,2,1,0:T(8,128)(2,1)S(1)} %get-tuple-element.36.values, s32[4]{0:T(128)S(1)} %copy-done.1), custom_call_target="tpu_custom_call" | custom-call | flops 150000000 | bytes 3000000 | tf_op jit(solution)/shard_map/pallas_call | solution.py:447
  59.8 1.9 %collective-permute-start.18 = (bf16[512,128]{1,0:T(8,128)(2,1)S(1)}, bf16[512,128]{1,0:T(8,128)(2,1)S(1)}, u32[]{:S(2)}, u32[]{:S(2)}) collective-permute-start(bf16[512,128]{1,0:T(8,128)(2,1)S(1)} %shard_map.94.refs_1_), channel_id=1, source_target_pairs={{0,24},{1,25},{2,26},{3,27},{4,28},{5,29},{6,30},{7,31},{8,16},{9,... | collective-permute-start | bytes 393224 | tf_op jit(solution)/shard_map/ppermute | solution.py:175
  61.7 0.7 collective-permute-start.17
  62.3 1.9 %collective-permute-start.16 = (bf16[512,128]{1,0:T(8,128)(2,1)S(1)}, bf16[512,128]{1,0:T(8,128)(2,1)S(1)}, u32[]{:S(2)}, u32[]{:S(2)}) collective-permute-start(bf16[512,128]{1,0:T(8,128)(2,1)S(1)} %shard_map.94.refs_1_), channel_id=1, source_target_pairs={{0,8},{1,9},{2,10},{3,11},{4,12},{5,13},{6,14},{7,15},{8,0},{9,1},... | collective-permute-start | bytes 393224 | tf_op jit(solution)/shard_map/ppermute | solution.py:175
  64.2 5.8 %shard_map.95 = (bf16[16384,512]{1,0:T(8,128)(2,1)S(1)}, bf16[512,128]{1,0:T(8,128)(2,1)S(1)}) custom-call(bf16[16384,512]{1,0:T(8,128)(2,1)} %refs_0_.3, bf16[512,128]{1,0:T(8,128)(2,1)S(1)} %shard_map.94.refs_1_), custom_call_target="tpu_custom_call" | custom-call | bytes 16908288 | tf_op jit(solution)/shard_map/pallas_call | solution.py:209
  70.0 3.7 %collective-permute-done.17.z2 = bf16[512,128]{1,0:T(8,128)(2,1)S(1)} collective-permute-done((bf16[512,128]{1,0:T(8,128)(2,1)S(1)}, bf16[512,128]{1,0:T(8,128)(2,1)S(1)}, u32[]{:S(2)}, u32[]{:S(2)}) %collective-permute-start.17) | collective-permute-done | bytes 131104 | tf_op jit(solution)/shard_map/ppermute | solution.py:175
  73.9 1.2 %collective-permute-start.19 = (bf16[64,16,128]{2,1,0:T(8,128)(2,1)S(1)}, bf16[64,16,128]{2,1,0:T(8,128)(2,1)S(1)}, u32[]{:S(2)}, u32[]{:S(2)}) collective-permute-start(bf16[64,16,128]{2,1,0:T(8,128)(2,1)S(1)} %get-tuple-element.38.refs_4_), channel_id=1, source_target_pairs={{0,2},{1,3},{2,0},{3,1},{4,6},{5,7},{6,4},{7,5},{8,10},{9,11},{10,... | collective-permute-start | bytes 786440 | tf_op jit(solution)/shard_map/ppermute | solution.py:175
  75.6 1.5 %collective-permute-start.25 = (bf16[64,16,128]{2,1,0:T(8,128)(2,1)S(1)}, bf16[64,16,128]{2,1,0:T(8,128)(2,1)S(1)}, u32[]{:S(2)}, u32[]{:S(2)}) collective-permute-start(bf16[64,16,128]{2,1,0:T(8,128)(2,1)S(1)} %get-tuple-element.38.refs_4_), channel_id=1, source_target_pairs={{0,4},{1,5},{2,6},{3,7},{4,0},{5,1},{6,2},{7,3},{8,12},{9,13},{10,... | collective-permute-start | bytes 786440 | tf_op jit(solution)/shard_map/ppermute | solution.py:175
  77.1 0.9 collective-permute-start.26
  78.0 4.9 %collective-permute-done.19.refs_5_ = bf16[64,16,128]{2,1,0:T(8,128)(2,1)S(1)} collective-permute-done((bf16[64,16,128]{2,1,0:T(8,128)(2,1)S(1)}, bf16[64,16,128]{2,1,0:T(8,128)(2,1)S(1)}, u32[]{:S(2)}, u32[]{:S(2)}) %collective-permute-start.19) | collective-permute-done | bytes 262176 | tf_op jit(solution)/shard_map/ppermute | solution.py:175
  83.0 0.5 collective-permute-start.20
  83.5 0.8 collective-permute-done.21.refs_7_
  84.3 0.9 collective-permute-start.22
  85.2 4.7 %collective-permute-done.25.refs_8_ = bf16[64,16,128]{2,1,0:T(8,128)(2,1)S(1)} collective-permute-done((bf16[64,16,128]{2,1,0:T(8,128)(2,1)S(1)}, bf16[64,16,128]{2,1,0:T(8,128)(2,1)S(1)}, u32[]{:S(2)}, u32[]{:S(2)}) %collective-permute-start.25) | collective-permute-done | bytes 262176 | tf_op jit(solution)/shard_map/ppermute | solution.py:175
  90.5 3.7 %collective-permute-done.20.refs_0_ = bf16[64,16,128]{2,1,0:T(8,128)(2,1)S(1)} collective-permute-done((bf16[64,16,128]{2,1,0:T(8,128)(2,1)S(1)}, bf16[64,16,128]{2,1,0:T(8,128)(2,1)S(1)}, u32[]{:S(2)}, u32[]{:S(2)}) %collective-permute-start.20) | collective-permute-done | bytes 262176 | tf_op jit(solution)/shard_map/ppermute | solution.py:175
  96.8 3.1 %shard_map.97 = bf16[128,512]{1,0:T(8,128)(2,1)} custom-call(bf16[64,16,128]{2,1,0:T(8,128)(2,1)S(1)} %collective-permute-done.20.refs_0_, bf16[64,16,128]{2,1,0:T(8,128)(2,1)S(1)} %collective-permute-done.22.refs_1_, bf16[64,16,128]{2,1,0:T(8,128)(2,1)S(1)} %collective-permute-done.23.refs_2_, bf16[64,16,128]{2,1,0:T(8,128)(2,1)S(1)} %collective-permute-done.24.refs_3_, ...), custom_call_target="tpu_custom_call" | custom-call | flops 2147483648 | bytes 20971520 | tf_op jit(solution)/shard_map/pallas_call | solution.py:333
  (44 shorter events, 6.7 us)
Async XLA Ops:
  0.0 12.7 %collective-permute-start = (bf16[4,16384]{1,0:T(4,128)(2,1)}, bf16[4,16384]{1,0:T(4,128)(2,1)S(1)}, u32[]{:S(2)}, u32[]{:S(2)}) collective-permute-start(bf16[4,16384]{1,0:T(4,128)(2,1)} %refs_0_.2), channel_id=1, source_target_pairs={{0,8},{1,9},{2,10},{3,11},{4,12},{5,13},{6,14},{7,15},{8,0},{9,1},... | collective-permute-start | bytes 393224 | tf_op jit(solution)/shard_map/ppermute | solution.py:175
  3.0 10.0 %collective-permute-start.2 = (bf16[4,16384]{1,0:T(4,128)(2,1)}, bf16[4,16384]{1,0:T(4,128)(2,1)S(1)}, u32[]{:S(2)}, u32[]{:S(2)}) collective-permute-start(bf16[4,16384]{1,0:T(4,128)(2,1)} %refs_0_.2), channel_id=1, source_target_pairs={{0,24},{1,25},{2,26},{3,27},{4,28},{5,29},{6,30},{7,31},{8,16},{9,... | collective-permute-start | bytes 393224 | tf_op jit(solution)/shard_map/ppermute | solution.py:175
  5.5 12.0 %collective-permute-start.1 = (bf16[4,16384]{1,0:T(4,128)(2,1)}, bf16[4,16384]{1,0:T(4,128)(2,1)S(1)}, u32[]{:S(2)}, u32[]{:S(2)}) collective-permute-start(bf16[4,16384]{1,0:T(4,128)(2,1)} %refs_0_.2), channel_id=1, source_target_pairs={{0,16},{1,17},{2,18},{3,19},{4,20},{5,21},{6,22},{7,23},{8,24},{9,... | collective-permute-start | bytes 393224 | tf_op jit(solution)/shard_map/ppermute | solution.py:175
  18.1 16.9 %collective-permute-start.11 = (bf16[128,16,128]{2,1,0:T(8,128)(2,1)S(1)}, bf16[128,16,128]{2,1,0:T(8,128)(2,1)S(1)}, u32[]{:S(2)}, u32[]{:S(2)}) collective-permute-start(bf16[128,16,128]{2,1,0:T(8,128)(2,1)S(1)} %get-tuple-element.29), channel_id=1, source_target_pairs={{0,1},{1,0},{2,3},{3,2},{4,5},{5,4},{6,7},{7,6},{8,9},{9,8},{10,11... | collective-permute-start | bytes 1572872 | tf_op jit(solution)/shard_map/ppermute | solution.py:175
  18.2 9.2 %collective-permute-start.3 = (bf16[64,16,128]{2,1,0:T(8,128)(2,1)S(1)}, bf16[64,16,128]{2,1,0:T(8,128)(2,1)S(1)}, u32[]{:S(2)}, u32[]{:S(2)}) collective-permute-start(bf16[64,16,128]{2,1,0:T(8,128)(2,1)S(1)} %get-tuple-element.27.refs_4_), channel_id=1, source_target_pairs={{0,2},{1,3},{2,0},{3,1},{4,6},{5,7},{6,4},{7,5},{8,10},{9,11},{10,... | collective-permute-start | bytes 786440 | tf_op jit(solution)/shard_map/ppermute | solution.py:175
  19.7 9.2 %collective-permute-start.5 = (bf16[64,16,128]{2,1,0:T(8,128)(2,1)S(1)}, bf16[64,16,128]{2,1,0:T(8,128)(2,1)S(1)}, u32[]{:S(2)}, u32[]{:S(2)}) collective-permute-start(bf16[64,16,128]{2,1,0:T(8,128)(2,1)S(1)} %get-tuple-element.28.refs_6_), channel_id=1, source_target_pairs={{0,4},{1,5},{2,6},{3,7},{4,0},{5,1},{6,2},{7,3},{8,12},{9,13},{10,... | collective-permute-start | bytes 786440 | tf_op jit(solution)/shard_map/ppermute | solution.py:175
  21.3 13.2 %collective-permute-start.9 = (bf16[64,16,128]{2,1,0:T(8,128)(2,1)S(1)}, bf16[64,16,128]{2,1,0:T(8,128)(2,1)S(1)}, u32[]{:S(2)}, u32[]{:S(2)}) collective-permute-start(bf16[64,16,128]{2,1,0:T(8,128)(2,1)S(1)} %get-tuple-element.27.refs_4_), channel_id=1, source_target_pairs={{0,4},{1,5},{2,6},{3,7},{4,0},{5,1},{6,2},{7,3},{8,12},{9,13},{10,... | collective-permute-start | bytes 786440 | tf_op jit(solution)/shard_map/ppermute | solution.py:175
  21.8 12.7 %collective-permute-start.10 = (bf16[64,16,128]{2,1,0:T(8,128)(2,1)S(1)}, bf16[64,16,128]{2,1,0:T(8,128)(2,1)S(1)}, u32[]{:S(2)}, u32[]{:S(2)}) collective-permute-start(bf16[64,16,128]{2,1,0:T(8,128)(2,1)S(1)} %get-tuple-element.28.refs_6_), channel_id=1, source_target_pairs={{0,2},{1,3},{2,0},{3,1},{4,6},{5,7},{6,4},{7,5},{8,10},{9,11},{10,... | collective-permute-start | bytes 786440 | tf_op jit(solution)/shard_map/ppermute | solution.py:175
  27.4 12.0 %collective-permute-start.4 = (bf16[64,16,128]{2,1,0:T(8,128)(2,1)S(1)}, bf16[64,16,128]{2,1,0:T(8,128)(2,1)S(1)}, u32[]{:S(2)}, u32[]{:S(2)}) collective-permute-start(bf16[64,16,128]{2,1,0:T(8,128)(2,1)S(1)} %collective-permute-done.3.refs_5_), channel_id=1, source_target_pairs={{0,4},{1,5},{2,6},{3,7},{4,0},{5,1},{6,2},{7,3},{8,12},{9,13},{10,... | collective-permute-start | bytes 786440 | tf_op jit(solution)/shard_map/ppermute | solution.py:175
  28.9 10.5 %collective-permute-start.6 = (bf16[64,16,128]{2,1,0:T(8,128)(2,1)S(1)}, bf16[64,16,128]{2,1,0:T(8,128)(2,1)S(1)}, u32[]{:S(2)}, u32[]{:S(2)}) collective-permute-start(bf16[64,16,128]{2,1,0:T(8,128)(2,1)S(1)} %collective-permute-done.5.refs_7_), channel_id=1, source_target_pairs={{0,2},{1,3},{2,0},{3,1},{4,6},{5,7},{6,4},{7,5},{8,10},{9,11},{10,... | collective-permute-start | bytes 786440 | tf_op jit(solution)/shard_map/ppermute | solution.py:175
  34.5 5.4 %collective-permute-start.12 = (bf16[64,16,128]{2,1,0:T(8,128)(2,1)S(1)}, bf16[64,16,128]{2,1,0:T(8,128)(2,1)S(1)}, u32[]{:S(2)}, u32[]{:S(2)}) collective-permute-start(bf16[64,16,128]{2,1,0:T(8,128)(2,1)S(1)} %collective-permute-done.3.refs_5_), channel_id=1, source_target_pairs={{0,1},{1,0},{2,3},{3,2},{4,5},{5,4},{6,7},{7,6},{8,9},{9,8},{10,11... | collective-permute-start | bytes 786440 | tf_op jit(solution)/shard_map/ppermute | solution.py:175
  34.5 5.4 %collective-permute-start.15 = (bf16[64,16,128]{2,1,0:T(8,128)(2,1)S(1)}, bf16[64,16,128]{2,1,0:T(8,128)(2,1)S(1)}, u32[]{:S(2)}, u32[]{:S(2)}) collective-permute-start(bf16[64,16,128]{2,1,0:T(8,128)(2,1)S(1)} %collective-permute-done.5.refs_7_), channel_id=1, source_target_pairs={{0,1},{1,0},{2,3},{3,2},{4,5},{5,4},{6,7},{7,6},{8,9},{9,8},{10,11... | collective-permute-start | bytes 786440 | tf_op jit(solution)/shard_map/ppermute | solution.py:175
  35.0 6.2 %collective-permute-start.13 = (bf16[64,16,128]{2,1,0:T(8,128)(2,1)S(1)}, bf16[64,16,128]{2,1,0:T(8,128)(2,1)S(1)}, u32[]{:S(2)}, u32[]{:S(2)}) collective-permute-start(bf16[64,16,128]{2,1,0:T(8,128)(2,1)S(1)} %collective-permute-done.9.refs_8_), channel_id=1, source_target_pairs={{0,1},{1,0},{2,3},{3,2},{4,5},{5,4},{6,7},{7,6},{8,9},{9,8},{10,11... | collective-permute-start | bytes 786440 | tf_op jit(solution)/shard_map/ppermute | solution.py:175
  39.4 1.5 %collective-permute-start.7 = (bf16[64,16,128]{2,1,0:T(8,128)(2,1)S(1)}, bf16[64,16,128]{2,1,0:T(8,128)(2,1)S(1)}, u32[]{:S(2)}, u32[]{:S(2)}) collective-permute-start(bf16[64,16,128]{2,1,0:T(8,128)(2,1)S(1)} %collective-permute-done.4.refs_0_), channel_id=1, source_target_pairs={{0,1},{1,0},{2,3},{3,2},{4,5},{5,4},{6,7},{7,6},{8,9},{9,8},{10,11... | collective-permute-start | bytes 786440 | tf_op jit(solution)/shard_map/ppermute | solution.py:175
  39.4 1.9 %collective-permute-start.8 = (bf16[64,16,128]{2,1,0:T(8,128)(2,1)S(1)}, bf16[64,16,128]{2,1,0:T(8,128)(2,1)S(1)}, u32[]{:S(2)}, u32[]{:S(2)}) collective-permute-start(bf16[64,16,128]{2,1,0:T(8,128)(2,1)S(1)} %collective-permute-done.6.refs_1_), channel_id=1, source_target_pairs={{0,1},{1,0},{2,3},{3,2},{4,5},{5,4},{6,7},{7,6},{8,9},{9,8},{10,11... | collective-permute-start | bytes 786440 | tf_op jit(solution)/shard_map/ppermute | solution.py:175
  39.9 1.8 %collective-permute-start.14 = (bf16[64,16,128]{2,1,0:T(8,128)(2,1)S(1)}, bf16[64,16,128]{2,1,0:T(8,128)(2,1)S(1)}, u32[]{:S(2)}, u32[]{:S(2)}) collective-permute-start(bf16[64,16,128]{2,1,0:T(8,128)(2,1)S(1)} %collective-permute-done.10.refs_9_), channel_id=1, source_target_pairs={{0,1},{1,0},{2,3},{3,2},{4,5},{5,4},{6,7},{7,6},{8,9},{9,8},{10,11... | collective-permute-start | bytes 786440 | tf_op jit(solution)/shard_map/ppermute | solution.py:175
  59.8 10.3 %collective-permute-start.18 = (bf16[512,128]{1,0:T(8,128)(2,1)S(1)}, bf16[512,128]{1,0:T(8,128)(2,1)S(1)}, u32[]{:S(2)}, u32[]{:S(2)}) collective-permute-start(bf16[512,128]{1,0:T(8,128)(2,1)S(1)} %shard_map.94.refs_1_), channel_id=1, source_target_pairs={{0,24},{1,25},{2,26},{3,27},{4,28},{5,29},{6,30},{7,31},{8,16},{9,... | collective-permute-start | bytes 393224 | tf_op jit(solution)/shard_map/ppermute | solution.py:175
  61.7 12.1 %collective-permute-start.17 = (bf16[512,128]{1,0:T(8,128)(2,1)S(1)}, bf16[512,128]{1,0:T(8,128)(2,1)S(1)}, u32[]{:S(2)}, u32[]{:S(2)}) collective-permute-start(bf16[512,128]{1,0:T(8,128)(2,1)S(1)} %shard_map.94.refs_1_), channel_id=1, source_target_pairs={{0,16},{1,17},{2,18},{3,19},{4,20},{5,21},{6,22},{7,23},{8,24},{9,... | collective-permute-start | bytes 393224 | tf_op jit(solution)/shard_map/ppermute | solution.py:175
  62.3 11.4 %collective-permute-start.16 = (bf16[512,128]{1,0:T(8,128)(2,1)S(1)}, bf16[512,128]{1,0:T(8,128)(2,1)S(1)}, u32[]{:S(2)}, u32[]{:S(2)}) collective-permute-start(bf16[512,128]{1,0:T(8,128)(2,1)S(1)} %shard_map.94.refs_1_), channel_id=1, source_target_pairs={{0,8},{1,9},{2,10},{3,11},{4,12},{5,13},{6,14},{7,15},{8,0},{9,1},... | collective-permute-start | bytes 393224 | tf_op jit(solution)/shard_map/ppermute | solution.py:175
  73.9 9.1 %collective-permute-start.19 = (bf16[64,16,128]{2,1,0:T(8,128)(2,1)S(1)}, bf16[64,16,128]{2,1,0:T(8,128)(2,1)S(1)}, u32[]{:S(2)}, u32[]{:S(2)}) collective-permute-start(bf16[64,16,128]{2,1,0:T(8,128)(2,1)S(1)} %get-tuple-element.38.refs_4_), channel_id=1, source_target_pairs={{0,2},{1,3},{2,0},{3,1},{4,6},{5,7},{6,4},{7,5},{8,10},{9,11},{10,... | collective-permute-start | bytes 786440 | tf_op jit(solution)/shard_map/ppermute | solution.py:175
  75.1 9.2 %collective-permute-start.21 = (bf16[64,16,128]{2,1,0:T(8,128)(2,1)S(1)}, bf16[64,16,128]{2,1,0:T(8,128)(2,1)S(1)}, u32[]{:S(2)}, u32[]{:S(2)}) collective-permute-start(bf16[64,16,128]{2,1,0:T(8,128)(2,1)S(1)} %get-tuple-element.39.refs_6_), channel_id=1, source_target_pairs={{0,4},{1,5},{2,6},{3,7},{4,0},{5,1},{6,2},{7,3},{8,12},{9,13},{10,... | collective-permute-start | bytes 786440 | tf_op jit(solution)/shard_map/ppermute | solution.py:175
  75.6 19.1 %collective-permute-start.27 = (bf16[128,16,128]{2,1,0:T(8,128)(2,1)S(1)}, bf16[128,16,128]{2,1,0:T(8,128)(2,1)S(1)}, u32[]{:S(2)}, u32[]{:S(2)}) collective-permute-start(bf16[128,16,128]{2,1,0:T(8,128)(2,1)S(1)} %get-tuple-element.40), channel_id=1, source_target_pairs={{0,1},{1,0},{2,3},{3,2},{4,5},{5,4},{6,7},{7,6},{8,9},{9,8},{10,11... | collective-permute-start | bytes 1572872 | tf_op jit(solution)/shard_map/ppermute | solution.py:175
  75.6 14.3 %collective-permute-start.25 = (bf16[64,16,128]{2,1,0:T(8,128)(2,1)S(1)}, bf16[64,16,128]{2,1,0:T(8,128)(2,1)S(1)}, u32[]{:S(2)}, u32[]{:S(2)}) collective-permute-start(bf16[64,16,128]{2,1,0:T(8,128)(2,1)S(1)} %get-tuple-element.38.refs_4_), channel_id=1, source_target_pairs={{0,4},{1,5},{2,6},{3,7},{4,0},{5,1},{6,2},{7,3},{8,12},{9,13},{10,... | collective-permute-start | bytes 786440 | tf_op jit(solution)/shard_map/ppermute | solution.py:175
  77.1 12.8 %collective-permute-start.26 = (bf16[64,16,128]{2,1,0:T(8,128)(2,1)S(1)}, bf16[64,16,128]{2,1,0:T(8,128)(2,1)S(1)}, u32[]{:S(2)}, u32[]{:S(2)}) collective-permute-start(bf16[64,16,128]{2,1,0:T(8,128)(2,1)S(1)} %get-tuple-element.39.refs_6_), channel_id=1, source_target_pairs={{0,2},{1,3},{2,0},{3,1},{4,6},{5,7},{6,4},{7,5},{8,10},{9,11},{10,... | collective-permute-start | bytes 786440 | tf_op jit(solution)/shard_map/ppermute | solution.py:175
  83.0 11.2 %collective-permute-start.20 = (bf16[64,16,128]{2,1,0:T(8,128)(2,1)S(1)}, bf16[64,16,128]{2,1,0:T(8,128)(2,1)S(1)}, u32[]{:S(2)}, u32[]{:S(2)}) collective-permute-start(bf16[64,16,128]{2,1,0:T(8,128)(2,1)S(1)} %collective-permute-done.19.refs_5_), channel_id=1, source_target_pairs={{0,4},{1,5},{2,6},{3,7},{4,0},{5,1},{6,2},{7,3},{8,12},{9,13},{10,... | collective-permute-start | bytes 786440 | tf_op jit(solution)/shard_map/ppermute | solution.py:175
  84.3 9.9 %collective-permute-start.22 = (bf16[64,16,128]{2,1,0:T(8,128)(2,1)S(1)}, bf16[64,16,128]{2,1,0:T(8,128)(2,1)S(1)}, u32[]{:S(2)}, u32[]{:S(2)}) collective-permute-start(bf16[64,16,128]{2,1,0:T(8,128)(2,1)S(1)} %collective-permute-done.21.refs_7_), channel_id=1, source_target_pairs={{0,2},{1,3},{2,0},{3,1},{4,6},{5,7},{6,4},{7,5},{8,10},{9,11},{10,... | collective-permute-start | bytes 786440 | tf_op jit(solution)/shard_map/ppermute | solution.py:175
  89.9 4.8 %collective-permute-start.28 = (bf16[64,16,128]{2,1,0:T(8,128)(2,1)S(1)}, bf16[64,16,128]{2,1,0:T(8,128)(2,1)S(1)}, u32[]{:S(2)}, u32[]{:S(2)}) collective-permute-start(bf16[64,16,128]{2,1,0:T(8,128)(2,1)S(1)} %collective-permute-done.19.refs_5_), channel_id=1, source_target_pairs={{0,1},{1,0},{2,3},{3,2},{4,5},{5,4},{6,7},{7,6},{8,9},{9,8},{10,11... | collective-permute-start | bytes 786440 | tf_op jit(solution)/shard_map/ppermute | solution.py:175
  90.0 5.3 %collective-permute-start.31 = (bf16[64,16,128]{2,1,0:T(8,128)(2,1)S(1)}, bf16[64,16,128]{2,1,0:T(8,128)(2,1)S(1)}, u32[]{:S(2)}, u32[]{:S(2)}) collective-permute-start(bf16[64,16,128]{2,1,0:T(8,128)(2,1)S(1)} %collective-permute-done.21.refs_7_), channel_id=1, source_target_pairs={{0,1},{1,0},{2,3},{3,2},{4,5},{5,4},{6,7},{7,6},{8,9},{9,8},{10,11... | collective-permute-start | bytes 786440 | tf_op jit(solution)/shard_map/ppermute | solution.py:175
  94.2 1.5 %collective-permute-start.23 = (bf16[64,16,128]{2,1,0:T(8,128)(2,1)S(1)}, bf16[64,16,128]{2,1,0:T(8,128)(2,1)S(1)}, u32[]{:S(2)}, u32[]{:S(2)}) collective-permute-start(bf16[64,16,128]{2,1,0:T(8,128)(2,1)S(1)} %collective-permute-done.20.refs_0_), channel_id=1, source_target_pairs={{0,1},{1,0},{2,3},{3,2},{4,5},{5,4},{6,7},{7,6},{8,9},{9,8},{10,11... | collective-permute-start | bytes 786440 | tf_op jit(solution)/shard_map/ppermute | solution.py:175
  94.2 1.9 %collective-permute-start.24 = (bf16[64,16,128]{2,1,0:T(8,128)(2,1)S(1)}, bf16[64,16,128]{2,1,0:T(8,128)(2,1)S(1)}, u32[]{:S(2)}, u32[]{:S(2)}) collective-permute-start(bf16[64,16,128]{2,1,0:T(8,128)(2,1)S(1)} %collective-permute-done.22.refs_1_), channel_id=1, source_target_pairs={{0,1},{1,0},{2,3},{3,2},{4,5},{5,4},{6,7},{7,6},{8,9},{9,8},{10,11... | collective-permute-start | bytes 786440 | tf_op jit(solution)/shard_map/ppermute | solution.py:175
  94.7 1.8 %collective-permute-start.29 = (bf16[64,16,128]{2,1,0:T(8,128)(2,1)S(1)}, bf16[64,16,128]{2,1,0:T(8,128)(2,1)S(1)}, u32[]{:S(2)}, u32[]{:S(2)}) collective-permute-start(bf16[64,16,128]{2,1,0:T(8,128)(2,1)S(1)} %collective-permute-done.25.refs_8_), channel_id=1, source_target_pairs={{0,1},{1,0},{2,3},{3,2},{4,5},{5,4},{6,7},{7,6},{8,9},{9,8},{10,11... | collective-permute-start | bytes 786440 | tf_op jit(solution)/shard_map/ppermute | solution.py:175
  94.8 2.1 %collective-permute-start.30 = (bf16[64,16,128]{2,1,0:T(8,128)(2,1)S(1)}, bf16[64,16,128]{2,1,0:T(8,128)(2,1)S(1)}, u32[]{:S(2)}, u32[]{:S(2)}) collective-permute-start(bf16[64,16,128]{2,1,0:T(8,128)(2,1)S(1)} %collective-permute-done.26.refs_9_), channel_id=1, source_target_pairs={{0,1},{1,0},{2,3},{3,2},{4,5},{5,4},{6,7},{7,6},{8,9},{9,8},{10,11... | collective-permute-start | bytes 786440 | tf_op jit(solution)/shard_map/ppermute | solution.py:175
  (2 other events, 87.0 us)
